TPU v7x, 32 devices: a whole 2x2x4 slice. The times are simulated.
32 devices in a mesh: lon: 8 (over y, x, core), lat: 4 (over z).
Axes of the slice: x: 2, y: 2, z: 4, core: 2. Of those that a mesh axis runs over, the one named last changes fastest.
Arguments:
- volume_b: float32 [4, 40, 192, 1024], P(None, None, 'lat', 'lon'), may hold values from -6 to 6
- tokens_a: bfloat16 [8, 24, 128, 768], P(None, 'lat', 'lon'), may hold values from -6 to 6
- embed_weight: bfloat16 [4032, 768], P('lat'), may hold values from -0.09375 to 0.09375
- unembed_weight: bfloat16 [4032, 768], P('lat'), may hold values from -0.21875 to 0.21875
Outputs:
- tokens_b: bfloat16 [8, 24, 128, 768], P(None, 'lat', 'lon')
- volume_a: float32 [4, 40, 192, 1024], P(None, None, 'lat', 'lon')
All inputs are finite; a program needn't handle non-finite values.
Results may differ from a plain program's by a relative error of at most 0.005.
Values may be sent and summed in bfloat16 or wider, within the bound.
No kernel may reach another device: no remote copies, remote signals or barrier semaphores. Data moves between devices by JAX's collectives and lax.ppermute only.
A program may use at most 704 MiB of HBM per device.

v0:
```python
import jax
import jax.numpy as jnp
from jax import lax
from jax.sharding import PartitionSpec as P


def padded_2(array, sides, width, wrap):
    for axis, dim in sides:
        size, length = (lax.axis_size(axis), array.shape[dim])
        up = [(i, (i + 1) % size) for i in range(size if wrap else size - 1)]
        down = [(j, i) for i, j in up]
        last = lax.slice_in_dim(array, length - width, length, axis=dim)
        leading = lax.slice_in_dim(array, 0, width, axis=dim)
        before = lax.ppermute(last, axis, up)
        after = lax.ppermute(leading, axis, down)
        array = jnp.concatenate([before, array, after], axis=dim)
    return array


def unfold_blocks(source, axis_at, blocks, stride, extent):
    dims_now = source.shape
    reshaped = source.reshape(dims_now[:axis_at] + (blocks + 1, stride) + dims_now[axis_at + 1 :])
    leading = lax.slice_in_dim(reshaped, 0, blocks, axis=axis_at)
    trailing = lax.slice_in_dim(reshaped, 1, blocks + 1, axis=axis_at)
    trailing = lax.slice_in_dim(trailing, 0, extent - stride, axis=axis_at + 1)
    return jnp.concatenate([leading, trailing], axis=axis_at + 1)


def fold_blocks(source, axis_at, stride):
    extent = source.shape[axis_at + 1]
    primary = lax.slice_in_dim(source, 0, stride, axis=axis_at + 1)
    overflow = lax.slice_in_dim(source, stride, extent, axis=axis_at + 1)
    widths_main = [(0, 0)] * source.ndim
    widths_main[axis_at] = (0, 1)
    widths_over = [(0, 0)] * source.ndim
    widths_over[axis_at] = (1, 0)
    widths_over[axis_at + 1] = (0, 2 * stride - extent)
    summed = jnp.pad(primary, widths_main) + jnp.pad(overflow, widths_over)
    new_dims = (
        source.shape[:axis_at]
        + (stride * (source.shape[axis_at] + 1),)
        + source.shape[axis_at + 2 :]
    )
    return summed.reshape(new_dims)


def spread_out(patch_grid, levels):
    patch_grid = patch_grid.transpose(3, 0, 4, 1, 5, 2, 6)
    patch_grid = fold_blocks(patch_grid, 5, 8)
    patch_grid = fold_blocks(patch_grid, 3, 8)
    patch_grid = fold_blocks(patch_grid, 1, 5)
    return patch_grid[:, 1 : 1 + levels]


def per_device(volume_b, tokens_a, embed_weight, unembed_weight):
    level_tok, lat_tok, lon_tok, model_width = tokens_a.shape
    variables, levels, lat_cells, lon_cells = volume_b.shape
    volume = volume_b.astype(jnp.bfloat16)
    grown = padded_2(volume, (("lon", 3), ("lat", 2)), 2, True)
    row_index = jnp.arange(lat_cells + 4)
    lat_place = lax.axis_index("lat")
    lat_count = lax.axis_size("lat")
    discard = (row_index < 2) & (lat_place == 0) | (row_index >= lat_cells + 2) & (
        lat_place == lat_count - 1
    )
    grown = jnp.where(discard[:, None], jnp.zeros((), jnp.bfloat16), grown)
    grown = jnp.pad(grown, ((0, 0), (1, 4), (0, 4), (0, 4)))
    windows = unfold_blocks(grown, 1, level_tok, 5, 7)
    windows = unfold_blocks(windows, 3, lat_tok, 8, 12)
    windows = unfold_blocks(windows, 5, lon_tok, 8, 12)
    token_count = level_tok * lat_tok * lon_tok
    patches = windows.transpose(1, 3, 5, 0, 2, 4, 6).reshape(token_count, -1)
    summed = jnp.dot(
        patches,
        lax.all_gather(embed_weight, "lat", axis=0, tiled=True),
        preferred_element_type=jnp.float32,
    )
    tokens_b = summed.astype(jnp.bfloat16).reshape(level_tok, lat_tok, lon_tok, model_width)
    flattened = tokens_a.reshape(token_count, model_width)
    spread = lax.dot_general(
        flattened,
        lax.all_gather(unembed_weight, "lat", axis=0, tiled=True),
        (((1,), (1,)), ((), ())),
        preferred_element_type=jnp.float32,
    )
    spread = spread.reshape(level_tok, lat_tok, lon_tok, variables, 7, 12, 12)
    padded = spread_out(spread, levels)
    rim_pair = jnp.concatenate(
        [padded[..., 0:2], padded[..., lon_cells + 2 : lon_cells + 4]], axis=3
    )
    edges = padded_2(rim_pair.astype(jnp.bfloat16), (("lon", 3),), 2, True).astype(rim_pair.dtype)
    inner = padded[..., 2 : lon_cells + 2]
    inner = inner.at[..., 0:2].add(edges[..., 0:2])
    inner = inner.at[..., lon_cells - 2 : lon_cells].add(edges[..., 6:8])
    rim_pair = jnp.concatenate(
        [inner[:, :, 0:2], inner[:, :, lat_cells + 2 : lat_cells + 4]], axis=2
    )
    edges = padded_2(rim_pair.astype(jnp.bfloat16), (("lat", 2),), 2, False).astype(rim_pair.dtype)
    volume_a = inner[:, :, 2 : lat_cells + 2]
    volume_a = volume_a.at[:, :, 0:2].add(edges[:, :, 0:2])
    volume_a = volume_a.at[:, :, lat_cells - 2 : lat_cells].add(edges[:, :, 6:8])
    return (tokens_b, volume_a)


def solution(mesh):
    placed = (
        P(None, None, "lat", "lon"),
        P(None, "lat", "lon", None),
        P("lat", None),
        P("lat", None),
    )
    return jax.shard_map(
        per_device,
        mesh=mesh,
        in_specs=placed,
        out_specs=(P(None, "lat", "lon", None), P(None, None, "lat", "lon")),
        check_vma=False,
    )
```

profile of v0, /device:TPU:0, one launch (start us, length us, event | category | flops | bytes accessed | tf_op | source)
XLA Modules:
  0.0 1363.5 jit_solution(2981544533296436352)
XLA Ops:
  8.0 7.3 copy.54
  16.7 2.9 collective-permute-start.1
  21.7 7.3 pad_maximum_fusion.1
  29.1 10.6 fusion.5
  39.7 5.7 copy.55
  47.8 5.6 copy.56
  58.2 5.2 copy.57
  63.4 5.5 collective-permute-done.3
  68.9 5.1 copy.58
  74.0 12.7 maximum_select_fusion
  86.7 9.6 copy.74
  96.3 3.1 pad.36.clone
  103.2 3.9 maximum_bitcast_fusion.1
  112.3 12.8 pad_maximum_fusion
  125.1 39.2 %copy.60 = bf16[4,8,7,6,12,136]{4,5,3,2,1,0:T(8,128)(2,1)} copy(bf16[4,8,7,6,12,136]{5,4,3,2,1,0:T(8,128)(2,1)} %pad_maximum_fusion) | data formatting | bytes 8773632 | tf_op jit(solution)/shard_map/concatenate | solution.py:26
  164.3 29.7 %slice.252 = bf16[4,8,7,6,12,16,8]{4,6,5,3,2,1,0:T(8,128)(2,1)} slice(bf16[4,8,7,6,12,17,8]{4,6,5,3,2,1,0:T(8,128)(2,1)} %bitcast.25), slice={[0:4], [0:8], [0:7], [0:6], [0:12], [0:16], [0:8]} | slice | bytes 8257536 | tf_op jit(solution)/shard_map/slice | solution.py:23
  194.0 22.7 %slice.253 = bf16[4,8,7,6,12,16,4]{4,6,5,3,2,1,0:T(4,128)(2,1)} slice(bf16[4,8,7,6,12,17,8]{4,6,5,3,2,1,0:T(8,128)(2,1)} %bitcast.26), slice={[0:4], [0:8], [0:7], [0:6], [0:12], [1:17], [0:4]} | slice | bytes 4128768 | tf_op jit(solution)/shard_map/slice | solution.py:25
  216.7 10.5 reshape.179
  227.2 60.0 %convolution_bitcast_fusion = f32[4,8,7,6,12,16,12]{5,6,4,2,0,3,1:T(8,128)} fusion(bf16[4,7,12,12,768,1,1]{4,3,2,1,0,5,6:T(8,128)(2,1)} %reshape.179, bf16[8,6,16,768]{3,2,1,0:T(8,128)(2,1)S(1)} %copy-done), kind=kOutput, calls=%fused_computation.3 | convolution fusion | flops 4756340736 | bytes 19759104 | tf_op jit(solution)/shard_map/dot_general | solution.py:80
  287.2 44.6 %slice.254 = f32[4,8,7,6,12,16,8]{5,6,4,2,0,3,1:T(8,128)} slice(f32[4,8,7,6,12,16,12]{5,6,4,2,0,3,1:T(8,128)} %convolution_bitcast_fusion), slice={[0:4], [0:8], [0:7], [0:6], [0:12], [0:16], [0:8]} | slice | bytes 16515072 | tf_op jit(solution)/shard_map/slice | solution.py:31
  331.8 32.0 %slice.255 = f32[4,8,7,6,12,16,4]{5,6,4,2,0,3,1:T(4,128)} slice(f32[4,8,7,6,12,16,12]{5,6,4,2,0,3,1:T(8,128)} %convolution_bitcast_fusion), slice={[0:4], [0:8], [0:7], [0:6], [0:12], [0:16], [8:12]} | slice | bytes 8257536 | tf_op jit(solution)/shard_map/slice | solution.py:32
  363.8 53.2 %pad_add_fusion.1 = f32[4,8,7,6,12,17,8]{5,6,4,2,0,3,1:T(8,128)} fusion(f32[4,8,7,6,12,16,4]{5,6,4,2,0,3,1:T(4,128)} %slice.255, f32[4,8,7,6,12,16,8]{5,6,4,2,0,3,1:T(8,128)} %slice.254), kind=kLoop, calls=%fused_computation.2 | loop fusion | flops 2193408 | bytes 21159936 | tf_op jit(solution)/shard_map/add | solution.py:38
  417.0 91.1 %copy.62 = f32[4,8,7,6,12,17,8]{4,6,5,3,2,1,0:T(8,128)} copy(f32[4,8,7,6,12,17,8]{5,6,4,2,0,3,1:T(8,128)} %pad_add_fusion.1) | data formatting | bytes 17547264 | tf_op jit(solution)/shard_map/add | solution.py:38
  508.1 62.0 %slice.257 = f32[4,8,7,6,4,136]{4,5,3,2,1,0:T(8,128)} slice(f32[4,8,7,6,12,136]{4,5,3,2,1,0:T(8,128)} %bitcast.9), slice={[0:4], [0:8], [0:7], [0:6], [8:12], [0:136]} | slice | bytes 5849088 | tf_op jit(solution)/shard_map/slice | solution.py:32
  570.1 94.4 %pad_add_fusion = f32[4,8,7,7,8,136]{4,5,3,2,1,0:T(8,128)} fusion(f32[4,8,7,6,4,136]{4,5,3,2,1,0:T(8,128)} %slice.257, f32[4,8,7,6,8,136]{4,5,3,2,1,0:T(8,128)} %bitcast.24), kind=kLoop, calls=%fused_computation | loop fusion | flops 1705984 | bytes 15597568 | tf_op jit(solution)/shard_map/add | solution.py:38
  664.5 73.6 %copy.63 = f32[4,8,7,7,8,136]{5,4,3,2,1,0:T(8,128)} copy(f32[4,8,7,7,8,136]{4,5,3,2,1,0:T(8,128)} %pad_add_fusion) | data formatting | bytes 13647872 | tf_op jit(solution)/shard_map/add | solution.py:38
  738.2 8.1 slice.258
  748.5 8.6 pad_add_fusion.2
  757.1 12.9 copy.64
  770.1 8.4 convert.12
  782.2 50.8 %maximum_bitcast_fusion = bf16[8,6,16,4,7,12,12]{5,6,2,1,4,0,3:T(8,128)(2,1)} fusion(bf16[4,8,7,6,12,16,4]{4,6,5,3,2,1,0:T(4,128)(2,1)} %slice.253, bf16[4,8,7,6,12,16,8]{4,6,5,3,2,1,0:T(8,128)(2,1)} %slice.252), kind=kLoop, calls=%fused_computation.1 | loop fusion | flops 12386304 | bytes 12386304 | tf_op jit(solution)/shard_map/transpose | solution.py:72
  833.0 179.3 %copy.61 = bf16[8,6,16,4,7,12,12]{2,1,0,6,5,4,3:T(8,128)(2,1)} copy(bf16[8,6,16,4,7,12,12]{5,6,2,1,4,0,3:T(8,128)(2,1)} %maximum_bitcast_fusion) | data formatting | bytes 12386304 | tf_op jit(solution)/shard_map/transpose | solution.py:72
  1012.3 70.5 %reshape.173 = bf16[768,4032]{0,1:T(8,128)(2,1)} reshape(bf16[8,6,16,4,7,12,12]{2,1,0,6,5,4,3:T(8,128)(2,1)} %copy.61) | data formatting | bytes 12386304 | tf_op jit(solution)/shard_map/reshape | solution.py:72
  1082.8 9.4 slice.260
  1095.5 7.0 convert.13
  1102.5 10.5 fusion.6
  1113.0 5.2 copy.67
  1119.8 5.4 copy.68
  1126.5 9.9 convolution_convert_fusion
  1136.4 10.7 slice.265
  1147.1 4.0 copy.69
  1151.2 4.0 copy.70
  1155.1 14.6 %maximum_convert_fusion = f32[4,40,8,128]{2,1,3,0:T(8,128)} fusion(bf16[4,40,2,128]{2,1,3,0:T(8,128)(2,1)} %copy.70, bf16[4,40,2,128]{2,1,3,0:T(8,128)(2,1)} %get-tuple-element.60, bf16[4,40,2,128]{2,1,3,0:T(8,128)(2,1)} %get-tuple-element.61, bf16[4,40,2,128]{2,1,3,0:T(8,128)(2,1)} %copy.69), kind=kLoop, calls=%fused_computation.12 | loop fusion | flops 1310720 | bytes 983040 | tf_op jit(solution)/shard_map/convert_element_type | solution.py:98
  1169.8 13.7 %slice_add_fusion.1 = f32[4,40,2,128]{2,1,3,0:T(8,128)} fusion(f32[4,40,8,128]{2,1,3,0:T(8,128)} %maximum_convert_fusion, f32[4,40,56,128]{2,1,3,0:T(8,128)} %fusion.2), kind=kLoop, calls=%fused_computation.6 | loop fusion | flops 40960 | bytes 491520 | tf_op jit(solution)/shard_map/add | solution.py:100
  1183.4 52.8 %scatter-add.16 = f32[4,40,48,128]{2,1,3,0:T(8,128)} dynamic-update-slice(f32[4,40,48,128]{2,1,3,0:T(8,128)} %slice.265, f32[4,40,2,128]{2,1,3,0:T(8,128)} %slice_add_fusion.1, s32[]{:T(128)} %constant.117.clone.1, s32[]{:T(128)} %constant.117.clone.1, s32[]{:T(128)} %constant.117.clone.1, s32[]{:T(128)} %constant.117.clone.1) | dynamic-update-slice | bytes 327684 | tf_op jit(solution)/shard_map/scatter-add | solution.py:100
  1236.3 16.4 %slice_add_fusion = f32[4,40,2,128]{2,1,3,0:T(8,128)} fusion(f32[4,40,8,128]{2,1,3,0:T(8,128)} %maximum_convert_fusion, f32[4,40,48,128]{2,1,3,0:T(8,128)} %scatter-add.16), kind=kLoop, calls=%fused_computation.5 | loop fusion | flops 40960 | bytes 491520 | tf_op jit(solution)/shard_map/add | solution.py:101
  1252.7 95.0 %scatter-add.19 = f32[4,40,48,128]{2,1,3,0:T(8,128)} dynamic-update-slice(f32[4,40,48,128]{2,1,3,0:T(8,128)} %scatter-add.16, f32[4,40,2,128]{2,1,3,0:T(8,128)} %slice_add_fusion, s32[]{:T(128)} %constant.117.clone.1, s32[]{:T(128)} %constant.117.clone.1, s32[]{:T(128)} %constant.123.clone.1, s32[]{:T(128)} %constant.117.clone.1) | dynamic-update-slice | bytes 327684 | tf_op jit(solution)/shard_map/scatter-add | solution.py:101
  1347.7 8.6 copy.71
  (34 shorter events, 32.6 us)
Async XLA Ops:
  7.2 220.1 %copy-start = (bf16[8,6,16,768]{3,2,1,0:T(8,128)(2,1)S(1)}, bf16[8,6,16,768]{3,2,1,0:T(8,128)(2,1)}, u32[]{:S(2)}) copy-start(bf16[8,6,16,768]{3,2,1,0:T(8,128)(2,1)} %param.13) | copy-start | bytes 3538948
  7.2 209.5 %all-gather.5.cloned.1.call-start = ((), (), s32[]{:S(2)}) async-start(), calls=%async_computation.1 | async-start | bytes 7741440 | tf_op jit(solution)/shard_map/all_gather | solution.py:82
  7.9 1118.6 %all-gather.3.cloned.1.call-start = ((), (), s32[]{:S(2)}) async-start(), calls=%async_computation | async-start | bytes 7741440 | tf_op jit(solution)/shard_map/all_gather | solution.py:75
  16.2 5.5 collective-permute-start
  16.7 5.0 collective-permute-start.1
  45.3 12.9 collective-permute-start.2
  53.4 15.5 %collective-permute-start.3 = (bf16[4,40,2,132]{3,1,2,0:T(8,128)(2,1)S(1)}, bf16[4,40,2,132]{3,1,2,0:T(8,128)(2,1)S(1)}, u32[]{:S(2)}, u32[]{:S(2)}) collective-permute-start(bf16[4,40,2,132]{3,1,2,0:T(8,128)(2,1)S(1)} %copy.56), channel_id=1, source_target_pairs={{1,0},{2,1},{3,2},{0,3},{5,4},{6,5},{7,6},{4,7},{9,8},{10,9},{11,1... | collective-permute-start | bytes 253448 | tf_op jit(solution)/shard_map/ppermute | solution.py:15
  779.5 312.7 %collective-permute-start.4 = (bf16[4,40,56,2]{2,1,3,0:T(8,128)(2,1)S(1)}, bf16[4,40,56,2]{2,1,3,0:T(8,128)(2,1)S(1)}, u32[]{:S(2)}, u32[]{:S(2)}) collective-permute-start(bf16[4,40,56,2]{2,1,3,0:T(8,128)(2,1)S(1)} %get-tuple-element.56), channel_id=1, source_target_pairs={{0,4},{4,8},{8,12},{12,16},{16,20},{20,24},{24,28},{28,0},{1,5},{5... | collective-permute-start | bytes 107528 | tf_op jit(solution)/shard_map/ppermute | solution.py:14
  779.7 312.5 %collective-permute-start.5 = (bf16[4,40,56,2]{2,1,3,0:T(8,128)(2,1)S(1)}, bf16[4,40,56,2]{2,1,3,0:T(8,128)(2,1)S(1)}, u32[]{:S(2)}, u32[]{:S(2)}) collective-permute-start(bf16[4,40,56,2]{2,1,3,0:T(8,128)(2,1)S(1)} %get-tuple-element.57), channel_id=1, source_target_pairs={{4,0},{8,4},{12,8},{16,12},{20,16},{24,20},{28,24},{0,28},{5,1},{9... | collective-permute-start | bytes 107528 | tf_op jit(solution)/shard_map/ppermute | solution.py:15
  1118.1 29.0 %collective-permute-start.6 = (bf16[4,40,2,128]{3,1,2,0:T(8,128)(2,1)S(1)}, bf16[4,40,2,128]{3,1,2,0:T(8,128)(2,1)S(1)}, u32[]{:S(2)}, u32[]{:S(2)}) collective-permute-start(bf16[4,40,2,128]{3,1,2,0:T(8,128)(2,1)S(1)} %copy.67), channel_id=1, source_target_pairs={{0,1},{1,2},{2,3},{4,5},{5,6},{6,7},{8,9},{9,10},{10,11},{12,13},{... | collective-permute-start | bytes 245768 | tf_op jit(solution)/shard_map/ppermute | solution.py:14
  1125.2 26.0 %collective-permute-start.7 = (bf16[4,40,2,128]{3,1,2,0:T(8,128)(2,1)S(1)}, bf16[4,40,2,128]{3,1,2,0:T(8,128)(2,1)S(1)}, u32[]{:S(2)}, u32[]{:S(2)}) collective-permute-start(bf16[4,40,2,128]{3,1,2,0:T(8,128)(2,1)S(1)} %copy.68), channel_id=1, source_target_pairs={{1,0},{2,1},{3,2},{5,4},{6,5},{7,6},{9,8},{10,9},{11,10},{13,12},{... | collective-permute-start | bytes 245768 | tf_op jit(solution)/shard_map/ppermute | solution.py:15
  1252.7 103.6 %copy-start.1 = (bf16[8,6,16,768]{3,2,1,0:T(8,128)(2,1)S(1)}, bf16[8,6,16,768]{3,2,1,0:T(8,128)(2,1)}, u32[]{:S(2)}) copy-start(bf16[8,6,16,768]{3,2,1,0:T(8,128)(2,1)} %param.13) | copy-start | bytes 3538948
Sparse Core Ops, SparseCore 0:
  9.6 123.4 all-gather.4
  134.6 111.9 all-gather.2
where the time goes:
time: 1380 us; the launch traced here: 1360 us
  local copies, waits for them, and re-layouts  947 us (69%)
  other arithmetic  307 us (22%)
  matrix products  69.9 us (5%)
  between operations  14.6 us (1%)
    transpose x1, local copies, waits for them, and re-layouts, per_device(): patches = windows.transpose(1, 3, 5, 0, 2, 4, 6).reshape(token_count, -1)  179 us
    add x2, local copies, waits for them, and re-layouts, fold_blocks(): summed = jnp.pad(primary, widths_main) + jnp.pad(overflow, widths_over)  165 us
    add x3, other arithmetic, fold_blocks(): summed = jnp.pad(primary, widths_main) + jnp.pad(overflow, widths_over)  156 us
    slice x3, local copies, waits for them, and re-layouts, fold_blocks(): overflow = lax.slice_in_dim(source, stride, extent, axis=axis_at + 1)  96.3 us
    scatter-add x1, local copies, waits for them, and re-layouts, per_device(): volume_a = volume_a.at[:, :, lat_cells - 2:lat_cells].add(edges[:, :, 6:8])  95 us
    reshape x1, local copies, waits for them, and re-layouts, per_device(): patches = windows.transpose(1, 3, 5, 0, 2, 4, 6).reshape(token_count, -1)  70.5 us
    dot_general x1, matrix products, per_device(): lax.dot_general(flattened, lax.all_gather(unembed_weight, 'lat', axis=0,...  60 us
    scatter-add x1, local copies, waits for them, and re-layouts, per_device(): volume_a = volume_a.at[:, :, 0:2].add(edges[:, :, 0:2])  52.8 us
  transfers between devices with their start and end apart: 10, of which 3 were waited for; matrix products, arithmetic and copies ran while one was open for 82% of the time, Pallas kernels for 0%

commit v1 on v0

v1 whole, which is shorter than its diff:
```python
import functools

import jax
import jax.numpy as jnp
from jax import lax
from jax.experimental import pallas as pl
from jax.experimental.pallas import tpu as pltpu
from jax.sharding import PartitionSpec as P

BF = jnp.bfloat16
F32 = jnp.float32
VMEM_LIMIT = 56 * 1024 * 1024
DZ, DY, DX = 7, 12, 12
SK, SY, SX = 5, 8, 8
GROUP = 8


def params():
    return pltpu.CompilerParams(vmem_limit_bytes=VMEM_LIMIT)


def spread_matrix(nk, ni, nx):
    rows = jnp.arange(nk * nx, dtype=jnp.int32)[:, None]
    cols = jnp.arange(DX * nk * ni, dtype=jnp.int32)[None, :]
    dx, k, i = cols // (nk * ni), cols // ni % nk, cols % ni
    return ((rows // nx == k) & (rows % nx == SX * i - 2 + dx)).astype(BF)


def edge_lanes(nv, nk):
    lane = jnp.arange(4 * nv * nk, dtype=jnp.int32)
    return lane // (2 * nv * nk), lane // (2 * nk) % nv, lane // nk % 2, lane % nk


def pick_matrix(nv, nk, nx):
    side, v, c, k = edge_lanes(nv, nk)
    rows = jnp.arange(nk * nx, dtype=jnp.int32)[None, :, None]
    x = jnp.where(side == 0, nx - 2 + c, c)
    own = jnp.arange(nv, dtype=jnp.int32)[:, None, None] == v
    return (own & (rows // nx == k) & (rows % nx == x)).astype(BF)


def edge_matrix(nv, nk, ni):
    side, v, c, k = (jnp.tile(a, 2)[None, :, None] for a in edge_lanes(nv, nk))
    half = (jnp.arange(8 * nv * nk, dtype=jnp.int32) // (4 * nv * nk))[None, :, None]
    cols = jnp.arange(4 * nk * ni, dtype=jnp.int32)[None, None, :]
    d, kk, i = cols // (nk * ni), cols // ni % nk, cols % ni
    own = jnp.arange(nv, dtype=jnp.int32)[:, None, None] == v
    left = (half == 0) & (side == 0) & (i == 0) & (d == c)
    right = (half == 1) & (side == 1) & (i == ni - 1) & (d == 2 + c)
    return (own & (k == kk) & (left | right)).astype(BF)


def out_edge_matrix(nk, ni):
    rows = jnp.arange(DX * nk * ni, dtype=jnp.int32)[:, None]
    lane = jnp.arange(128, dtype=jnp.int32)[None, :]
    dx, k, i = rows // (nk * ni), rows // ni % nk, rows % ni
    side, c, kk = lane // (2 * nk), lane // nk % 2, lane % nk
    left = (side == 0) & (i == 0) & (dx == c)
    right = (side == 1) & (i == ni - 1) & (dx == DX - 2 + c)
    return ((k == kk) & (left | right)).astype(BF)


def in_edge_matrix(nk, nx):
    row = jnp.arange(256, dtype=jnp.int32)[:, None]
    half, lane = row // 128, row % 128
    side, c, k = lane // (2 * nk), lane // nk % 2, lane % nk
    cols = jnp.arange(nk * nx, dtype=jnp.int32)[None, :]
    kk, x = cols // nx, cols % nx
    from_left = (half == 0) & (side == 1) & (x == c)
    from_right = (half == 1) & (side == 0) & (x == nx - 2 + c)
    return ((k == kk) & (from_left | from_right)).astype(BF)


def stack_levels(read, levels, nk, zeros, lhs, at, rows, dz):
    for k in range(nk):
        level = SK * k - 1 + dz
        block = read(level) if 0 <= level < levels else zeros
        lhs[at : at + rows, k * 128 : (k + 1) * 128] = block


def pack_kernel(nk, vol, pick, out, lhs, acc):
    v = pl.program_id(0)
    _, levels, ny, nx = vol.shape
    for dz in range(DZ):
        stack_levels(lambda l: vol[0, l].astype(BF), levels, nk, jnp.zeros((ny, nx), BF), lhs, dz * ny, ny, dz)
    part = jnp.dot(lhs[...], pick[0], preferred_element_type=F32)

    @pl.when(v == 0)
    def _():
        acc[...] = part

    @pl.when(v > 0)
    def _():
        acc[...] += part

    @pl.when(v == pl.num_programs(0) - 1)
    def _():
        out[...] = acc[...].astype(BF)


def im2col_kernel(nk, ni, nj, shard, vol, rim, edge, spread, edge_hot, out, lhs, q):
    _, levels, ny, nx = vol.shape
    main = DZ * ny
    for dz in range(DZ):
        stack_levels(lambda l: vol[0, l].astype(BF), levels, nk, jnp.zeros((ny, nx), BF), lhs, dz * ny, ny, dz)
    none = jnp.zeros((8, nx), F32)
    for k in range(nk):
        blocks = []
        for dz in range(DZ + 1):
            level = SK * k - 1 + dz
            blocks.append(rim[0, level] if 0 <= level < levels and dz < DZ else none)
        lhs[main : main + 64, k * 128 : (k + 1) * 128] = jnp.concatenate(blocks, axis=0).astype(BF)
    for pair in range(DX // 2):
        got = jnp.dot(lhs[...], spread[:, pair * 256 : (pair + 1) * 256], preferred_element_type=F32)
        if pair in (0, DX // 2 - 1):
            which = 0 if pair == 0 else 1
            got += jnp.dot(edge[...], edge_hot[0, :, which * 256 : (which + 1) * 256], preferred_element_type=F32)
        for h in range(2):
            dx = 2 * pair + h
            mine = got[:, h * 128 : (h + 1) * 128]
            for dz in range(DZ):
                q[dz, pl.ds(2 * DX + dx, ny, stride=DX), :] = mine[dz * ny : (dz + 1) * ny]
                at = main + 8 * dz
                q[dz, pl.ds(dx, 2, stride=DX), :] = mine[at : at + 2]
                q[dz, pl.ds(DX * (ny + 2) + dx, 2, stride=DX), :] = mine[at + 2 : at + 4]
    rows, padded, piece = shard
    head = piece * (GROUP - 1)
    per = SY * DX
    for j in range(nj):
        columns = jnp.concatenate([q[dz, per * j : per * j + DY * DX, :] for dz in range(DZ)], axis=0)
        gap = jnp.zeros((padded - rows, 128), F32)
        columns = jnp.concatenate([columns[:head], gap, columns[head:]], axis=0)
        out[0, j] = columns.T.astype(BF)


def weight_copies(gathered, sources, step, me, slot, sems):
    padded = slot.shape[0]
    piece = padded // GROUP
    if not gathered:
        (source,) = sources
        rows = source.shape[1]
        head = piece * (GROUP - 1)
        return [
            pltpu.make_async_copy(source.at[step, pl.ds(0, head)], slot.at[pl.ds(0, head)], sems.at[0]),
            pltpu.make_async_copy(source.at[step, pl.ds(rows - piece, piece)], slot.at[pl.ds(head, piece)], sems.at[1]),
        ]
    core = lax.rem(me, 2)
    a, b = 2 + 2 * core, 4 - 2 * core
    distances = ((0, a), (b, 6), (1, 1 + b), (1 + a, 7))
    copies = []
    for n, (source, pair) in enumerate(zip(sources, distances)):
        for h, distance in enumerate(pair):
            place = pl.multiple_of(lax.bitwise_xor(me, jnp.int32(distance)) * piece, piece)
            copies.append(
                pltpu.make_async_copy(source.at[h, step], slot.at[pl.ds(place, piece)], sems.at[2 * n + h])
            )
    return copies


def embed_kernel(n, gathered, first, last, vid, me, a, *refs):
    n_w = 4 if gathered else 1
    sources, refs = refs[:n_w], refs[n_w:]
    if not first:
        prev, refs = refs[0], refs[1:]
    out, a_buf, w_buf, acc, a_sem, w_sem = refs

    def copies(s):
        slot = s % 2
        return [pltpu.make_async_copy(a.at[vid[s]], a_buf.at[slot], a_sem.at[slot])] + weight_copies(
            gathered, sources, s, me[0], w_buf.at[slot], w_sem.at[slot]
        )

    for c in copies(0):
        c.start()
    total = None
    for s in range(n):
        if s + 1 < n:
            for c in copies(s + 1):
                c.start()
        for c in copies(s):
            c.wait()
        got = jnp.dot(a_buf[s % 2], w_buf[s % 2], preferred_element_type=F32)
        if s > 0:
            got += acc[...]
        elif not first:
            got += prev[...]
        if s < n - 1:
            acc[...] = got
        elif last:
            nk, nj, ni, width = out.shape
            for j in range(nj):
                out[:, j] = got[j * nk * ni : (j + 1) * nk * ni].astype(BF).reshape(nk, ni, width)
        else:
            out[...] = got


def unembed_kernel(gathered, first, vid, me, tokens, spread, out_hot, *refs):
    n_w = 4 if gathered else 1
    sources, refs = refs[:n_w], refs[n_w:]
    if not first:
        edge_before, refs = refs[0], refs[3:]
    vol, rim, edge, w_buf, t, r, q, lhs, rim_q, w_sem = refs
    s, n = pl.program_id(0), pl.num_programs(0)
    nk, nj, ni, _ = tokens.shape
    _, levels, ny, nx = vol.shape
    main, per, over, block = DZ * ny, SY * DX, (DY - SY) * DX, DY * DX
    padded = w_buf.shape[1]
    head, gap = padded // GROUP * (GROUP - 1), padded - DZ * block

    def copies(step):
        slot = lax.rem(step, 2)
        return weight_copies(gathered, sources, step, me[0], w_buf.at[slot], w_sem.at[slot])

    @pl.when(s == 0)
    def _():
        for c in copies(s):
            c.start()
        for j in range(nj):
            for k in range(nk):
                t[(j * nk + k) * ni : (j * nk + k + 1) * ni, :] = tokens[k, j]
        rim_q[...] = jnp.zeros_like(rim_q)
        if first:
            edge[...] = jnp.zeros_like(edge)
        else:
            edge[...] = edge_before[...]

    @pl.when(s + 1 < n)
    def _():
        for c in copies(s + 1):
            c.start()

    for c in copies(s):
        c.wait()
    r[...] = lax.dot_general(w_buf[lax.rem(s, 2)], t[...], (((1,), (1,)), ((), ())), preferred_element_type=F32)

    def rows_of(dz, j, start, stop):
        lanes = slice(j * 128, (j + 1) * 128)
        lo, hi = dz * block + start, dz * block + stop
        if hi <= head:
            return r[lo:hi, lanes]
        if lo >= head:
            return r[lo + gap : hi + gap, lanes]
        return jnp.concatenate([r[lo:head, lanes], r[head + gap : hi + gap, lanes]], axis=0)

    for dz in range(DZ):
        for j in range(nj + 1):
            if j == nj:
                q[dz, per * j : per * j + over, :] = rows_of(dz, j - 1, per, block)
            else:
                lead = rows_of(dz, j, 0, over)
                if j > 0:
                    lead += rows_of(dz, j - 1, per, block)
                q[dz, per * j : per * j + over, :] = lead
                q[dz, per * j + over : per * (j + 1), :] = rows_of(dz, j, over, per)
    for dx in range(DX):
        lanes = slice(dx * 128, (dx + 1) * 128)
        for dz in range(DZ):
            lhs[dz * ny : (dz + 1) * ny, lanes] = q[dz, pl.ds(2 * DX + dx, ny, stride=DX), :].astype(BF)
            rim_q[8 * dz : 8 * dz + 2, lanes] = q[dz, pl.ds(dx, 2, stride=DX), :]
            rim_q[8 * dz + 2 : 8 * dz + 4, lanes] = q[dz, pl.ds(DX * (ny + 2) + dx, 2, stride=DX), :]
    lhs[main : main + 64, :] = rim_q[...].astype(BF)
    side = jnp.dot(lhs[...], out_hot[...], preferred_element_type=F32)
    edge[...] += pltpu.roll(side, vid[s] * 32, 1)

    carry = None
    for pair in range(nk // 2):
        got = lax.dot_general(
            lhs[...], spread[pair * 256 : (pair + 1) * 256, :], (((1,), (1,)), ((), ())), preferred_element_type=F32
        )
        for h in range(2):
            k = 2 * pair + h
            mine = got[:, h * 128 : (h + 1) * 128]
            for dz in range(DZ):
                level = SK * k - 1 + dz
                here = mine[dz * ny : (dz + 1) * ny]
                beside = mine[main + 8 * dz : main + 8 * (dz + 1)]
                if dz < DZ - SK and k > 0:
                    here, beside = here + carry[dz][0], beside + carry[dz][1]
                if 0 <= level < levels and (dz < SK or k == nk - 1):
                    vol[0, level], rim[0, level] = here, beside
            carry = [
                (mine[dz * ny : (dz + 1) * ny], mine[main + 8 * dz : main + 8 * (dz + 1)]) for dz in range(SK, DZ)
            ]


def add_edges(edge, at, rows, hot, levels, nk, v, apply):
    mine = edge[at : at + rows * (DZ + (rows == 8)), :].astype(F32)
    width = mine.shape[1] // 2
    shift = lax.rem(128 - 32 * v, 128)
    mine = jnp.concatenate([pltpu.roll(mine[:, :width], shift, 1), pltpu.roll(mine[:, width:], shift, 1)], axis=1)
    mine = mine.astype(BF)
    carry = None
    for pair in range(nk // 2):
        got = jnp.dot(mine, hot[:, pair * 256 : (pair + 1) * 256], preferred_element_type=F32)
        for h in range(2):
            k = 2 * pair + h
            part = got[:, h * 128 : (h + 1) * 128]
            for dz in range(DZ):
                level = SK * k - 1 + dz
                here = part[dz * rows : (dz + 1) * rows]
                if dz < DZ - SK and k > 0:
                    here = here + carry[dz]
                if 0 <= level < levels and (dz < SK or k == nk - 1):
                    apply(level, here)
            carry = [part[dz * rows : (dz + 1) * rows] for dz in range(SK, DZ)]


def rim_kernel(nk, rim, edge, hot, out):
    _, levels, _, _ = rim.shape
    main = edge.shape[0] - 64

    def apply(level, here):
        out[0, level] = rim[0, level] + here

    add_edges(edge, main, 8, hot, levels, nk, pl.program_id(0), apply)


def close_kernel(nk, vol, edge, hot, beside, out):
    _, levels, ny, _ = vol.shape
    row = lax.broadcasted_iota(jnp.int32, (8, 128), 0)

    def apply(level, here):
        got = vol[0, level] + here
        lat = beside[0, level]
        out[0, level, 0:8] = got[0:8] + jnp.where(row < 2, lat, 0.0)
        out[0, level, 8 : ny - 8] = got[8 : ny - 8]
        out[0, level, ny - 8 : ny] = got[ny - 8 : ny] + jnp.where(row >= 6, lat, 0.0)

    add_edges(edge, 0, ny, hot, levels, nk, pl.program_id(0), apply)


def whole(shape):
    return pl.BlockSpec(shape, lambda *_: (0,) * len(shape))


def lead(shape):
    return pl.BlockSpec((1,) + tuple(shape[1:]), lambda v, *_: (v,) + (0,) * (len(shape) - 1))


ANY = pl.BlockSpec(memory_space=pl.ANY)


def cost(flops, bytes_accessed):
    return pl.CostEstimate(flops=int(flops), bytes_accessed=int(bytes_accessed), transcendentals=0)


def pack_edges(volume, nk):
    nv, levels, ny, nx = volume.shape
    pick = pick_matrix(nv, nk, nx)
    return pl.pallas_call(
        functools.partial(pack_kernel, nk),
        grid=(nv,),
        in_specs=[lead(volume.shape), lead(pick.shape)],
        out_specs=whole((DZ * ny, 128)),
        out_shape=jax.ShapeDtypeStruct((DZ * ny, 128), BF),
        scratch_shapes=[pltpu.VMEM((DZ * ny, nk * nx), BF), pltpu.VMEM((DZ * ny, 128), F32)],
        compiler_params=params(),
        cost_estimate=cost(2 * nv * DZ * ny * nk * nx * 256, volume.size * 4),
        name="pack_edges",
    )(volume, pick)


def im2col(volume, rim, edge, spread, dims):
    nk, nj, ni, padded = dims
    nv, levels, ny, nx = volume.shape
    hot = edge_matrix(nv, nk, ni)
    rows = DZ * ny + 64
    shape = (nv, nj, nk * ni, padded)
    return pl.pallas_call(
        functools.partial(im2col_kernel, nk, ni, nj, (DZ * DY * DX, padded, padded // GROUP)),
        grid=(nv,),
        in_specs=[lead(volume.shape), lead(rim.shape), whole(edge.shape), whole(spread.shape), lead(hot.shape)],
        out_specs=lead(shape),
        out_shape=jax.ShapeDtypeStruct(shape, BF),
        scratch_shapes=[pltpu.VMEM((rows, nk * nx), BF), pltpu.VMEM((DZ, DX * (ny + 4), 128), F32)],
        compiler_params=params(),
        cost_estimate=cost(3 * nv * rows * nk * nx * DX * 128, volume.size * 4 + 2 * nv * nj * 128 * padded),
        name="im2col",
    )(volume, rim, edge, spread, hot)


def embed(a, weights, vid, me, prev, gathered, last, token_shape):
    n = vid.shape[0]
    nv, rows, padded = a.shape
    width = weights[0].shape[-1]
    first = prev is None
    out_shape = jax.ShapeDtypeStruct(token_shape, BF) if last else jax.ShapeDtypeStruct((rows, width), F32)
    smem = pl.BlockSpec(memory_space=pltpu.SMEM)
    vmem = pl.BlockSpec(memory_space=pltpu.VMEM)
    return pl.pallas_call(
        functools.partial(embed_kernel, n, gathered, first, last),
        in_specs=[smem, smem, ANY] + [ANY] * len(weights) + ([] if first else [vmem]),
        out_specs=vmem,
        out_shape=out_shape,
        scratch_shapes=[
            pltpu.VMEM((2, rows, padded), BF),
            pltpu.VMEM((2, padded, width), BF),
            pltpu.VMEM((rows, width) if n > 1 else (8, 128), F32),
            pltpu.SemaphoreType.DMA((2,)),
            pltpu.SemaphoreType.DMA((2, GROUP)),
        ],
        compiler_params=params(),
        cost_estimate=cost(2 * n * rows * padded * width, 2 * n * padded * (rows + width) + 4 * rows * width),
        name="embed",
    )(vid, me, a, *weights, *([] if first else [prev]))


def unembed(tokens, weights, vid, me, spread, out_hot, prev, gathered, volume_shape, padded):
    n = vid.shape[0]
    nk, nj, ni, width = tokens.shape
    nv, levels, ny, nx = volume_shape
    first = prev is None
    rows = DZ * ny + 64
    out_shape = (
        jax.ShapeDtypeStruct(volume_shape, F32),
        jax.ShapeDtypeStruct((nv, levels, 8, nx), F32),
        jax.ShapeDtypeStruct((rows, 128), F32),
    )

    def chosen(shape):
        return pl.BlockSpec((1,) + tuple(shape[1:]), lambda s, vid, me: (vid[s],) + (0,) * (len(shape) - 1))

    n_in = 5 + len(weights)
    before = () if first else (prev[2], prev[0], prev[1])
    return pl.pallas_call(
        functools.partial(unembed_kernel, gathered, first),
        grid_spec=pltpu.PrefetchScalarGridSpec(
            num_scalar_prefetch=2,
            grid=(n,),
            in_specs=[whole(tokens.shape), whole(spread.shape), whole(out_hot.shape)]
            + [ANY] * len(weights)
            + ([] if first else [whole((rows, 128)), ANY, ANY]),
            out_specs=(chosen(volume_shape), chosen((nv, levels, 8, nx)), whole((rows, 128))),
            scratch_shapes=[
                pltpu.VMEM((2, padded, width), BF),
                pltpu.VMEM((nj * nk * ni, width), BF),
                pltpu.VMEM((padded, nj * nk * ni), F32),
                pltpu.VMEM((DZ, DX * (ny + 4), 128), F32),
                pltpu.VMEM((rows, DX * nk * ni), BF),
                pltpu.VMEM((64, DX * nk * ni), F32),
                pltpu.SemaphoreType.DMA((2, GROUP)),
            ],
        ),
        out_shape=out_shape,
        input_output_aliases={} if first else {n_in + 1: 0, n_in + 2: 1},
        compiler_params=params(),
        cost_estimate=cost(6 * n * padded * width * nj * 128, 2 * n * padded * width + 4 * n * levels * ny * nx),
        name="unembed",
    )(vid, me, tokens, spread, out_hot, *weights, *before)


def rim_sums(rim, edge, hot, nk):
    return pl.pallas_call(
        functools.partial(rim_kernel, nk),
        grid=(rim.shape[0],),
        in_specs=[lead(rim.shape), whole(edge.shape), whole(hot.shape)],
        out_specs=lead(rim.shape),
        out_shape=jax.ShapeDtypeStruct(rim.shape, F32),
        compiler_params=params(),
        cost_estimate=cost(1e8, 8 * rim.size),
        name="rim_sums",
    )(rim, edge, hot)


def close_volume(vol, edge, hot, beside, nk):
    return pl.pallas_call(
        functools.partial(close_kernel, nk),
        grid=(vol.shape[0],),
        in_specs=[lead(vol.shape), whole(edge.shape), whole(hot.shape), lead(beside.shape)],
        out_specs=lead(vol.shape),
        out_shape=jax.ShapeDtypeStruct(vol.shape, F32),
        compiler_params=params(),
        cost_estimate=cost(1e9, 8 * vol.size),
        name="close_volume",
    )(vol, edge, hot, beside)


def both_ways(up_rows, down_rows, axis, wrap):
    size = lax.axis_size(axis)
    up = [(i, (i + 1) % size) for i in range(size if wrap else size - 1)]
    return lax.ppermute(up_rows, axis, up), lax.ppermute(down_rows, axis, [(j, i) for i, j in up])


def piece_rows(rows):
    return -(-rows // (16 * GROUP)) * 16


def gather_rows(weight, me):
    rows, piece = weight.shape[0], piece_rows(weight.shape[0])
    size, devices = lax.axis_size("lat"), lax.axis_size("lon")
    own = lax.dynamic_slice_in_dim(weight, jnp.minimum(me * piece, rows - piece), piece, 0)
    got = [lax.ppermute(own, "lat", [(i, (i + s) % size) for i in range(size)]) for s in range(1, size)]
    near = jnp.stack(got)
    first = [(i, i ^ (2 + 2 * (i & 1))) for i in range(devices)]
    second = [(i, i ^ (4 - 2 * (i & 1))) for i in range(devices)]
    partner = [(i, i ^ 1) for i in range(devices)]
    pair = jnp.stack([near, lax.ppermute(near, "lon", first)])
    rest = lax.ppermute(pair, "lon", second)
    return pair, rest, lax.ppermute(pair, "lon", partner), lax.ppermute(rest, "lon", partner)


def per_device(volume_b, tokens_a, embed_weight, unembed_weight):
    nk, nj, ni, width = tokens_a.shape
    nv, levels, ny, nx = volume_b.shape
    rows = DZ * DY * DX
    padded = piece_rows(rows) * GROUP
    main = DZ * ny
    lat, lats = lax.axis_index("lat"), lax.axis_size("lat")
    me = lax.rem(lax.axis_index("lon"), GROUP).astype(jnp.int32)
    me1 = me.reshape(1)
    fast = embed_weight.shape[0] == rows and lax.axis_size("lon") % GROUP == 0
    spread = spread_matrix(nk, ni, nx)
    out_hot = out_edge_matrix(nk, ni)
    in_hot = in_edge_matrix(nk, nx)

    if fast:
        unembed_rest = gather_rows(unembed_weight, me)
        embed_rest = gather_rows(embed_weight, me)

    packed = pack_edges(volume_b, nk)
    from_left, from_right = both_ways(packed, packed, "lon", True)

    def lat_rows(at):
        voxels = volume_b[:, :, at : at + 2].astype(BF).reshape(-1, nx)
        corners = [a.reshape(DZ, ny, 128)[:, at : at + 2].reshape(-1, 128) for a in (from_left, from_right)]
        return jnp.concatenate([voxels] + corners, axis=0)

    above, below = both_ways(lat_rows(ny - 2), lat_rows(0), "lat", False)
    n_vox = nv * levels * 2

    def split(got):
        voxels = got[:n_vox].reshape(nv, levels, 2, nx)
        corners = got[n_vox:].reshape(2, DZ, 2, 128)
        return voxels, jnp.concatenate([corners[0], corners[1]], axis=-1)

    (vox_above, cor_above), (vox_below, cor_below) = split(above), split(below)
    rim = jnp.concatenate([vox_above, vox_below, jnp.zeros((nv, levels, 4, nx), BF)], axis=2).astype(F32)
    corners = jnp.concatenate([cor_above, cor_below, jnp.zeros((DZ, 4, 256), BF)], axis=1).reshape(8 * DZ, 256)
    edge = jnp.concatenate(
        [jnp.concatenate([from_left, from_right], axis=1), corners, jnp.zeros((64 - 8 * DZ, 256), BF)], axis=0
    )
    a = im2col(volume_b, rim, edge, spread, (nk, nj, ni, padded)).reshape(nv, nj * nk * ni, padded)

    if fast:
        own = lat.astype(jnp.int32).reshape(1)
        others = lax.rem(lat - jnp.arange(1, lats, dtype=jnp.int32) + lats, lats).astype(jnp.int32)
        part = unembed(
            tokens_a, (unembed_weight[None],), own, me1, spread, out_hot, None, False, volume_b.shape, padded
        )
        vol, vol_rim, vol_edge = unembed(
            tokens_a, unembed_rest, others, me1, spread, out_hot, part, True, volume_b.shape, padded
        )
        sums = embed(a, (embed_weight[None],), own, me1, None, False, False, tokens_a.shape)
        tokens_b = embed(a, embed_rest, others, me1, sums, True, True, tokens_a.shape)
    else:
        every = jnp.arange(nv, dtype=jnp.int32)
        weights = [
            lax.all_gather(w, "lat", axis=0, tiled=True).reshape(nv, rows, width)
            for w in (unembed_weight, embed_weight)
        ]
        vol, vol_rim, vol_edge = unembed(
            tokens_a, weights[:1], every, me1, spread, out_hot, None, False, volume_b.shape, padded
        )
        tokens_b = embed(a, weights[1:], every, me1, None, False, True, tokens_a.shape)

    sent = vol_edge.astype(BF)
    edges = jnp.concatenate(both_ways(sent, sent, "lon", True), axis=1)
    outer = rim_sums(vol_rim, edges, in_hot, nk)
    down, up = (outer[:, :, at : at + 2].astype(BF).reshape(-1, nx) for at in (0, 2))
    above, below = (x.reshape(nv, levels, 2, nx) for x in both_ways(up, down, "lat", False))
    beside = jnp.concatenate([above, jnp.zeros((nv, levels, 4, nx), BF), below], axis=2).astype(F32)
    volume_a = close_volume(vol, edges, in_hot, beside, nk)
    return tokens_b, volume_a


def solution(mesh):
    placed = (
        P(None, None, "lat", "lon"),
        P(None, "lat", "lon", None),
        P("lat", None),
        P("lat", None),
    )
    return jax.shard_map(
        per_device,
        mesh=mesh,
        in_specs=placed,
        out_specs=(P(None, "lat", "lon", None), P(None, None, "lat", "lon")),
        check_vma=False,
    )
```

time: 1380 us -> 154 us (0.11); the launches traced: 1360 us -> 154 us
  local copies, waits for them, and re-layouts: 947 us -> 9.88 us
  other arithmetic: 307 us -> 21.4 us
  matrix products: 69.9 us -> 0 us
  Pallas kernels: 0 us -> 67.7 us
  starting transfers between devices: 13.7 us -> 29.9 us
    slice x21 -> x8, local copies, waits for them, and re-layouts: 275 us -> 1.74 us  [the longest x2 1.48 us: lat_rows(): a.reshape(DZ, ny, 128)[:, at:at + 2].reshape(-1, 128)]
    add x5 -> x3, other arithmetic: 186 us -> 0.6 us  [the longest x1 0.58 us: out_edge_matrix(): right = (side == 1) & (i == ni - 1) & (dx == DX - 2 + c)]
    transpose x1 -> x0, local copies, waits for them, and re-layouts: 179 us -> none  [per_device(): patches = windows.transpose(1, 3, 5, 0, 2, 4, 6).reshape(token_count, -1)]
    add x2 -> x0, local copies, waits for them, and re-layouts: 165 us -> none  [fold_blocks(): summed = jnp.pad(primary, widths_main) + jnp.pad(overflow, widths_over)]
    scatter-add x2 -> x0, local copies, waits for them, and re-layouts: 148 us -> none  [the longest x1 95 us: per_device(): volume_a = volume_a.at[:, :, lat_cells - 2:lat_cells].add(edges[:, :, 6:8])]
    reshape x2 -> x4, local copies, waits for them, and re-layouts: 83.4 us -> 0.07 us  [lat_rows(): a.reshape(DZ, ny, 128)[:, at:at + 2].reshape(-1, 128)]
    dot_general x2 -> x0, matrix products: 69.9 us -> none  [the longest x1 60 us: per_device(): lax.dot_general(flattened, lax.all_gather(unembed_weight, 'lat', axis=0,...]
    pallas_call x0 -> x8, Pallas kernels: none -> 67.7 us  [the longest x2 26.1 us: unembed(): pl.pallas_call(functools.partial(unembed_kernel, gathered, first), grid_s...]
  transfers between devices with their start and end apart: 10 -> 22, of which waited for: 3 -> 8; matrix products, arithmetic and copies ran while one was open for 82% -> 17% of each run, Pallas kernels for 0% -> 37%
where the time goes in v1:
time: 154 us
  Pallas kernels  67.7 us (44%)
  starting transfers between devices  29.9 us (19%)
  waiting for transfers between devices  23.5 us (15%)
  other arithmetic  21.4 us (14%)
  local copies, waits for them, and re-layouts  9.88 us (6%)
    pallas_call x2, Pallas kernels, unembed(): pl.pallas_call(functools.partial(unembed_kernel, gathered, first), grid_s...  26.1 us
    pallas_call x2, Pallas kernels, embed(): pl.pallas_call(functools.partial(embed_kernel, n, gathered, first, last),...  16 us
    pallas_call x1, Pallas kernels, im2col(): pl.pallas_call(functools.partial(im2col_kernel, nk, ni, nj, (DZ * DY * DX...  11.6 us
    ppermute x6, starting transfers between devices, gather_rows(): lax.ppermute(own, 'lat', [(i, (i + s) % size) for i in range(size)])  10.9 us
    ppermute x4, waiting for transfers between devices, both_ways(): lax.ppermute(down_rows, axis, [(j, i) for i, j in up])  8.4 us
    ppermute x4, starting transfers between devices, both_ways(): lax.ppermute(down_rows, axis, [(j, i) for i, j in up])  6.75 us
    ppermute x4, starting transfers between devices, both_ways(): lax.ppermute(up_rows, axis, up)  6.31 us
    ppermute x6, waiting for transfers between devices, gather_rows(): lax.ppermute(own, 'lat', [(i, (i + s) % size) for i in range(size)])  5.57 us
  transfers between devices with their start and end apart: 22, of which 8 were waited for; matrix products, arithmetic and copies ran while one was open for 17% of the time, Pallas kernels for 37%

profile of v1, /device:TPU:0, one launch (start us, length us, event | category | flops | bytes accessed | tf_op | source)
XLA Modules:
  0.0 153.6 jit_solution(7729320740993633481)
XLA Ops:
  0.6 1.0 constant_dynamic-slice_fusion
  1.6 3.1 %collective-permute-start.11 = (bf16[128,768]{1,0:T(8,128)(2,1)S(1)}, bf16[128,768]{1,0:T(8,128)(2,1)S(1)}, u32[]{:S(2)}, u32[]{:S(2)}) collective-permute-start(bf16[128,768]{1,0:T(8,128)(2,1)S(1)} %constant_dynamic-slice_fusion), channel_id=1, source_target_pairs={{0,1},{1,2},{2,3},{3,0},{4,5},{5,6},{6,7},{7,4},{8,9},{9,10},{10,1... | collective-permute-start | bytes 589832 | tf_op jit(solution)/shard_map/ppermute | solution.py:492
  4.7 2.6 %collective-permute-start.12 = (bf16[128,768]{1,0:T(8,128)(2,1)S(1)}, bf16[128,768]{1,0:T(8,128)(2,1)S(1)}, u32[]{:S(2)}, u32[]{:S(2)}) collective-permute-start(bf16[128,768]{1,0:T(8,128)(2,1)S(1)} %constant_dynamic-slice_fusion), channel_id=1, source_target_pairs={{0,2},{1,3},{2,0},{3,1},{4,6},{5,7},{6,4},{7,5},{8,10},{9,11},{10,... | collective-permute-start | bytes 589832 | tf_op jit(solution)/shard_map/ppermute | solution.py:492
  7.3 1.3 collective-permute-start.13
  9.1 1.3 and_convert_fusion.2.pick
  10.4 4.4 %pack_edges.1 = bf16[336,128]{1,0:T(8,128)(2,1)} custom-call(f32[4,40,48,128]{3,2,1,0:T(8,128)} %vol.3, bf16[4,1024,128]{2,1,0:T(8,128)(2,1)} %and_convert_fusion.2.pick), custom_call_target="tpu_custom_call" | custom-call | flops 704643072 | bytes 3932160 | tf_op jit(solution)/shard_map/pack_edges/pallas_call | solution.py:350
  14.8 2.6 %collective-permute-start.1 = (bf16[336,128]{1,0:T(8,128)(2,1)}, bf16[336,128]{1,0:T(8,128)(2,1)}, u32[]{:S(2)}, u32[]{:S(2)}) collective-permute-start(bf16[336,128]{1,0:T(8,128)(2,1)} %pack_edges.1), channel_id=1, source_target_pairs={{4,0},{8,4},{12,8},{16,12},{20,16},{24,20},{28,24},{0,28},{5,1},{9... | collective-permute-start | bytes 258056 | tf_op jit(solution)/shard_map/ppermute | solution.py:481
  18.8 1.8 %constant_dynamic-slice_fusion.1 = bf16[128,768]{1,0:T(8,128)(2,1)} fusion(bf16[1008,768]{1,0:T(8,128)(2,1)} %param.6, s32[]{:T(128)S(6)} %select_n.491), kind=kLoop, calls=%fused_computation.138 | loop fusion | bytes 393220 | tf_op jit(solution)/shard_map/dynamic_slice | solution.py:491
  21.0 1.4 and_convert_fusion.1.edge_hot
  22.4 1.2 and_convert_fusion.3.hot
  23.7 0.7 collective-permute-start.4
  27.6 3.6 %and_convert_fusion.4.out_hot = bf16[1536,128]{1,0:T(8,128)(2,1)} fusion(s32[128]{0:T(128)} %broadcast_add_fusion.1, s32[128]{0:T(128)} %copy-done.9, s32[128]{0:T(128)} %copy-done.7, s32[1536]{0:T(1024)S(1)} %get-tuple-element.40, s32[1536]{0:T(1024)S(1)} %add_select_fusion, pred[128]{0:T(512)(128)(4,1)} %get-tuple-element.39, ...), kind=kLoop, calls=%fused_computation.6 | loop fusion | flops 1966080 | bytes 410368 | tf_op jit(solution)/shard_map/convert_element_type | solution.py:60
  31.2 3.7 %collective-permute-done.14 = bf16[3,128,768]{2,1,0:T(8,128)(2,1)} collective-permute-done((bf16[3,128,768]{2,1,0:T(8,128)(2,1)S(1)}, bf16[3,128,768]{2,1,0:T(8,128)(2,1)}, u32[]{:S(2)}, u32[]{:S(2)}) %collective-permute-start.14) | collective-permute-done | bytes 589856 | tf_op jit(solution)/shard_map/ppermute | solution.py:497
  34.8 2.2 %pad_maximum_fusion.1.refs_0_ = bf16[2,3,128,768]{3,2,1,0:T(8,128)(2,1)} fusion(bf16[1,3,128,768]{3,2,1,0:T(8,128)(2,1)} %bitcast.25, bf16[1,3,128,768]{3,2,1,0:T(8,128)(2,1)S(1)} %get-tuple-element.16), kind=kLoop, calls=%fused_computation.4 | loop fusion | flops 589824 | bytes 2359296 | tf_op jit(solution)/shard_map/stack | solution.py:497
  37.0 1.5 collective-permute-start.15
  38.7 2.5 %and_convert_fusion.spread = bf16[1024,1536]{1,0:T(8,128)(2,1)} fusion(s32[1536]{0:T(1024)S(1)} %get-tuple-element.41, s32[1536]{0:T(1024)S(1)} %get-tuple-element.40, s32[1024]{0:T(1024)S(1)} %get-tuple-element.42, s32[1024]{0:T(1024)S(1)} %get-tuple-element.43), kind=kLoop, calls=%fused_computation | loop fusion | flops 6291456 | bytes 3166208 | tf_op jit(solution)/shard_map/convert_element_type | solution.py:26
  41.1 8.7 %unembed.2 = (f32[4,40,48,128]{3,2,1,0:T(8,128)}, f32[4,40,8,128]{3,2,1,0:T(8,128)}, f32[400,128]{1,0:T(8,128)}) custom-call(s32[1]{0:T(128)} %bitcast.19.vid, s32[1]{0:T(128)} %bitcast.me, bf16[8,6,16,768]{3,2,1,0:T(8,128)(2,1)} %tokens.3, bf16[1024,1536]{1,0:T(8,128)(2,1)} %and_convert_fusion.spread, bf16[1536,128]{1,0:T(8,128)(2,1)} %and_convert_fusion.4.out_hot, ...), custom_call_target="tpu_custom_call" | custom-call | flops 3623878656 | bytes 2555904 | tf_op jit(solution)/shard_map/unembed/pallas_call | solution.py:425
  50.4 3.1 %collective-permute-done.15.refs_1_ = bf16[2,3,128,768]{3,2,1,0:T(8,128)(2,1)} collective-permute-done((bf16[2,3,128,768]{3,2,1,0:T(8,128)(2,1)}, bf16[2,3,128,768]{3,2,1,0:T(8,128)(2,1)}, u32[]{:S(2)}, u32[]{:S(2)}) %collective-permute-start.15) | collective-permute-done | bytes 1179680 | tf_op jit(solution)/shard_map/ppermute | solution.py:498
  53.5 0.7 fusion.44
  54.3 2.9 %collective-permute-start.6 = (bf16[128,768]{1,0:T(8,128)(2,1)}, bf16[128,768]{1,0:T(8,128)(2,1)S(1)}, u32[]{:S(2)}, u32[]{:S(2)}) collective-permute-start(bf16[128,768]{1,0:T(8,128)(2,1)} %constant_dynamic-slice_fusion.1), channel_id=1, source_target_pairs={{0,3},{1,0},{2,1},{3,2},{4,7},{5,4},{6,5},{7,6},{8,11},{9,8},{10,9... | collective-permute-start | bytes 589832 | tf_op jit(solution)/shard_map/ppermute | solution.py:492
  57.2 0.7 fusion.45
  58.0 5.6 %collective-permute-done.6 = bf16[128,768]{1,0:T(8,128)(2,1)S(1)} collective-permute-done((bf16[128,768]{1,0:T(8,128)(2,1)}, bf16[128,768]{1,0:T(8,128)(2,1)S(1)}, u32[]{:S(2)}, u32[]{:S(2)}) %collective-permute-start.6) | collective-permute-done | bytes 196640 | tf_op jit(solution)/shard_map/ppermute | solution.py:492
  64.3 3.7 %collective-permute-start.2 = (bf16[348,128]{1,0:T(8,128)(2,1)S(1)}, bf16[348,128]{1,0:T(8,128)(2,1)S(1)}, u32[]{:S(2)}, u32[]{:S(2)}) collective-permute-start(bf16[348,128]{1,0:T(8,128)(2,1)S(1)} %pad_maximum_fusion.4), channel_id=1, source_target_pairs={{0,1},{1,2},{2,3},{4,5},{5,6},{6,7},{8,9},{9,10},{10,11},{12,13},{... | collective-permute-start | bytes 267272 | tf_op jit(solution)/shard_map/ppermute | solution.py:481
  68.0 1.3 collective-permute-start.3
  69.3 1.0 collective-permute-done.2
  70.4 4.1 %collective-permute-done.3 = bf16[348,128]{1,0:T(8,128)(2,1)S(1)} collective-permute-done((bf16[348,128]{1,0:T(8,128)(2,1)S(1)}, bf16[348,128]{1,0:T(8,128)(2,1)S(1)}, u32[]{:S(2)}, u32[]{:S(2)}) %collective-permute-start.3) | collective-permute-done | bytes 89120 | tf_op jit(solution)/shard_map/ppermute | solution.py:481
  74.7 1.5 collective-permute-start.8
  76.2 1.0 copy-done.10
  77.2 17.4 %unembed.3 = (f32[4,40,48,128]{3,2,1,0:T(8,128)}, f32[4,40,8,128]{3,2,1,0:T(8,128)}, f32[400,128]{1,0:T(8,128)}) custom-call(s32[3]{0:T(128)} %compare_select_fusion.6.vid, s32[1]{0:T(128)} %bitcast.me, bf16[8,6,16,768]{3,2,1,0:T(8,128)(2,1)} %tokens.3, bf16[1024,1536]{1,0:T(8,128)(2,1)} %and_convert_fusion.spread, ...), custom_call_target="tpu_custom_call", output_to_operand_aliasing={{0}: (10, {}), {1}: (11, {})} | custom-call | flops 10871635968 | bytes 7667712 | tf_op jit(solution)/shard_map/unembed/pallas_call | solution.py:425
  94.6 0.9 convert_element_type.41
  95.7 1.5 %collective-permute-start.9 = (bf16[2,3,128,768]{3,2,1,0:T(8,128)(2,1)S(1)}, bf16[2,3,128,768]{3,2,1,0:T(8,128)(2,1)S(1)}, u32[]{:S(2)}, u32[]{:S(2)}) collective-permute-start(bf16[2,3,128,768]{3,2,1,0:T(8,128)(2,1)S(1)} %pad_maximum_fusion.refs_0_), channel_id=1, source_target_pairs={{0,4},{4,0},{8,12},{12,8},{16,20},{20,16},{24,28},{28,24},{1,5},{5... | collective-permute-start | bytes 3538952 | tf_op jit(solution)/shard_map/ppermute | solution.py:499
  97.4 1.5 collective-permute-start.19
  98.9 1.7 %collective-permute-done.18 = bf16[400,128]{1,0:T(8,128)(2,1)S(1)} collective-permute-done((bf16[400,128]{1,0:T(8,128)(2,1)S(1)}, bf16[400,128]{1,0:T(8,128)(2,1)S(1)}, u32[]{:S(2)}, u32[]{:S(2)}) %collective-permute-start.18) | collective-permute-done | bytes 102432 | tf_op jit(solution)/shard_map/ppermute | solution.py:481
  100.6 0.8 collective-permute-done.19
  101.5 0.7 copy-done.2
  102.2 4.0 %rim_sums.1 = f32[4,40,8,128]{3,2,1,0:T(8,128)} custom-call(f32[4,40,8,128]{3,2,1,0:T(8,128)} %get-tuple-element.13.rim, bf16[400,256]{1,0:T(8,128)(2,1)} %copy-done.2, bf16[256,1024]{1,0:T(8,128)(2,1)} %and_convert_fusion.3.hot), custom_call_target="tpu_custom_call" | custom-call | flops 100000000 | bytes 1310720 | tf_op jit(solution)/shard_map/rim_sums/pallas_call | solution.py:453
  106.2 1.1 convert.9
  107.4 2.6 %collective-permute-start.20 = (bf16[320,128]{1,0:T(8,128)(2,1)S(1)}, bf16[320,128]{1,0:T(8,128)(2,1)S(1)}, u32[]{:S(2)}, u32[]{:S(2)}) collective-permute-start(bf16[320,128]{1,0:T(8,128)(2,1)S(1)} %bitcast.57), channel_id=1, source_target_pairs={{0,1},{1,2},{2,3},{4,5},{5,6},{6,7},{8,9},{9,10},{10,11},{12,13},{... | collective-permute-start | bytes 245768 | tf_op jit(solution)/shard_map/ppermute | solution.py:481
  110.0 1.3 collective-permute-start.21
  111.3 1.8 %maximum_maximum_fusion.edge = bf16[400,256]{1,0:T(8,128)(2,1)} fusion(bf16[56,256]{1,0:T(8,128)(2,1)S(1)} %maximum_bitcast_fusion, bf16[336,128]{1,0:T(8,128)(2,1)} %collective-permute-done.1, bf16[336,128]{1,0:T(8,128)(2,1)} %collective-permute-done, bf16[400]{0:T(512)(128)(2,1)S(1)} %copy-done.6), kind=kLoop, calls=%fused_computation.15 | loop fusion | flops 819200 | bytes 406304 | tf_op jit(solution)/shard_map/concatenate | solution.py:539
  113.1 3.4 %collective-permute-done.21 = bf16[320,128]{1,0:T(8,128)(2,1)S(1)} collective-permute-done((bf16[320,128]{1,0:T(8,128)(2,1)S(1)}, bf16[320,128]{1,0:T(8,128)(2,1)S(1)}, u32[]{:S(2)}, u32[]{:S(2)}) %collective-permute-start.21) | collective-permute-done | bytes 81952 | tf_op jit(solution)/shard_map/ppermute | solution.py:481
  116.6 1.5 %maximum_convert_fusion.1 = (f32[4,40,8,128]{3,2,1,0:T(8,128)}, f32[4,40,8,128]{3,2,1,0:T(8,128)}) fusion(bf16[4,40,2,128]{3,2,1,0:T(2,128)(2,1)S(1)} %bitcast.55, bf16[4,40,4,128]{3,2,1,0:T(4,128)(2,1)S(1)} %broadcast.1654, bf16[4,40,2,128]{3,2,1,0:T(2,128)(2,1)S(1)} %bitcast.54, bf16[4,40,2,128]{3,2,1,0:T(2,128)(2,1)S(1)} %bitcast.45, ...), kind=kLoop, calls=%fused_computation.11 | loop fusion | flops 1966080 | bytes 1802240 | tf_op jit(solution)/shard_map/convert_element_type | solution.py:571
  118.1 5.5 %close_volume.1 = f32[4,40,48,128]{3,2,1,0:T(8,128)} custom-call(f32[4,40,48,128]{3,2,1,0:T(8,128)} %get-tuple-element.11.vol, bf16[400,256]{1,0:T(8,128)(2,1)} %copy-done.2, bf16[256,1024]{1,0:T(8,128)(2,1)} %and_convert_fusion.3.hot, f32[4,40,8,128]{3,2,1,0:T(8,128)} %get-tuple-element.22.beside), custom_call_target="tpu_custom_call" | custom-call | flops 1000000000 | bytes 7864320 | tf_op jit(solution)/shard_map/close_volume/pallas_call | solution.py:466
  123.7 11.6 %im2col.1 = bf16[4,6,128,1024]{3,2,1,0:T(8,128)(2,1)} custom-call(f32[4,40,48,128]{3,2,1,0:T(8,128)} %vol.3, f32[4,40,8,128]{3,2,1,0:T(8,128)} %get-tuple-element.23.rim, bf16[400,256]{1,0:T(8,128)(2,1)} %maximum_maximum_fusion.edge, bf16[1024,1536]{1,0:T(8,128)(2,1)} %and_convert_fusion.spread, bf16[4,256,512]{2,1,0:T(8,128)(2,1)} %and_convert_fusion.1.edge_hot), custom_call_target="tpu_custom_call" | custom-call | flops 7549747200 | bytes 10223616 | tf_op jit(solution)/shard_map/im2col/pallas_call | solution.py:369
  135.3 4.8 %embed.2.refs_4_ = f32[768,768]{1,0:T(8,128)} custom-call(s32[1]{0:T(128)} %bitcast.19.vid, s32[1]{0:T(128)} %bitcast.me, bf16[4,768,1024]{2,1,0:T(8,128)(2,1)} %bitcast.40, bf16[1,1008,768]{2,1,0:T(8,128)(2,1)} %bitcast.42), custom_call_target="tpu_custom_call" | custom-call | flops 1207959552 | bytes 5505024 | tf_op jit(solution)/shard_map/embed/pallas_call | solution.py:390
  140.1 1.1 copy-done.4
  141.2 1.0 copy-done.5
  142.3 11.2 %embed.3 = bf16[8,6,16,768]{3,2,1,0:T(8,128)(2,1)} custom-call(s32[3]{0:T(128)} %compare_select_fusion.6.vid, s32[1]{0:T(128)} %bitcast.me, bf16[4,768,1024]{2,1,0:T(8,128)(2,1)} %bitcast.41, bf16[2,3,128,768]{3,2,1,0:T(8,128)(2,1)} %copy-done.1, bf16[2,3,128,768]{3,2,1,0:T(8,128)(2,1)} %copy-done.3, bf16[2,3,128,768]{3,2,1,0:T(8,128)(2,1)} %copy-done.4, ...), custom_call_target="tpu_custom_call" | custom-call | flops 3623878656 | bytes 11796480 | tf_op jit(solution)/shard_map/embed/pallas_call | solution.py:390
  (96 shorter events, 7.6 us)
Async XLA Ops:
  1.6 22.0 %collective-permute-start.11 = (bf16[128,768]{1,0:T(8,128)(2,1)S(1)}, bf16[128,768]{1,0:T(8,128)(2,1)S(1)}, u32[]{:S(2)}, u32[]{:S(2)}) collective-permute-start(bf16[128,768]{1,0:T(8,128)(2,1)S(1)} %constant_dynamic-slice_fusion), channel_id=1, source_target_pairs={{0,1},{1,2},{2,3},{3,0},{4,5},{5,6},{6,7},{7,4},{8,9},{9,10},{10,1... | collective-permute-start | bytes 589832 | tf_op jit(solution)/shard_map/ppermute | solution.py:492
  4.7 19.6 %collective-permute-start.12 = (bf16[128,768]{1,0:T(8,128)(2,1)S(1)}, bf16[128,768]{1,0:T(8,128)(2,1)S(1)}, u32[]{:S(2)}, u32[]{:S(2)}) collective-permute-start(bf16[128,768]{1,0:T(8,128)(2,1)S(1)} %constant_dynamic-slice_fusion), channel_id=1, source_target_pairs={{0,2},{1,3},{2,0},{3,1},{4,6},{5,7},{6,4},{7,5},{8,10},{9,11},{10,... | collective-permute-start | bytes 589832 | tf_op jit(solution)/shard_map/ppermute | solution.py:492
  7.3 17.4 %collective-permute-start.13 = (bf16[128,768]{1,0:T(8,128)(2,1)S(1)}, bf16[128,768]{1,0:T(8,128)(2,1)S(1)}, u32[]{:S(2)}, u32[]{:S(2)}) collective-permute-start(bf16[128,768]{1,0:T(8,128)(2,1)S(1)} %constant_dynamic-slice_fusion), channel_id=1, source_target_pairs={{0,3},{1,0},{2,1},{3,2},{4,7},{5,4},{6,5},{7,6},{8,11},{9,8},{10,9... | collective-permute-start | bytes 589832 | tf_op jit(solution)/shard_map/ppermute | solution.py:492
  8.7 10.0 %copy-start.9 = (s32[128]{0:T(128)}, s32[128]{0:T(128)S(1)}, u32[]{:S(2)}) copy-start(s32[128]{0:T(128)S(1)} %get-tuple-element.32) | copy-start | bytes 1540
  8.7 10.1 %copy-start.7 = (s32[128]{0:T(128)}, s32[128]{0:T(128)S(1)}, u32[]{:S(2)}) copy-start(s32[128]{0:T(128)S(1)} %get-tuple-element.33) | copy-start | bytes 1540
  14.8 35.6 %collective-permute-start = (bf16[336,128]{1,0:T(8,128)(2,1)}, bf16[336,128]{1,0:T(8,128)(2,1)}, u32[]{:S(2)}, u32[]{:S(2)}) collective-permute-start(bf16[336,128]{1,0:T(8,128)(2,1)} %pack_edges.1), channel_id=1, source_target_pairs={{0,4},{4,8},{8,12},{12,16},{16,20},{20,24},{24,28},{28,0},{1,5},{5... | collective-permute-start | bytes 258056 | tf_op jit(solution)/shard_map/ppermute | solution.py:481
  14.8 39.5 %collective-permute-start.1 = (bf16[336,128]{1,0:T(8,128)(2,1)}, bf16[336,128]{1,0:T(8,128)(2,1)}, u32[]{:S(2)}, u32[]{:S(2)}) collective-permute-start(bf16[336,128]{1,0:T(8,128)(2,1)} %pack_edges.1), channel_id=1, source_target_pairs={{4,0},{8,4},{12,8},{16,12},{20,16},{24,20},{28,24},{0,28},{5,1},{9... | collective-permute-start | bytes 258056 | tf_op jit(solution)/shard_map/ppermute | solution.py:481
  18.8 7.2 %copy-start = (f32[4,40,48,128]{3,2,1,0:T(8,128)S(1)}, f32[4,40,48,128]{3,2,1,0:T(8,128)}, u32[]{:S(2)}) copy-start(f32[4,40,48,128]{3,2,1,0:T(8,128)} %vol.3) | copy-start | bytes 11796484
  23.7 34.3 %collective-permute-start.4 = (bf16[128,768]{1,0:T(8,128)(2,1)}, bf16[128,768]{1,0:T(8,128)(2,1)S(1)}, u32[]{:S(2)}, u32[]{:S(2)}) collective-permute-start(bf16[128,768]{1,0:T(8,128)(2,1)} %constant_dynamic-slice_fusion.1), channel_id=1, source_target_pairs={{0,1},{1,2},{2,3},{3,0},{4,5},{5,6},{6,7},{7,4},{8,9},{9,10},{10,1... | collective-permute-start | bytes 589832 | tf_op jit(solution)/shard_map/ppermute | solution.py:492
  24.3 33.6 %collective-permute-start.5 = (bf16[128,768]{1,0:T(8,128)(2,1)}, bf16[128,768]{1,0:T(8,128)(2,1)S(1)}, u32[]{:S(2)}, u32[]{:S(2)}) collective-permute-start(bf16[128,768]{1,0:T(8,128)(2,1)} %constant_dynamic-slice_fusion.1), channel_id=1, source_target_pairs={{0,2},{1,3},{2,0},{3,1},{4,6},{5,7},{6,4},{7,5},{8,10},{9,11},{10,... | collective-permute-start | bytes 589832 | tf_op jit(solution)/shard_map/ppermute | solution.py:492
  24.8 10.1 %collective-permute-start.14 = (bf16[3,128,768]{2,1,0:T(8,128)(2,1)S(1)}, bf16[3,128,768]{2,1,0:T(8,128)(2,1)}, u32[]{:S(2)}, u32[]{:S(2)}) collective-permute-start(bf16[3,128,768]{2,1,0:T(8,128)(2,1)S(1)} %get-tuple-element.17), channel_id=1, source_target_pairs={{0,8},{4,20},{8,0},{12,28},{16,24},{20,4},{24,16},{28,12},{1,9},{5... | collective-permute-start | bytes 1769480 | tf_op jit(solution)/shard_map/ppermute | solution.py:497
  37.0 16.5 %collective-permute-start.15 = (bf16[2,3,128,768]{3,2,1,0:T(8,128)(2,1)}, bf16[2,3,128,768]{3,2,1,0:T(8,128)(2,1)}, u32[]{:S(2)}, u32[]{:S(2)}) collective-permute-start(bf16[2,3,128,768]{3,2,1,0:T(8,128)(2,1)} %pad_maximum_fusion.1.refs_0_), channel_id=1, source_target_pairs={{0,16},{4,12},{8,24},{12,4},{16,0},{20,28},{24,8},{28,20},{1,17},{... | collective-permute-start | bytes 3538952 | tf_op jit(solution)/shard_map/ppermute | solution.py:498
  50.4 25.8 %collective-permute-start.16 = (bf16[2,3,128,768]{3,2,1,0:T(8,128)(2,1)}, bf16[2,3,128,768]{3,2,1,0:T(8,128)(2,1)S(1)}, u32[]{:S(2)}, u32[]{:S(2)}) collective-permute-start(bf16[2,3,128,768]{3,2,1,0:T(8,128)(2,1)} %pad_maximum_fusion.1.refs_0_), channel_id=1, source_target_pairs={{0,4},{4,0},{8,12},{12,8},{16,20},{20,16},{24,28},{28,24},{1,5},{5... | collective-permute-start | bytes 3538952 | tf_op jit(solution)/shard_map/ppermute | solution.py:499
  53.5 22.7 %collective-permute-start.17 = (bf16[2,3,128,768]{3,2,1,0:T(8,128)(2,1)}, bf16[2,3,128,768]{3,2,1,0:T(8,128)(2,1)}, u32[]{:S(2)}, u32[]{:S(2)}) collective-permute-start(bf16[2,3,128,768]{3,2,1,0:T(8,128)(2,1)} %collective-permute-done.15.refs_1_), channel_id=1, source_target_pairs={{0,4},{4,0},{8,12},{12,8},{16,20},{20,16},{24,28},{28,24},{1,5},{5... | collective-permute-start | bytes 3538952 | tf_op jit(solution)/shard_map/ppermute | solution.py:499
  54.3 9.2 %collective-permute-start.6 = (bf16[128,768]{1,0:T(8,128)(2,1)}, bf16[128,768]{1,0:T(8,128)(2,1)S(1)}, u32[]{:S(2)}, u32[]{:S(2)}) collective-permute-start(bf16[128,768]{1,0:T(8,128)(2,1)} %constant_dynamic-slice_fusion.1), channel_id=1, source_target_pairs={{0,3},{1,0},{2,1},{3,2},{4,7},{5,4},{6,5},{7,6},{8,11},{9,8},{10,9... | collective-permute-start | bytes 589832 | tf_op jit(solution)/shard_map/ppermute | solution.py:492
  63.6 10.9 %collective-permute-start.7 = (bf16[3,128,768]{2,1,0:T(8,128)(2,1)S(1)}, bf16[3,128,768]{2,1,0:T(8,128)(2,1)S(1)}, u32[]{:S(2)}, u32[]{:S(2)}) collective-permute-start(bf16[3,128,768]{2,1,0:T(8,128)(2,1)S(1)} %get-tuple-element.19), channel_id=1, source_target_pairs={{0,8},{4,20},{8,0},{12,28},{16,24},{20,4},{24,16},{28,12},{1,9},{5... | collective-permute-start | bytes 1769480 | tf_op jit(solution)/shard_map/ppermute | solution.py:497
  64.3 6.1 %collective-permute-start.2 = (bf16[348,128]{1,0:T(8,128)(2,1)S(1)}, bf16[348,128]{1,0:T(8,128)(2,1)S(1)}, u32[]{:S(2)}, u32[]{:S(2)}) collective-permute-start(bf16[348,128]{1,0:T(8,128)(2,1)S(1)} %pad_maximum_fusion.4), channel_id=1, source_target_pairs={{0,1},{1,2},{2,3},{4,5},{5,6},{6,7},{8,9},{9,10},{10,11},{12,13},{... | collective-permute-start | bytes 267272 | tf_op jit(solution)/shard_map/ppermute | solution.py:481
  68.0 6.5 %collective-permute-start.3 = (bf16[348,128]{1,0:T(8,128)(2,1)S(1)}, bf16[348,128]{1,0:T(8,128)(2,1)S(1)}, u32[]{:S(2)}, u32[]{:S(2)}) collective-permute-start(bf16[348,128]{1,0:T(8,128)(2,1)S(1)} %pad_maximum_fusion.5), channel_id=1, source_target_pairs={{1,0},{2,1},{3,2},{5,4},{6,5},{7,6},{9,8},{10,9},{11,10},{13,12},{... | collective-permute-start | bytes 267272 | tf_op jit(solution)/shard_map/ppermute | solution.py:481
  74.7 21.1 %copy-start.1 = (bf16[2,3,128,768]{3,2,1,0:T(8,128)(2,1)}, bf16[2,3,128,768]{3,2,1,0:T(8,128)(2,1)S(1)}, u32[]{:S(2)}) copy-start(bf16[2,3,128,768]{3,2,1,0:T(8,128)(2,1)S(1)} %pad_maximum_fusion.refs_0_) | copy-start | bytes 3538948
  74.7 22.6 %collective-permute-start.8 = (bf16[2,3,128,768]{3,2,1,0:T(8,128)(2,1)S(1)}, bf16[2,3,128,768]{3,2,1,0:T(8,128)(2,1)S(1)}, u32[]{:S(2)}, u32[]{:S(2)}) collective-permute-start(bf16[2,3,128,768]{3,2,1,0:T(8,128)(2,1)S(1)} %pad_maximum_fusion.refs_0_), channel_id=1, source_target_pairs={{0,16},{4,12},{8,24},{12,4},{16,0},{20,28},{24,8},{28,20},{1,17},{... | collective-permute-start | bytes 3538952 | tf_op jit(solution)/shard_map/ppermute | solution.py:498
  76.2 1.0 copy-start.10
  77.2 18.5 %copy-start.8 = (bf16[8]{0:T(256)(128)(2,1)S(1)}, bf16[8]{0:T(256)(128)(2,1)}, u32[]{:S(2)}) copy-start(bf16[8]{0:T(256)(128)(2,1)} %pad.21.clone) | copy-start | bytes 52
  95.6 5.0 %collective-permute-start.18 = (bf16[400,128]{1,0:T(8,128)(2,1)S(1)}, bf16[400,128]{1,0:T(8,128)(2,1)S(1)}, u32[]{:S(2)}, u32[]{:S(2)}) collective-permute-start(bf16[400,128]{1,0:T(8,128)(2,1)S(1)} %convert_element_type.41), channel_id=1, source_target_pairs={{0,4},{4,8},{8,12},{12,16},{16,20},{20,24},{24,28},{28,0},{1,5},{5... | collective-permute-start | bytes 307208 | tf_op jit(solution)/shard_map/ppermute | solution.py:481
  95.7 44.4 %collective-permute-start.9 = (bf16[2,3,128,768]{3,2,1,0:T(8,128)(2,1)S(1)}, bf16[2,3,128,768]{3,2,1,0:T(8,128)(2,1)S(1)}, u32[]{:S(2)}, u32[]{:S(2)}) collective-permute-start(bf16[2,3,128,768]{3,2,1,0:T(8,128)(2,1)S(1)} %pad_maximum_fusion.refs_0_), channel_id=1, source_target_pairs={{0,4},{4,0},{8,12},{12,8},{16,20},{20,16},{24,28},{28,24},{1,5},{5... | collective-permute-start | bytes 3538952 | tf_op jit(solution)/shard_map/ppermute | solution.py:499
  97.3 26.4 %copy-start.3 = (bf16[2,3,128,768]{3,2,1,0:T(8,128)(2,1)}, bf16[2,3,128,768]{3,2,1,0:T(8,128)(2,1)S(1)}, u32[]{:S(2)}) copy-start(bf16[2,3,128,768]{3,2,1,0:T(8,128)(2,1)S(1)} %collective-permute-done.8.refs_1_) | copy-start | bytes 3538948
  97.3 42.8 %collective-permute-start.10 = (bf16[2,3,128,768]{3,2,1,0:T(8,128)(2,1)S(1)}, bf16[2,3,128,768]{3,2,1,0:T(8,128)(2,1)S(1)}, u32[]{:S(2)}, u32[]{:S(2)}) collective-permute-start(bf16[2,3,128,768]{3,2,1,0:T(8,128)(2,1)S(1)} %collective-permute-done.8.refs_1_), channel_id=1, source_target_pairs={{0,4},{4,0},{8,12},{12,8},{16,20},{20,16},{24,28},{28,24},{1,5},{5... | collective-permute-start | bytes 3538952 | tf_op jit(solution)/shard_map/ppermute | solution.py:499
  97.4 4.1 %collective-permute-start.19 = (bf16[400,128]{1,0:T(8,128)(2,1)S(1)}, bf16[400,128]{1,0:T(8,128)(2,1)S(1)}, u32[]{:S(2)}, u32[]{:S(2)}) collective-permute-start(bf16[400,128]{1,0:T(8,128)(2,1)S(1)} %convert_element_type.41), channel_id=1, source_target_pairs={{4,0},{8,4},{12,8},{16,12},{20,16},{24,20},{28,24},{0,28},{5,1},{9... | collective-permute-start | bytes 307208 | tf_op jit(solution)/shard_map/ppermute | solution.py:481
  101.5 0.7 copy-start.2
  102.2 9.1 %copy-start.6 = (bf16[400]{0:T(512)(128)(2,1)S(1)}, bf16[400]{0:T(512)(128)(2,1)}, u32[]{:S(2)}) copy-start(bf16[400]{0:T(512)(128)(2,1)} %pad.16.clone) | copy-start | bytes 2404
  107.4 5.7 %collective-permute-start.20 = (bf16[320,128]{1,0:T(8,128)(2,1)S(1)}, bf16[320,128]{1,0:T(8,128)(2,1)S(1)}, u32[]{:S(2)}, u32[]{:S(2)}) collective-permute-start(bf16[320,128]{1,0:T(8,128)(2,1)S(1)} %bitcast.57), channel_id=1, source_target_pairs={{0,1},{1,2},{2,3},{4,5},{5,6},{6,7},{8,9},{9,10},{10,11},{12,13},{... | collective-permute-start | bytes 245768 | tf_op jit(solution)/shard_map/ppermute | solution.py:481
  110.0 6.5 %collective-permute-start.21 = (bf16[320,128]{1,0:T(8,128)(2,1)S(1)}, bf16[320,128]{1,0:T(8,128)(2,1)S(1)}, u32[]{:S(2)}, u32[]{:S(2)}) collective-permute-start(bf16[320,128]{1,0:T(8,128)(2,1)S(1)} %bitcast.56), channel_id=1, source_target_pairs={{1,0},{2,1},{3,2},{5,4},{6,5},{7,6},{9,8},{10,9},{11,10},{13,12},{... | collective-permute-start | bytes 245768 | tf_op jit(solution)/shard_map/ppermute | solution.py:481
  140.1 1.1 copy-start.4
  141.2 1.0 copy-start.5

commit v2 on v1

v2 whole, which is shorter than its diff:
```python
import functools

import jax
import jax.numpy as jnp
import numpy as np
from jax import lax
from jax.experimental import pallas as pl
from jax.experimental.pallas import tpu as pltpu
from jax.sharding import PartitionSpec as P

BF = jnp.bfloat16
F32 = jnp.float32
VMEM_LIMIT = 56 * 1024 * 1024
DZ, DY, DX = 7, 12, 12
SK, SY, SX = 5, 8, 8
GROUP = 8


def params():
    return pltpu.CompilerParams(vmem_limit_bytes=VMEM_LIMIT)


def spread_matrix(nk, ni, nx):
    rows = np.arange(nk * nx)[:, None]
    cols = np.arange(DX * nk * ni)[None, :]
    dx, k, i = cols // (nk * ni), cols // ni % nk, cols % ni
    return ((rows // nx == k) & (rows % nx == SX * i - 2 + dx)).astype(BF)


def edge_lanes(nv, nk):
    lane = np.arange(4 * nv * nk)
    return lane // (2 * nv * nk), lane // (2 * nk) % nv, lane // nk % 2, lane % nk


def pick_matrix(nv, nk, nx):
    side, v, c, k = edge_lanes(nv, nk)
    rows = np.arange(nk * nx)[None, :, None]
    x = np.where(side == 0, nx - 2 + c, c)
    own = np.arange(nv)[:, None, None] == v
    return (own & (rows // nx == k) & (rows % nx == x)).astype(BF)


def edge_matrix(nv, nk, ni):
    side, v, c, k = (np.tile(a, 2)[None, :, None] for a in edge_lanes(nv, nk))
    half = (np.arange(8 * nv * nk) // (4 * nv * nk))[None, :, None]
    cols = np.arange(4 * nk * ni)[None, None, :]
    d, kk, i = cols // (nk * ni), cols // ni % nk, cols % ni
    own = np.arange(nv)[:, None, None] == v
    left = (half == 0) & (side == 0) & (i == 0) & (d == c)
    right = (half == 1) & (side == 1) & (i == ni - 1) & (d == 2 + c)
    return (own & (k == kk) & (left | right)).astype(BF)


def column_lanes(nk, nj):
    tall = nj + 2
    lanes = -(-2 * nk * tall // 128) * 128
    return tall, lanes


def decode_matrix(nk, nj, ni, nx):
    tall, lanes = column_lanes(nk, nj)
    rows = np.arange(nk * nx)[:, None]
    cols = np.arange(2 * lanes)[None, :]
    c, lane = cols // lanes, cols % lanes
    side, k = lane // (nk * tall), lane // tall % nk
    x = np.where(side == 0, c, nx - 2 + c)
    beside = (side < 2) & (rows // nx == k) & (rows % nx == x)
    return np.concatenate([spread_matrix(nk, ni, nx), beside.astype(BF)], axis=1)


def stack_levels(read, levels, nk, zeros, lhs, at, rows, dz):
    for k in range(nk):
        level = SK * k - 1 + dz
        block = read(level) if 0 <= level < levels else zeros
        lhs[at : at + rows, k * 128 : (k + 1) * 128] = block


def pack_kernel(nk, vol, pick, dep, out, lhs, acc):
    v = pl.program_id(0)
    _, levels, ny, nx = vol.shape
    for dz in range(DZ):
        stack_levels(lambda l: vol[0, l].astype(BF), levels, nk, jnp.zeros((ny, nx), BF), lhs, dz * ny, ny, dz)
    part = jnp.dot(lhs[...], pick[0], preferred_element_type=F32)

    @pl.when(v == 0)
    def _():
        acc[...] = part

    @pl.when(v > 0)
    def _():
        acc[...] += part

    @pl.when(v == pl.num_programs(0) - 1)
    def _():
        out[...] = acc[...].astype(BF)


def im2col_kernel(nk, ni, nj, shard, with_own, vol, rim, edge, spread, edge_hot, dep, dep2, *refs):
    if with_own:
        own, weight, out, sums, lhs, q, w_buf, w_sem = refs
    else:
        out, lhs, q = refs
    v = pl.program_id(0)
    if with_own:
        copies = weight_copies(False, (weight,), 0, 0, w_buf, w_sem)

        @pl.when(v == 0)
        def _():
            for c in copies:
                c.start()

    _, levels, ny, nx = vol.shape
    main = DZ * ny
    for dz in range(DZ):
        stack_levels(lambda l: vol[0, l].astype(BF), levels, nk, jnp.zeros((ny, nx), BF), lhs, dz * ny, ny, dz)
    none = jnp.zeros((8, nx), F32)
    for k in range(nk):
        blocks = []
        for dz in range(DZ + 1):
            level = SK * k - 1 + dz
            blocks.append(rim[0, level] if 0 <= level < levels and dz < DZ else none)
        lhs[main : main + 64, k * 128 : (k + 1) * 128] = jnp.concatenate(blocks, axis=0).astype(BF)
    for pair in range(DX // 2):
        got = jnp.dot(lhs[...], spread[:, pair * 256 : (pair + 1) * 256], preferred_element_type=F32)
        if pair in (0, DX // 2 - 1):
            which = 0 if pair == 0 else 1
            got += jnp.dot(edge[...], edge_hot[0, :, which * 256 : (which + 1) * 256], preferred_element_type=F32)
        for h in range(2):
            dx = 2 * pair + h
            mine = got[:, h * 128 : (h + 1) * 128]
            for dz in range(DZ):
                q[dz, pl.ds(2 * DX + dx, ny, stride=DX), :] = mine[dz * ny : (dz + 1) * ny]
                at = main + 8 * dz
                q[dz, pl.ds(dx, 2, stride=DX), :] = mine[at : at + 2]
                q[dz, pl.ds(DX * (ny + 2) + dx, 2, stride=DX), :] = mine[at + 2 : at + 4]
    rows, padded, piece = shard
    head = piece * (GROUP - 1)
    per = SY * DX
    for j in range(nj):
        columns = jnp.concatenate([q[dz, per * j : per * j + DY * DX, :] for dz in range(DZ)], axis=0)
        gap = jnp.zeros((padded - rows, 128), F32)
        columns = jnp.concatenate([columns[:head], gap, columns[head:]], axis=0)
        out[0, j] = columns.T.astype(BF)
    if with_own:

        @pl.when(v == 0)
        def _():
            for c in copies:
                c.wait()

        @pl.when(v == own[0])
        def _():
            windows = out[0].reshape(nj * nk * ni, padded)
            sums[...] = jnp.dot(windows, w_buf[...], preferred_element_type=F32)


def weight_copies(gathered, sources, step, me, slot, sems):
    padded = slot.shape[0]
    piece = padded // GROUP
    if not gathered:
        (source,) = sources
        rows = source.shape[1]
        head = piece * (GROUP - 1)
        return [
            pltpu.make_async_copy(source.at[step, pl.ds(0, head)], slot.at[pl.ds(0, head)], sems.at[0]),
            pltpu.make_async_copy(source.at[step, pl.ds(rows - piece, piece)], slot.at[pl.ds(head, piece)], sems.at[1]),
        ]
    core = lax.rem(me, 2)
    a, b = 2 + 2 * core, 4 - 2 * core
    distances = ((0, a), (b, 6), (1, 1 + b), (1 + a, 7))
    copies = []
    for n, (source, pair) in enumerate(zip(sources, distances)):
        for h, distance in enumerate(pair):
            place = pl.multiple_of(lax.bitwise_xor(me, jnp.int32(distance)) * piece, piece)
            copies.append(
                pltpu.make_async_copy(source.at[h, step], slot.at[pl.ds(place, piece)], sems.at[2 * n + h])
            )
    return copies


def embed_kernel(n, gathered, first, vid, me, a, *refs):
    n_w = 4 if gathered else 1
    sources, refs = refs[:n_w], refs[n_w:]
    if not first:
        prev, refs = refs[0], refs[1:]
    out, a_buf, w_buf, acc, before, a_sem, w_sem, p_sem = refs

    def copies(s):
        slot = s % 2
        return [pltpu.make_async_copy(a.at[vid[s]], a_buf.at[slot], a_sem.at[slot])] + weight_copies(
            gathered, sources, s, me[0], w_buf.at[slot], w_sem.at[slot]
        )

    for c in copies(0):
        c.start()
    for s in range(n):
        for c in copies(s):
            c.wait()
        if s + 1 < n:
            for c in copies(s + 1):
                c.start()
        if s == max(n - 2, 0) and not first:
            extra = pltpu.make_async_copy(prev, before, p_sem)
            extra.start()
        got = jnp.dot(a_buf[s % 2], w_buf[s % 2], preferred_element_type=F32)
        if s > 0:
            got += acc[...]
        if s < n - 1:
            acc[...] = got
            continue
        if not first:
            extra.wait()
            got += before[...]
        nk, nj, ni, width = out.shape
        for j in range(nj):
            out[:, j] = got[j * nk * ni : (j + 1) * nk * ni].astype(BF).reshape(nk, ni, width)


def unembed_kernel(kinds, vid, me, tokens, above, below, left, right, hot_hbm, own, dep, *refs):
    gathered = any(kind is not None for kind in kinds)
    sources, refs = (refs[:4], refs[4:]) if gathered else ((), refs)
    if kinds[0] is not None:
        refs = refs[1:]
    vol, w_buf, t, t_side, r, q, qc, lhs, hot, w_sem, t_sem, hot_sem = refs
    s, n = pl.program_id(0), pl.num_programs(0)
    nk, nj, ni, width = tokens.shape
    _, levels, ny, nx = vol.shape
    per, over, block = SY * DX, (DY - SY) * DX, DY * DX
    padded = w_buf.shape[1]
    head, gap = padded // GROUP * (GROUP - 1), padded - DZ * block
    tall, c_lanes = column_lanes(nk, nj)
    half = nk * tall
    row = nk * ni
    c_at = (nj + 2) * row

    def copies(step, kind):
        slot = lax.rem(step, 2)
        if kind is None:
            return weight_copies(False, (own,), step, 0, w_buf.at[slot], w_sem.at[slot])
        return weight_copies(True, sources, kind + step, me[0], w_buf.at[slot], w_sem.at[slot])

    begin = None if kinds[0] is None else kinds[0]
    rest = None if kinds[-1] is None else kinds[-1] - len(kinds) + 1
    hot_copy = pltpu.make_async_copy(hot_hbm, hot, hot_sem)
    token_copies = [pltpu.make_async_copy(tokens.at[:, j], t.at[j], t_sem.at[j]) for j in range(nj)] + [
        pltpu.make_async_copy(above, t.at[nj], t_sem.at[nj]),
        pltpu.make_async_copy(below, t.at[nj + 1], t_sem.at[nj + 1]),
        pltpu.make_async_copy(left, t_side.at[pl.ds(0, half)], t_sem.at[nj + 2]),
        pltpu.make_async_copy(right, t_side.at[pl.ds(half, half)], t_sem.at[nj + 3]),
    ]

    @pl.when(s == 0)
    def _():
        for c in copies(s, begin) + token_copies:
            c.start()
        hot_copy.start()
        if c_lanes > 2 * half:
            t_side[2 * half :, :] = jnp.zeros((c_lanes - 2 * half, width), BF)

    @pl.when(s == 0)
    def _():
        for c in copies(s, begin) + token_copies:
            c.wait()

    @pl.when(s > 0)
    def _():
        for c in copies(s, rest):
            c.wait()

    @pl.when(s + 1 < n)
    def _():
        for c in copies(s + 1, rest):
            c.start()

    weight = w_buf[lax.rem(s, 2)]
    for ref, start, stop in ((t, 0, c_at), (t_side, c_at, c_at + c_lanes)):
        r[:, start:stop] = lax.dot_general(
            weight, ref[...].reshape(-1, width), (((1,), (1,)), ((), ())), preferred_element_type=F32
        )

    def rows_of(dz, at, start, stop, lanes=128):
        lo, hi = dz * block + start, dz * block + stop
        if hi <= head:
            return r[lo:hi, at : at + lanes]
        if lo >= head:
            return r[lo + gap : hi + gap, at : at + lanes]
        return jnp.concatenate([r[lo:head, at : at + lanes], r[head + gap : hi + gap, at : at + lanes]], axis=0)

    up, down = nj * row, (nj + 1) * row
    lane = lax.broadcasted_iota(jnp.int32, (8, c_lanes), 1)[:1]
    side, place = lane // half, lax.rem(lane, tall)
    edge2 = 2 * DX
    for dz in range(DZ):
        for j in range(nj + 1):
            at = per * j
            first, last = (edge2 if j == 0 else 0), (edge2 if j == nj else over)
            before = up if j == 0 else (j - 1) * row
            after = down if j == nj else j * row
            q[dz, at + first : at + last, :] = rows_of(dz, after, first, last) + rows_of(
                dz, before, per + first, per + last
            )
            qc[dz, at + first : at + last, :] = jnp.where(
                place == j + 1,
                rows_of(dz, c_at, first, last, c_lanes),
                jnp.where(place == j, rows_of(dz, c_at, per + first, per + last, c_lanes), 0.0),
            )
            if j < nj:
                q[dz, at + over : at + per, :] = rows_of(dz, after, over, per)
                qc[dz, at + over : at + per, :] = jnp.where(place == j + 1, rows_of(dz, c_at, over, per, c_lanes), 0.0)
    for dz in range(DZ):
        rows = slice(dz * ny, (dz + 1) * ny)
        for dx in range(DX):
            lhs[rows, dx * row : (dx + 1) * row] = q[dz, pl.ds(2 * DX + dx, ny, stride=DX), :].astype(BF)
        for c in range(2):
            far = qc[dz, pl.ds(2 * DX + DX - 2 + c, ny, stride=DX), :]
            near = qc[dz, pl.ds(2 * DX + c, ny, stride=DX), :]
            at = DX * row + c * c_lanes
            lhs[rows, at : at + c_lanes] = jnp.where(side == 0, far, near).astype(BF)

    @pl.when(s == 0)
    def _():
        hot_copy.wait()

    carry = None
    for pair in range(nk // 2):
        got = lax.dot_general(
            lhs[...], hot[pair * 256 : (pair + 1) * 256, :], (((1,), (1,)), ((), ())), preferred_element_type=F32
        )
        for h in range(2):
            k = 2 * pair + h
            mine = got[:, h * 128 : (h + 1) * 128]
            for dz in range(DZ):
                level = SK * k - 1 + dz
                here = mine[dz * ny : (dz + 1) * ny]
                if dz < DZ - SK and k > 0:
                    here = here + carry[dz]
                if 0 <= level < levels and (dz < SK or k == nk - 1):
                    vol[0, level] = here
            carry = [mine[dz * ny : (dz + 1) * ny] for dz in range(SK, DZ)]


def whole(shape):
    return pl.BlockSpec(shape, lambda *_: (0,) * len(shape))


def lead(shape):
    return pl.BlockSpec((1,) + tuple(shape[1:]), lambda v, *_: (v,) + (0,) * (len(shape) - 1))


HBM = pl.BlockSpec(memory_space=pltpu.HBM)


def cost(flops, bytes_accessed):
    return pl.CostEstimate(flops=int(flops), bytes_accessed=int(bytes_accessed), transcendentals=0)


def pack_edges(volume, nk, dep):
    nv, levels, ny, nx = volume.shape
    pick = pick_matrix(nv, nk, nx)
    return pl.pallas_call(
        functools.partial(pack_kernel, nk),
        grid=(nv,),
        in_specs=[lead(volume.shape), lead(pick.shape), HBM],
        out_specs=whole((DZ * ny, 128)),
        out_shape=jax.ShapeDtypeStruct((DZ * ny, 128), BF),
        scratch_shapes=[pltpu.VMEM((DZ * ny, nk * nx), BF), pltpu.VMEM((DZ * ny, 128), F32)],
        compiler_params=params(),
        cost_estimate=cost(2 * nv * DZ * ny * nk * nx * 256, volume.size * 4),
        name="pack_edges",
    )(volume, pick, dep)


def im2col(volume, rim, edge, spread, dims, own, weight, dep):
    nk, nj, ni, padded = dims
    nv, levels, ny, nx = volume.shape
    hot = edge_matrix(nv, nk, ni)
    rows = DZ * ny + 64
    shape = (nv, nj, nk * ni, padded)
    width = None if weight is None else weight.shape[-1]
    with_own = weight is not None
    extra_specs, extra, extra_out, extra_scratch = [], [], [], []
    if with_own:
        extra_specs, extra = [pl.BlockSpec(memory_space=pltpu.SMEM), HBM], [own, weight]
        extra_out = [(nj * nk * ni, width)]
        extra_scratch = [pltpu.VMEM((padded, width), BF), pltpu.SemaphoreType.DMA((2,))]
    return pl.pallas_call(
        functools.partial(im2col_kernel, nk, ni, nj, (DZ * DY * DX, padded, padded // GROUP), with_own),
        grid=(nv,),
        in_specs=[lead(volume.shape), lead(rim.shape), whole(edge.shape), whole(spread.shape), lead(hot.shape), HBM, HBM]
        + extra_specs,
        out_specs=[lead(shape)] + [whole(x) for x in extra_out],
        out_shape=[jax.ShapeDtypeStruct(shape, BF)] + [jax.ShapeDtypeStruct(x, F32) for x in extra_out],
        scratch_shapes=[pltpu.VMEM((rows, nk * nx), BF), pltpu.VMEM((DZ, DX * (ny + 4), 128), F32)] + extra_scratch,
        compiler_params=params(),
        cost_estimate=cost(3 * nv * rows * nk * nx * DX * 128, volume.size * 4 + 2 * nv * nj * 128 * padded),
        name="im2col",
    )(volume, rim, edge, spread, hot, *dep, *extra)


def embed(a, weights, vid, me, prev, gathered, token_shape):
    n = vid.shape[0]
    nv, rows, padded = a.shape
    width = weights[0].shape[-1]
    first = prev is None
    smem = pl.BlockSpec(memory_space=pltpu.SMEM)
    return pl.pallas_call(
        functools.partial(embed_kernel, n, gathered, first),
        in_specs=[smem, smem, HBM] + [HBM] * (len(weights) + (not first)),
        out_specs=pl.BlockSpec(memory_space=pltpu.VMEM),
        out_shape=jax.ShapeDtypeStruct(token_shape, BF),
        scratch_shapes=[
            pltpu.VMEM((2, rows, padded), BF),
            pltpu.VMEM((2, padded, width), BF),
            pltpu.VMEM((rows, width), F32),
            pltpu.VMEM((8, 128) if first else (rows, width), F32),
            pltpu.SemaphoreType.DMA((2,)),
            pltpu.SemaphoreType.DMA((2, GROUP)),
            pltpu.SemaphoreType.DMA,
        ],
        compiler_params=params(),
        cost_estimate=cost(2 * n * rows * padded * width, 2 * n * padded * (rows + width) + 4 * rows * width),
        name="embed",
    )(vid, me, a, *weights, *([] if first else [prev]))


def unembed(tokens, beside, own, gathered, kinds, vid, me, prev, dep, volume_shape, padded):
    nk, nj, ni, width = tokens.shape
    nv, levels, ny, nx = volume_shape
    hot = decode_matrix(nk, nj, ni, nx)
    tall, c_lanes = column_lanes(nk, nj)
    before = () if prev is None else (prev,)
    n = len(kinds)
    count = (nj + 2) * nk * ni + c_lanes
    return pl.pallas_call(
        functools.partial(unembed_kernel, kinds),
        grid_spec=pltpu.PrefetchScalarGridSpec(
            num_scalar_prefetch=2,
            grid=(len(kinds),),
            in_specs=[HBM] * (4 + len(beside) + len(gathered) + len(before)),
            out_specs=pl.BlockSpec((1, levels, ny, nx), lambda s, vid, me: (vid[s], 0, 0, 0)),
            scratch_shapes=[
                pltpu.VMEM((2, padded, width), BF),
                pltpu.VMEM((nj + 2, nk, ni, width), BF),
                pltpu.VMEM((c_lanes, width), BF),
                pltpu.VMEM((padded, count), F32),
                pltpu.VMEM((DZ, DX * (ny + 4), nk * ni), F32),
                pltpu.VMEM((DZ, DX * (ny + 4), c_lanes), F32),
                pltpu.VMEM((DZ * ny, hot.shape[1]), BF),
                pltpu.VMEM(hot.shape, BF),
                pltpu.SemaphoreType.DMA((2, GROUP)),
                pltpu.SemaphoreType.DMA((nj + 4,)),
                pltpu.SemaphoreType.DMA,
            ],
        ),
        out_shape=jax.ShapeDtypeStruct(volume_shape, F32),
        input_output_aliases={} if prev is None else {len(beside) + 6 + len(gathered): 0},
        compiler_params=params(),
        cost_estimate=cost(8 * n * padded * width * nj * 128, 2 * n * padded * width + 4 * n * levels * ny * nx),
        name="unembed",
    )(vid, me, tokens, *beside, hot, own, dep, *gathered, *before)


def both_ways(up_rows, down_rows, axis, wrap):
    size = lax.axis_size(axis)
    up = [(i, (i + 1) % size) for i in range(size if wrap else size - 1)]
    return lax.ppermute(up_rows, axis, up), lax.ppermute(down_rows, axis, [(j, i) for i, j in up])


def piece_rows(rows):
    return -(-rows // (16 * GROUP)) * 16


def after(x, *others):
    return lax.optimization_barrier((x,) + others)[0]


def own_piece(weight, me):
    rows, piece = weight.shape[0], piece_rows(weight.shape[0])
    return lax.dynamic_slice_in_dim(weight, jnp.minimum(me * piece, rows - piece), piece, 0)


def from_lat(piece):
    size = lax.axis_size("lat")
    got = [lax.ppermute(piece, "lat", [(i, (i + s) % size) for i in range(size)]) for s in range(1, size)]
    return got


def flip(x, mask):
    return lax.ppermute(x, "lon", [(i, i ^ mask(i)) for i in range(lax.axis_size("lon"))])


def first_mask(i):
    return 2 + 2 * (i & 1)


def second_mask(i):
    return 4 - 2 * (i & 1)


def core_mask(i):
    return 1


def per_device(volume_b, tokens_a, embed_weight, unembed_weight):
    nk, nj, ni, width = tokens_a.shape
    nv, levels, ny, nx = volume_b.shape
    rows = DZ * DY * DX
    padded = piece_rows(rows) * GROUP
    main = DZ * ny
    lat, lats = lax.axis_index("lat"), lax.axis_size("lat")
    me = lax.rem(lax.axis_index("lon"), GROUP).astype(jnp.int32)
    me1 = me.reshape(1)
    fast = embed_weight.shape[0] == rows and lax.axis_size("lon") % GROUP == 0
    spread = spread_matrix(nk, ni, nx)

    row_above, row_below = both_ways(tokens_a[:, nj - 1], tokens_a[:, 0], "lat", False)

    start = volume_b
    if fast:
        start = own_piece(unembed_weight, me)
        u_near = from_lat(start)
    packed = pack_edges(volume_b, nk, start)
    from_left, from_right = both_ways(packed, packed, "lon", True)

    def column(i):
        return jnp.concatenate([row_above[:, i][:, None], tokens_a[:, :, i], row_below[:, i][:, None]], axis=1)

    left, right = both_ways(column(ni - 1), column(0), "lon", True)
    beside = [row_above, row_below, left.reshape(-1, width), right.reshape(-1, width)]

    def lat_rows(at):
        voxels = volume_b[:, :, at : at + 2].astype(BF).reshape(-1, nx)
        corners = [a.reshape(DZ, ny, 128)[:, at : at + 2].reshape(-1, 128) for a in (from_left, from_right)]
        return jnp.concatenate([voxels] + corners, axis=0)

    above, below = both_ways(lat_rows(ny - 2), lat_rows(0), "lat", False)
    n_vox = nv * levels * 2

    def split(got):
        voxels = got[:n_vox].reshape(nv, levels, 2, nx)
        corners = got[n_vox:].reshape(2, DZ, 2, 128)
        return voxels, jnp.concatenate([corners[0], corners[1]], axis=-1)

    (vox_above, cor_above), (vox_below, cor_below) = split(above), split(below)
    rim = jnp.concatenate([vox_above, vox_below, jnp.zeros((nv, levels, 4, nx), BF)], axis=2).astype(F32)
    corners = jnp.concatenate([cor_above, cor_below, jnp.zeros((DZ, 4, 256), BF)], axis=1).reshape(8 * DZ, 256)
    edge = jnp.concatenate(
        [jnp.concatenate([from_left, from_right], axis=1), corners, jnp.zeros((64 - 8 * DZ, 256), BF)], axis=0
    )
    dims = (nk, nj, ni, padded)
    tokens = nj * nk * ni

    if fast:
        u_near = jnp.stack(u_near)
        u_pair = jnp.stack([u_near, after(flip(u_near, first_mask), row_above, row_below)])
        u_rest = flip(u_pair, second_mask)
        e_near = from_lat(after(own_piece(embed_weight, me), u_near))
        own = lat.astype(jnp.int32).reshape(1)
        others = lax.rem(lat - jnp.arange(1, lats, dtype=jnp.int32) + lats, lats).astype(jnp.int32)
        a, sums = im2col(volume_b, rim, edge, spread, dims, own, embed_weight[None], (u_pair, edge))
        u_rest = after(u_rest, sums)
        u_all = (u_pair, u_rest, flip(u_pair, core_mask), flip(u_rest, core_mask))
        e_near = jnp.stack(e_near)
        e_far = flip(after(e_near, sums), first_mask)
        first_two = jnp.concatenate([own, others[:1]])
        volume_a = unembed(
            tokens_a, beside, unembed_weight[None], u_all, (None, 0), first_two, me1, None, e_near, volume_b.shape, padded
        )
        e_pair = jnp.stack([e_near, after(e_far, volume_a)])
        e_rest = flip(e_pair, second_mask)
        volume_a = unembed(
            tokens_a, beside, unembed_weight[None], u_all, (1, 2), others[1:], me1, volume_a, e_pair, volume_b.shape, padded
        )
        e_rest = after(e_rest, volume_a)
        e_all = (e_pair, e_rest, flip(e_pair, core_mask), flip(e_rest, core_mask))
        tokens_b = embed(a.reshape(nv, tokens, padded), e_all, others, me1, sums, True, tokens_a.shape)
    else:
        every = jnp.arange(nv, dtype=jnp.int32)
        decode, encode = (
            lax.all_gather(w, "lat", axis=0, tiled=True).reshape(nv, rows, width)
            for w in (unembed_weight, embed_weight)
        )
        (a,) = im2col(volume_b, rim, edge, spread, dims, None, None, (edge, edge))
        volume_a = unembed(
            tokens_a, beside, decode, (), (None,) * nv, every, me1, None, edge, volume_b.shape, padded
        )
        tokens_b = embed(
            a.reshape(nv, tokens, padded), (encode,), every, me1, None, False, tokens_a.shape
        )
    return tokens_b, volume_a


def solution(mesh):
    placed = (
        P(None, None, "lat", "lon"),
        P(None, "lat", "lon", None),
        P("lat", None),
        P("lat", None),
    )
    return jax.shard_map(
        per_device,
        mesh=mesh,
        in_specs=placed,
        out_specs=(P(None, "lat", "lon", None), P(None, None, "lat", "lon")),
        check_vma=False,
    )
```

time: 154 us -> 133 us (0.86)
  other arithmetic: 21.4 us -> 4.51 us
  Pallas kernels: 67.7 us -> 56.3 us
  starting transfers between devices: 29.9 us -> 34.3 us
  waiting for transfers between devices: 23.5 us -> 25.5 us
    pallas_call x6 -> x3, Pallas kernels: 51.7 us -> 37.8 us  [the longest x2 27.8 us: unembed(): pl.pallas_call(functools.partial(unembed_kernel, kinds), grid_spec=pltpu....]
    convert_element_type x7 -> x1, other arithmetic: 12.4 us -> 1.01 us  [per_device(): jnp.concatenate([vox_above, vox_below, jnp.zeros((nv, levels, 4, nx), BF)...]
    ppermute x14, waiting for transfers between devices: 12.4 us -> 23.7 us  [the longest x6 20.4 us: from_lat(): lax.ppermute(piece, 'lat', [(i, (i + s) % size) for i in range(size)])]
    ppermute x4, waiting for transfers between devices: 8.4 us -> 0.31 us  [both_ways(): lax.ppermute(down_rows, axis, [(j, i) for i, j in up])]
    ppermute x4, starting transfers between devices: 6.31 us -> 10.4 us  [both_ways(): lax.ppermute(up_rows, axis, up)]
    another operation x6 -> x5, other arithmetic: 3.87 us -> 0.66 us  [the longest x4 2.47 us: gather_rows(): pair = jnp.stack([near, lax.ppermute(near, 'lon', first)])]
    slice x1 -> x8, local copies, waits for them, and re-layouts: 0.11 us -> 2.79 us  [the longest x3 1 us: column(): row_above[:, i][:, None]]
    pallas_call x1, Pallas kernels: 11.6 us -> 13.8 us  [im2col(): pl.pallas_call(functools.partial(im2col_kernel, nk, ni, nj, (DZ * DY * DX...]
  transfers between devices with their start and end apart: 22 -> 22, of which waited for: 8 -> 8; matrix products, arithmetic and copies ran while one was open for 17% -> 7% of each run, Pallas kernels for 37% -> 31%
where the time goes in v2:
time: 133 us; the launch traced here: 132 us
  Pallas kernels  56.3 us (42%)
  starting transfers between devices  34.3 us (26%)
  waiting for transfers between devices  25.5 us (19%)
  local copies, waits for them, and re-layouts  10.5 us (8%)
  other arithmetic  4.51 us (3%)
    pallas_call x2, Pallas kernels, unembed(): pl.pallas_call(functools.partial(unembed_kernel, kinds), grid_spec=pltpu....  27.8 us
    ppermute x6, waiting for transfers between devices, from_lat(): lax.ppermute(piece, 'lat', [(i, (i + s) % size) for i in range(size)])  20.4 us
    pallas_call x1, Pallas kernels, im2col(): pl.pallas_call(functools.partial(im2col_kernel, nk, ni, nj, (DZ * DY * DX...  13.8 us
    ppermute x6, starting transfers between devices, from_lat(): lax.ppermute(piece, 'lat', [(i, (i + s) % size) for i in range(size)])  11.3 us
    ppermute x4, starting transfers between devices, both_ways(): lax.ppermute(up_rows, axis, up)  10.4 us
    pallas_call x1, Pallas kernels, embed(): pl.pallas_call(functools.partial(embed_kernel, n, gathered, first), in_sp...  10 us
    ppermute x4, starting transfers between devices, both_ways(): lax.ppermute(down_rows, axis, [(j, i) for i, j in up])  8.53 us
    pallas_call x1, Pallas kernels, pack_edges(): pl.pallas_call(functools.partial(pack_kernel, nk), grid=(nv,), in_specs=[...  4.68 us
  transfers between devices with their start and end apart: 22, of which 8 were waited for; matrix products, arithmetic and copies ran while one was open for 7% of the time, Pallas kernels for 31%

profile of v2, /device:TPU:0, one launch (start us, length us, event | category | flops | bytes accessed | tf_op | source)
XLA Modules:
  0.0 132.3 jit_solution(17412277432431479065)
XLA Ops:
  0.6 1.7 %constant_dynamic-slice_fusion.1.dep = bf16[128,768]{1,0:T(8,128)(2,1)} fusion(bf16[1008,768]{1,0:T(8,128)(2,1)} %param.12, s32[]{:T(128)S(6)} %select_n.4), kind=kLoop, calls=%fused_computation.22 | loop fusion | bytes 393220 | tf_op jit(solution)/shard_map/dynamic_slice | solution.py:479
  2.3 4.7 %pack_edges.1 = bf16[336,128]{1,0:T(8,128)(2,1)} custom-call(f32[4,40,48,128]{3,2,1,0:T(8,128)} %vol.3, bf16[4,1024,128]{2,1,0:T(8,128)(2,1)} %constant.40.clone.pick, bf16[128,768]{1,0:T(8,128)(2,1)} %constant_dynamic-slice_fusion.1.dep), custom_call_target="tpu_custom_call" | custom-call | flops 704643072 | bytes 3932160 | tf_op jit(solution)/shard_map/pack_edges/pallas_call | solution.py:360
  7.0 3.3 %collective-permute-start.1 = (bf16[336,128]{1,0:T(8,128)(2,1)}, bf16[336,128]{1,0:T(8,128)(2,1)S(1)}, u32[]{:S(2)}, u32[]{:S(2)}) collective-permute-start(bf16[336,128]{1,0:T(8,128)(2,1)} %pack_edges.1), channel_id=1, source_target_pairs={{4,0},{8,4},{12,8},{16,12},{20,16},{24,20},{28,24},{0,28},{5,1},{9... | collective-permute-start | bytes 258056 | tf_op jit(solution)/shard_map/ppermute | solution.py:466
  10.3 3.6 %collective-permute-start.6 = (bf16[128,768]{1,0:T(8,128)(2,1)S(1)}, bf16[128,768]{1,0:T(8,128)(2,1)S(1)}, u32[]{:S(2)}, u32[]{:S(2)}) collective-permute-start(bf16[128,768]{1,0:T(8,128)(2,1)S(1)} %copy-done.6), channel_id=1, source_target_pairs={{0,3},{1,0},{2,1},{3,2},{4,7},{5,4},{6,5},{7,6},{8,11},{9,8},{10,9... | collective-permute-start | bytes 589832 | tf_op jit(solution)/shard_map/ppermute | solution.py:484
  13.9 1.0 collective-permute-start.4
  14.9 0.3 convert.4
  15.3 0.1 fusion.3
  15.6 1.3 collective-permute-start.9
  16.9 5.7 %collective-permute-start.8 = (bf16[8,16,768]{2,1,0:T(8,128)(2,1)S(1)}, bf16[8,16,768]{2,1,0:T(8,128)(2,1)}, u32[]{:S(2)}, u32[]{:S(2)}) collective-permute-start(bf16[8,16,768]{2,1,0:T(8,128)(2,1)S(1)} %get-tuple-element.23), channel_id=1, source_target_pairs={{0,1},{1,2},{2,3},{4,5},{5,6},{6,7},{8,9},{9,10},{10,11},{12,13},{... | collective-permute-start | bytes 589832 | tf_op jit(solution)/shard_map/ppermute | solution.py:466
  22.7 8.8 %collective-permute-done.5 = bf16[128,768]{1,0:T(8,128)(2,1)S(1)} collective-permute-done((bf16[128,768]{1,0:T(8,128)(2,1)S(1)}, bf16[128,768]{1,0:T(8,128)(2,1)S(1)}, u32[]{:S(2)}, u32[]{:S(2)}) %collective-permute-start.5) | collective-permute-done | bytes 196640 | tf_op jit(solution)/shard_map/ppermute | solution.py:484
  31.7 0.7 pad_maximum_fusion.7
  32.4 1.3 collective-permute-start.3
  33.7 0.6 pad_maximum_fusion.6
  34.3 4.5 %collective-permute-start.2 = (bf16[348,128]{1,0:T(8,128)(2,1)}, bf16[348,128]{1,0:T(8,128)(2,1)S(1)}, u32[]{:S(2)}, u32[]{:S(2)}) collective-permute-start(bf16[348,128]{1,0:T(8,128)(2,1)} %pad_maximum_fusion.6), channel_id=1, source_target_pairs={{0,1},{1,2},{2,3},{4,5},{5,6},{6,7},{8,9},{9,10},{10,11},{12,13},{... | collective-permute-start | bytes 267272 | tf_op jit(solution)/shard_map/ppermute | solution.py:466
  38.9 0.3 collective-permute-done.3
  39.2 0.6 copy-done.13
  39.8 1.5 %collective-permute-done.2 = bf16[348,128]{1,0:T(8,128)(2,1)S(1)} collective-permute-done((bf16[348,128]{1,0:T(8,128)(2,1)}, bf16[348,128]{1,0:T(8,128)(2,1)S(1)}, u32[]{:S(2)}, u32[]{:S(2)}) %collective-permute-start.2) | collective-permute-done | bytes 89120 | tf_op jit(solution)/shard_map/ppermute | solution.py:466
  41.4 0.2 collective-permute-done.7
  41.7 1.2 collective-permute-start.16
  43.0 0.8 maximum_maximum_fusion.edge.dep2
  43.8 1.0 maximum_convert_fusion.rim
  44.9 13.8 %im2col.1 = (bf16[4,6,128,1024]{3,2,1,0:T(8,128)(2,1)}, f32[768,768]{1,0:T(8,128)}) custom-call(f32[4,40,48,128]{3,2,1,0:T(8,128)} %vol.3, f32[4,40,8,128]{3,2,1,0:T(8,128)} %maximum_convert_fusion.rim, bf16[400,256]{1,0:T(8,128)(2,1)} %maximum_maximum_fusion.edge.dep2, bf16[1024,1536]{1,0:T(8,128)(2,1)} %constant.41.clone.spread, ...), custom_call_target="tpu_custom_call" | custom-call | flops 7549747200 | bytes 10223616 | tf_op jit(solution)/shard_map/im2col/pallas_call | solution.py:386
  58.7 0.6 collective-permute-start.18
  59.3 0.2 fusion.4
  59.6 1.0 fusion.6
  60.6 1.0 fusion.5
  61.6 0.1 collective-permute-start.14
  61.7 2.6 %collective-permute-start.15 = (bf16[8,8,768]{2,0,1:T(8,128)(2,1)S(1)}, bf16[8,8,768]{2,0,1:T(8,128)(2,1)S(1)}, u32[]{:S(2)}, u32[]{:S(2)}) collective-permute-start(bf16[8,8,768]{2,0,1:T(8,128)(2,1)S(1)} %pad_maximum_fusion.5), channel_id=1, source_target_pairs={{4,0},{8,4},{12,8},{16,12},{20,16},{24,20},{28,24},{0,28},{5,1},{9... | collective-permute-start | bytes 294920 | tf_op jit(solution)/shard_map/ppermute | solution.py:466
  64.4 1.0 constant_dynamic-slice_fusion
  65.4 5.0 %collective-permute-start.12 = (bf16[128,768]{1,0:T(8,128)(2,1)S(1)}, bf16[128,768]{1,0:T(8,128)(2,1)S(1)}, u32[]{:S(2)}, u32[]{:S(2)}) collective-permute-start(bf16[128,768]{1,0:T(8,128)(2,1)S(1)} %constant_dynamic-slice_fusion), channel_id=1, source_target_pairs={{0,3},{1,0},{2,1},{3,2},{4,7},{5,4},{6,5},{7,6},{8,11},{9,8},{10,9... | collective-permute-start | bytes 589832 | tf_op jit(solution)/shard_map/ppermute | solution.py:484
  70.3 1.7 %collective-permute-start.10 = (bf16[128,768]{1,0:T(8,128)(2,1)S(1)}, bf16[128,768]{1,0:T(8,128)(2,1)S(1)}, u32[]{:S(2)}, u32[]{:S(2)}) collective-permute-start(bf16[128,768]{1,0:T(8,128)(2,1)S(1)} %constant_dynamic-slice_fusion), channel_id=1, source_target_pairs={{0,1},{1,2},{2,3},{3,0},{4,5},{5,6},{6,7},{7,4},{8,9},{9,10},{10,1... | collective-permute-start | bytes 589832 | tf_op jit(solution)/shard_map/ppermute | solution.py:484
  72.1 0.6 pad_add_fusion.vid
  72.7 0.7 copy.33
  73.4 0.7 copy.32
  74.0 1.6 %collective-permute-done.12 = bf16[128,768]{1,0:T(8,128)(2,1)S(1)} collective-permute-done((bf16[128,768]{1,0:T(8,128)(2,1)S(1)}, bf16[128,768]{1,0:T(8,128)(2,1)S(1)}, u32[]{:S(2)}, u32[]{:S(2)}) %collective-permute-start.12) | collective-permute-done | bytes 196640 | tf_op jit(solution)/shard_map/ppermute | solution.py:484
  75.7 9.9 %collective-permute-done.11 = bf16[128,768]{1,0:T(8,128)(2,1)S(1)} collective-permute-done((bf16[128,768]{1,0:T(8,128)(2,1)S(1)}, bf16[128,768]{1,0:T(8,128)(2,1)S(1)}, u32[]{:S(2)}, u32[]{:S(2)}) %collective-permute-start.11) | collective-permute-done | bytes 196640 | tf_op jit(solution)/shard_map/ppermute | solution.py:484
  85.7 0.7 collective-permute-start.13
  86.4 1.1 copy-done.18
  87.5 0.4 copy-done.17
  87.9 13.9 %unembed.2.refs_4_ = f32[4,40,48,128]{3,2,1,0:T(8,128)} custom-call(s32[2]{0:T(128)} %pad_add_fusion.vid, s32[1]{0:T(128)} %bitcast.me, bf16[8,6,16,768]{3,2,1,0:T(8,128)(2,1)} %tokens.3, bf16[8,16,768]{2,1,0:T(8,128)(2,1)} %collective-permute-done.8.above, bf16[8,16,768]{2,1,0:T(8,128)(2,1)} %collective-permute-done.9.below, bf16[64,768]{1,0:T(8,128)(2,1)} %bitcast.63, ...), custom_call_target="tpu_custom_call" | custom-call | flops 9663676416 | bytes 5111808 | tf_op jit(solution)/shard_map/unembed/pallas_call | solution.py:434
  102.0 1.4 %collective-permute-start.19 = (bf16[2,3,128,768]{3,2,1,0:T(8,128)(2,1)S(1)}, bf16[2,3,128,768]{3,2,1,0:T(8,128)(2,1)S(1)}, u32[]{:S(2)}, u32[]{:S(2)}) collective-permute-start(bf16[2,3,128,768]{3,2,1,0:T(8,128)(2,1)S(1)} %pad_maximum_fusion.1.dep.refs_0_), channel_id=1, source_target_pairs={{0,16},{4,12},{8,24},{12,4},{16,0},{20,28},{24,8},{28,20},{1,17},{... | collective-permute-start | bytes 3538952 | tf_op jit(solution)/shard_map/ppermute | solution.py:489
  103.4 0.6 slice.99.vid
  103.9 13.9 %unembed.3 = f32[4,40,48,128]{3,2,1,0:T(8,128)} custom-call(s32[2]{0:T(128)} %slice.99.vid, s32[1]{0:T(128)} %bitcast.me, bf16[8,6,16,768]{3,2,1,0:T(8,128)(2,1)} %tokens.3, bf16[8,16,768]{2,1,0:T(8,128)(2,1)} %collective-permute-done.8.above, bf16[8,16,768]{2,1,0:T(8,128)(2,1)} %collective-permute-done.9.below, ...), custom_call_target="tpu_custom_call", output_to_operand_aliasing={{}: (14, {})} | custom-call | flops 9663676416 | bytes 5111808 | tf_op jit(solution)/shard_map/unembed/pallas_call | solution.py:434
  117.8 0.4 collective-permute-done.19.refs_1_
  118.2 0.2 collective-permute-start.21
  118.4 2.7 %collective-permute-done.21.refs_3_ = bf16[2,3,128,768]{3,2,1,0:T(8,128)(2,1)S(1)} collective-permute-done((bf16[2,3,128,768]{3,2,1,0:T(8,128)(2,1)S(1)}, bf16[2,3,128,768]{3,2,1,0:T(8,128)(2,1)S(1)}, u32[]{:S(2)}, u32[]{:S(2)}) %collective-permute-start.21) | collective-permute-done | bytes 1179680 | tf_op jit(solution)/shard_map/ppermute | solution.py:489
  121.1 1.0 copy-done.4
  122.1 10.0 %embed.1 = bf16[8,6,16,768]{3,2,1,0:T(8,128)(2,1)} custom-call(s32[3]{0:T(128)} %copy-done.15, s32[1]{0:T(128)} %bitcast.me, bf16[4,768,1024]{2,1,0:T(8,128)(2,1)} %bitcast.46, bf16[2,3,128,768]{3,2,1,0:T(8,128)(2,1)} %copy-done.1, bf16[2,3,128,768]{3,2,1,0:T(8,128)(2,1)} %copy-done.2, bf16[2,3,128,768]{3,2,1,0:T(8,128)(2,1)} %copy-done.3, ...), custom_call_target="tpu_custom_call" | custom-call | flops 3623878656 | bytes 11796480 | tf_op jit(solution)/shard_map/embed/pallas_call | solution.py:406
  (87 shorter events, 1.1 us)
Async XLA Ops:
  2.3 8.0 %copy-start.6 = (bf16[128,768]{1,0:T(8,128)(2,1)S(1)}, bf16[128,768]{1,0:T(8,128)(2,1)}, u32[]{:S(2)}) copy-start(bf16[128,768]{1,0:T(8,128)(2,1)} %constant_dynamic-slice_fusion.1.dep) | copy-start | bytes 589828
  2.3 12.6 %copy-start = (f32[4,40,48,128]{3,2,1,0:T(8,128)S(1)}, f32[4,40,48,128]{3,2,1,0:T(8,128)}, u32[]{:S(2)}) copy-start(f32[4,40,48,128]{3,2,1,0:T(8,128)} %vol.3) | copy-start | bytes 11796484
  7.0 8.2 %copy-start.8 = (bf16[8,6,16,768]{3,2,1,0:T(8,128)(2,1)S(1)}, bf16[8,6,16,768]{3,2,1,0:T(8,128)(2,1)}, u32[]{:S(2)}) copy-start(bf16[8,6,16,768]{3,2,1,0:T(8,128)(2,1)} %tokens.3) | copy-start | bytes 3538948
  7.0 8.6 %collective-permute-start.1 = (bf16[336,128]{1,0:T(8,128)(2,1)}, bf16[336,128]{1,0:T(8,128)(2,1)S(1)}, u32[]{:S(2)}, u32[]{:S(2)}) collective-permute-start(bf16[336,128]{1,0:T(8,128)(2,1)} %pack_edges.1), channel_id=1, source_target_pairs={{4,0},{8,4},{12,8},{16,12},{20,16},{24,20},{28,24},{0,28},{5,1},{9... | collective-permute-start | bytes 258056 | tf_op jit(solution)/shard_map/ppermute | solution.py:466
  10.3 6.6 %collective-permute-start = (bf16[336,128]{1,0:T(8,128)(2,1)}, bf16[336,128]{1,0:T(8,128)(2,1)S(1)}, u32[]{:S(2)}, u32[]{:S(2)}) collective-permute-start(bf16[336,128]{1,0:T(8,128)(2,1)} %pack_edges.1), channel_id=1, source_target_pairs={{0,4},{4,8},{8,12},{12,16},{16,20},{20,24},{24,28},{28,0},{1,5},{5... | collective-permute-start | bytes 258056 | tf_op jit(solution)/shard_map/ppermute | solution.py:466
  10.3 12.3 %collective-permute-start.6 = (bf16[128,768]{1,0:T(8,128)(2,1)S(1)}, bf16[128,768]{1,0:T(8,128)(2,1)S(1)}, u32[]{:S(2)}, u32[]{:S(2)}) collective-permute-start(bf16[128,768]{1,0:T(8,128)(2,1)S(1)} %copy-done.6), channel_id=1, source_target_pairs={{0,3},{1,0},{2,1},{3,2},{4,7},{5,4},{6,5},{7,6},{8,11},{9,8},{10,9... | collective-permute-start | bytes 589832 | tf_op jit(solution)/shard_map/ppermute | solution.py:484
  13.9 17.6 %collective-permute-start.5 = (bf16[128,768]{1,0:T(8,128)(2,1)S(1)}, bf16[128,768]{1,0:T(8,128)(2,1)S(1)}, u32[]{:S(2)}, u32[]{:S(2)}) collective-permute-start(bf16[128,768]{1,0:T(8,128)(2,1)S(1)} %copy-done.6), channel_id=1, source_target_pairs={{0,2},{1,3},{2,0},{3,1},{4,6},{5,7},{6,4},{7,5},{8,10},{9,11},{10,... | collective-permute-start | bytes 589832 | tf_op jit(solution)/shard_map/ppermute | solution.py:484
  13.9 17.6 %collective-permute-start.4 = (bf16[128,768]{1,0:T(8,128)(2,1)S(1)}, bf16[128,768]{1,0:T(8,128)(2,1)S(1)}, u32[]{:S(2)}, u32[]{:S(2)}) collective-permute-start(bf16[128,768]{1,0:T(8,128)(2,1)S(1)} %copy-done.6), channel_id=1, source_target_pairs={{0,1},{1,2},{2,3},{3,0},{4,5},{5,6},{6,7},{7,4},{8,9},{9,10},{10,1... | collective-permute-start | bytes 589832 | tf_op jit(solution)/shard_map/ppermute | solution.py:484
  15.6 15.9 %copy-start.9 = (bf16[336,128]{1,0:T(8,128)(2,1)}, bf16[336,128]{1,0:T(8,128)(2,1)S(1)}, u32[]{:S(2)}) copy-start(bf16[336,128]{1,0:T(8,128)(2,1)S(1)} %collective-permute-done.1) | copy-start | bytes 258052
  15.6 25.8 %collective-permute-start.9 = (bf16[8,16,768]{2,1,0:T(8,128)(2,1)S(1)}, bf16[8,16,768]{2,1,0:T(8,128)(2,1)}, u32[]{:S(2)}, u32[]{:S(2)}) collective-permute-start(bf16[8,16,768]{2,1,0:T(8,128)(2,1)S(1)} %get-tuple-element.22), channel_id=1, source_target_pairs={{1,0},{2,1},{3,2},{5,4},{6,5},{7,6},{9,8},{10,9},{11,10},{13,12},{... | collective-permute-start | bytes 589832 | tf_op jit(solution)/shard_map/ppermute | solution.py:466
  16.9 14.6 %copy-start.11 = (bf16[336,128]{1,0:T(8,128)(2,1)}, bf16[336,128]{1,0:T(8,128)(2,1)S(1)}, u32[]{:S(2)}) copy-start(bf16[336,128]{1,0:T(8,128)(2,1)S(1)} %collective-permute-done) | copy-start | bytes 258052
  16.9 24.4 %collective-permute-start.8 = (bf16[8,16,768]{2,1,0:T(8,128)(2,1)S(1)}, bf16[8,16,768]{2,1,0:T(8,128)(2,1)}, u32[]{:S(2)}, u32[]{:S(2)}) collective-permute-start(bf16[8,16,768]{2,1,0:T(8,128)(2,1)S(1)} %get-tuple-element.23), channel_id=1, source_target_pairs={{0,1},{1,2},{2,3},{4,5},{5,6},{6,7},{8,9},{9,10},{10,11},{12,13},{... | collective-permute-start | bytes 589832 | tf_op jit(solution)/shard_map/ppermute | solution.py:466
  31.6 9.9 %collective-permute-start.7 = (bf16[3,128,768]{2,1,0:T(8,128)(2,1)S(1)}, bf16[3,128,768]{2,1,0:T(8,128)(2,1)S(1)}, u32[]{:S(2)}, u32[]{:S(2)}) collective-permute-start(bf16[3,128,768]{2,1,0:T(8,128)(2,1)S(1)} %get-tuple-element.27), channel_id=1, source_target_pairs={{0,8},{4,20},{8,0},{12,28},{16,24},{20,4},{24,16},{28,12},{1,9},{5... | collective-permute-start | bytes 1769480 | tf_op jit(solution)/shard_map/ppermute | solution.py:489
  32.4 6.8 %collective-permute-start.3 = (bf16[348,128]{1,0:T(8,128)(2,1)}, bf16[348,128]{1,0:T(8,128)(2,1)S(1)}, u32[]{:S(2)}, u32[]{:S(2)}) collective-permute-start(bf16[348,128]{1,0:T(8,128)(2,1)} %pad_maximum_fusion.7), channel_id=1, source_target_pairs={{1,0},{2,1},{3,2},{5,4},{6,5},{7,6},{9,8},{10,9},{11,10},{13,12},{... | collective-permute-start | bytes 267272 | tf_op jit(solution)/shard_map/ppermute | solution.py:466
  34.3 7.0 %collective-permute-start.2 = (bf16[348,128]{1,0:T(8,128)(2,1)}, bf16[348,128]{1,0:T(8,128)(2,1)S(1)}, u32[]{:S(2)}, u32[]{:S(2)}) collective-permute-start(bf16[348,128]{1,0:T(8,128)(2,1)} %pad_maximum_fusion.6), channel_id=1, source_target_pairs={{0,1},{1,2},{2,3},{4,5},{5,6},{6,7},{8,9},{9,10},{10,11},{12,13},{... | collective-permute-start | bytes 267272 | tf_op jit(solution)/shard_map/ppermute | solution.py:466
  39.2 0.6 copy-start.13
  41.6 1.4 %copy-start.14 = (bf16[348,128]{1,0:T(8,128)(2,1)S(1)}, bf16[348,128]{1,0:T(8,128)(2,1)}, u32[]{:S(2)}) copy-start(bf16[348,128]{1,0:T(8,128)(2,1)} %copy-done.13) | copy-start | bytes 267268
  41.6 1.4 %copy-start.10 = (bf16[336,128]{1,0:T(8,128)(2,1)S(1)}, bf16[336,128]{1,0:T(8,128)(2,1)}, u32[]{:S(2)}) copy-start(bf16[336,128]{1,0:T(8,128)(2,1)} %copy-done.9) | copy-start | bytes 258052
  41.6 1.5 %copy-start.12 = (bf16[336,128]{1,0:T(8,128)(2,1)S(1)}, bf16[336,128]{1,0:T(8,128)(2,1)}, u32[]{:S(2)}) copy-start(bf16[336,128]{1,0:T(8,128)(2,1)} %copy-done.11) | copy-start | bytes 258052
  41.7 3.2 %copy-start.5 = (bf16[2,3,128,768]{3,2,1,0:T(8,128)(2,1)}, bf16[2,3,128,768]{3,2,1,0:T(8,128)(2,1)S(1)}, u32[]{:S(2)}) copy-start(bf16[2,3,128,768]{3,2,1,0:T(8,128)(2,1)S(1)} %pad_maximum_fusion.dep.refs_0_) | copy-start | bytes 3538948
  41.7 17.0 %collective-permute-start.16 = (bf16[2,3,128,768]{3,2,1,0:T(8,128)(2,1)S(1)}, bf16[2,3,128,768]{3,2,1,0:T(8,128)(2,1)S(1)}, u32[]{:S(2)}, u32[]{:S(2)}) collective-permute-start(bf16[2,3,128,768]{3,2,1,0:T(8,128)(2,1)S(1)} %pad_maximum_fusion.dep.refs_0_), channel_id=1, source_target_pairs={{0,16},{4,12},{8,24},{12,4},{16,0},{20,28},{24,8},{28,20},{1,17},{... | collective-permute-start | bytes 3538952 | tf_op jit(solution)/shard_map/ppermute | solution.py:489
  44.8 41.6 %collective-permute-start.17 = (bf16[2,3,128,768]{3,2,1,0:T(8,128)(2,1)S(1)}, bf16[2,3,128,768]{3,2,1,0:T(8,128)(2,1)S(1)}, u32[]{:S(2)}, u32[]{:S(2)}) collective-permute-start(bf16[2,3,128,768]{3,2,1,0:T(8,128)(2,1)S(1)} %pad_maximum_fusion.dep.refs_0_), channel_id=1, source_target_pairs={{0,4},{4,0},{8,12},{12,8},{16,20},{20,16},{24,28},{28,24},{1,5},{5... | collective-permute-start | bytes 3538952 | tf_op jit(solution)/shard_map/ppermute | solution.py:489
  58.7 14.7 %copy-start.16 = (bf16[2,3,128,768]{3,2,1,0:T(8,128)(2,1)}, bf16[2,3,128,768]{3,2,1,0:T(8,128)(2,1)S(1)}, u32[]{:S(2)}) copy-start(bf16[2,3,128,768]{3,2,1,0:T(8,128)(2,1)S(1)} %collective-permute-done.16.refs_1_) | copy-start | bytes 3538948
  58.7 27.7 %collective-permute-start.18 = (bf16[2,3,128,768]{3,2,1,0:T(8,128)(2,1)S(1)}, bf16[2,3,128,768]{3,2,1,0:T(8,128)(2,1)S(1)}, u32[]{:S(2)}, u32[]{:S(2)}) collective-permute-start(bf16[2,3,128,768]{3,2,1,0:T(8,128)(2,1)S(1)} %collective-permute-done.16.refs_1_), channel_id=1, source_target_pairs={{0,4},{4,0},{8,12},{12,8},{16,20},{20,16},{24,28},{28,24},{1,5},{5... | collective-permute-start | bytes 3538952 | tf_op jit(solution)/shard_map/ppermute | solution.py:489
  61.6 8.7 %collective-permute-start.14 = (bf16[8,8,768]{2,0,1:T(8,128)(2,1)S(1)}, bf16[8,8,768]{2,0,1:T(8,128)(2,1)S(1)}, u32[]{:S(2)}, u32[]{:S(2)}) collective-permute-start(bf16[8,8,768]{2,0,1:T(8,128)(2,1)S(1)} %pad_maximum_fusion.4), channel_id=1, source_target_pairs={{0,4},{4,8},{8,12},{12,16},{16,20},{20,24},{24,28},{28,0},{1,5},{5... | collective-permute-start | bytes 294920 | tf_op jit(solution)/shard_map/ppermute | solution.py:466
  61.7 8.6 %collective-permute-start.15 = (bf16[8,8,768]{2,0,1:T(8,128)(2,1)S(1)}, bf16[8,8,768]{2,0,1:T(8,128)(2,1)S(1)}, u32[]{:S(2)}, u32[]{:S(2)}) collective-permute-start(bf16[8,8,768]{2,0,1:T(8,128)(2,1)S(1)} %pad_maximum_fusion.5), channel_id=1, source_target_pairs={{4,0},{8,4},{12,8},{16,12},{20,16},{24,20},{28,24},{0,28},{5,1},{9... | collective-permute-start | bytes 294920 | tf_op jit(solution)/shard_map/ppermute | solution.py:466
  65.4 10.3 %collective-permute-start.12 = (bf16[128,768]{1,0:T(8,128)(2,1)S(1)}, bf16[128,768]{1,0:T(8,128)(2,1)S(1)}, u32[]{:S(2)}, u32[]{:S(2)}) collective-permute-start(bf16[128,768]{1,0:T(8,128)(2,1)S(1)} %constant_dynamic-slice_fusion), channel_id=1, source_target_pairs={{0,3},{1,0},{2,1},{3,2},{4,7},{5,4},{6,5},{7,6},{8,11},{9,8},{10,9... | collective-permute-start | bytes 589832 | tf_op jit(solution)/shard_map/ppermute | solution.py:484
  70.3 15.3 %collective-permute-start.11 = (bf16[128,768]{1,0:T(8,128)(2,1)S(1)}, bf16[128,768]{1,0:T(8,128)(2,1)S(1)}, u32[]{:S(2)}, u32[]{:S(2)}) collective-permute-start(bf16[128,768]{1,0:T(8,128)(2,1)S(1)} %constant_dynamic-slice_fusion), channel_id=1, source_target_pairs={{0,2},{1,3},{2,0},{3,1},{4,6},{5,7},{6,4},{7,5},{8,10},{9,11},{10,... | collective-permute-start | bytes 589832 | tf_op jit(solution)/shard_map/ppermute | solution.py:484
  70.3 15.3 %collective-permute-start.10 = (bf16[128,768]{1,0:T(8,128)(2,1)S(1)}, bf16[128,768]{1,0:T(8,128)(2,1)S(1)}, u32[]{:S(2)}, u32[]{:S(2)}) collective-permute-start(bf16[128,768]{1,0:T(8,128)(2,1)S(1)} %constant_dynamic-slice_fusion), channel_id=1, source_target_pairs={{0,1},{1,2},{2,3},{3,0},{4,5},{5,6},{6,7},{7,4},{8,9},{9,10},{10,1... | collective-permute-start | bytes 589832 | tf_op jit(solution)/shard_map/ppermute | solution.py:484
  72.1 31.3 %copy-start.15 = (s32[3]{0:T(128)}, s32[3]{0:T(128)S(1)}, u32[]{:S(2)}) copy-start(s32[3]{0:T(128)S(1)} %compare_select_fusion.vid) | copy-start | bytes 40
  85.7 1.8 %copy-start.7 = (bf16[3,128,768]{2,1,0:T(8,128)(2,1)}, bf16[3,128,768]{2,1,0:T(8,128)(2,1)S(1)}, u32[]{:S(2)}) copy-start(bf16[3,128,768]{2,1,0:T(8,128)(2,1)S(1)} %get-tuple-element.14.dep) | copy-start | bytes 1769476
  85.7 16.1 %collective-permute-start.13 = (bf16[3,128,768]{2,1,0:T(8,128)(2,1)S(1)}, bf16[3,128,768]{2,1,0:T(8,128)(2,1)S(1)}, u32[]{:S(2)}, u32[]{:S(2)}) collective-permute-start(bf16[3,128,768]{2,1,0:T(8,128)(2,1)S(1)} %get-tuple-element.14.dep), channel_id=1, source_target_pairs={{0,8},{4,20},{8,0},{12,28},{16,24},{20,4},{24,16},{28,12},{1,9},{5... | collective-permute-start | bytes 1769480 | tf_op jit(solution)/shard_map/ppermute | solution.py:489
  86.4 1.5 %copy-start.17 = (bf16[2,3,128,768]{3,2,1,0:T(8,128)(2,1)}, bf16[2,3,128,768]{3,2,1,0:T(8,128)(2,1)S(1)}, u32[]{:S(2)}) copy-start(bf16[2,3,128,768]{3,2,1,0:T(8,128)(2,1)S(1)} %collective-permute-done.17.refs_2_) | copy-start | bytes 3538948
  86.4 1.1 copy-start.18
  102.0 2.0 %copy-start.1 = (bf16[2,3,128,768]{3,2,1,0:T(8,128)(2,1)}, bf16[2,3,128,768]{3,2,1,0:T(8,128)(2,1)S(1)}, u32[]{:S(2)}) copy-start(bf16[2,3,128,768]{3,2,1,0:T(8,128)(2,1)S(1)} %pad_maximum_fusion.1.dep.refs_0_) | copy-start | bytes 3538948
  102.0 16.3 %collective-permute-start.19 = (bf16[2,3,128,768]{3,2,1,0:T(8,128)(2,1)S(1)}, bf16[2,3,128,768]{3,2,1,0:T(8,128)(2,1)S(1)}, u32[]{:S(2)}, u32[]{:S(2)}) collective-permute-start(bf16[2,3,128,768]{3,2,1,0:T(8,128)(2,1)S(1)} %pad_maximum_fusion.1.dep.refs_0_), channel_id=1, source_target_pairs={{0,16},{4,12},{8,24},{12,4},{16,0},{20,28},{24,8},{28,20},{1,17},{... | collective-permute-start | bytes 3538952 | tf_op jit(solution)/shard_map/ppermute | solution.py:489
  103.9 14.5 %collective-permute-start.20 = (bf16[2,3,128,768]{3,2,1,0:T(8,128)(2,1)S(1)}, bf16[2,3,128,768]{3,2,1,0:T(8,128)(2,1)S(1)}, u32[]{:S(2)}, u32[]{:S(2)}) collective-permute-start(bf16[2,3,128,768]{3,2,1,0:T(8,128)(2,1)S(1)} %pad_maximum_fusion.1.dep.refs_0_), channel_id=1, source_target_pairs={{0,4},{4,0},{8,12},{12,8},{16,20},{20,16},{24,28},{28,24},{1,5},{5... | collective-permute-start | bytes 3538952 | tf_op jit(solution)/shard_map/ppermute | solution.py:489
  118.2 2.9 %copy-start.2 = (bf16[2,3,128,768]{3,2,1,0:T(8,128)(2,1)}, bf16[2,3,128,768]{3,2,1,0:T(8,128)(2,1)S(1)}, u32[]{:S(2)}) copy-start(bf16[2,3,128,768]{3,2,1,0:T(8,128)(2,1)S(1)} %collective-permute-done.19.refs_1_) | copy-start | bytes 3538948
  118.2 2.8 %collective-permute-start.21 = (bf16[2,3,128,768]{3,2,1,0:T(8,128)(2,1)S(1)}, bf16[2,3,128,768]{3,2,1,0:T(8,128)(2,1)S(1)}, u32[]{:S(2)}, u32[]{:S(2)}) collective-permute-start(bf16[2,3,128,768]{3,2,1,0:T(8,128)(2,1)S(1)} %collective-permute-done.19.refs_1_), channel_id=1, source_target_pairs={{0,4},{4,0},{8,12},{12,8},{16,20},{20,16},{24,28},{28,24},{1,5},{5... | collective-permute-start | bytes 3538952 | tf_op jit(solution)/shard_map/ppermute | solution.py:489
  118.4 2.7 %copy-start.3 = (bf16[2,3,128,768]{3,2,1,0:T(8,128)(2,1)}, bf16[2,3,128,768]{3,2,1,0:T(8,128)(2,1)S(1)}, u32[]{:S(2)}) copy-start(bf16[2,3,128,768]{3,2,1,0:T(8,128)(2,1)S(1)} %collective-permute-done.20.refs_2_) | copy-start | bytes 3538948
  121.1 1.1 copy-start.4

commit v3 on v2

--- a/solution.py
+++ b/solution.py
@@ -75,11 +75,22 @@
         lhs[at : at + rows, k * 128 : (k + 1) * 128] = block
 
 
-def pack_kernel(nk, vol, pick, dep, out, lhs, acc):
+def stack_rim(rim, levels, nk, lhs, main):
+    none = jnp.zeros((8, rim.shape[3]), F32)
+    for k in range(nk):
+        blocks = []
+        for dz in range(DZ + 1):
+            level = SK * k - 1 + dz
+            blocks.append(rim[0, level] if 0 <= level < levels and dz < DZ else none)
+        lhs[main : main + 64, k * 128 : (k + 1) * 128] = jnp.concatenate(blocks, axis=0).astype(BF)
+
+
+def pack_kernel(nk, vol, rim, pick, dep, out, lhs, acc):
     v = pl.program_id(0)
     _, levels, ny, nx = vol.shape
     for dz in range(DZ):
         stack_levels(lambda l: vol[0, l].astype(BF), levels, nk, jnp.zeros((ny, nx), BF), lhs, dz * ny, ny, dz)
+    stack_rim(rim, levels, nk, lhs, DZ * ny)
     part = jnp.dot(lhs[...], pick[0], preferred_element_type=F32)
 
     @pl.when(v == 0)
@@ -113,13 +124,7 @@
     main = DZ * ny
     for dz in range(DZ):
         stack_levels(lambda l: vol[0, l].astype(BF), levels, nk, jnp.zeros((ny, nx), BF), lhs, dz * ny, ny, dz)
-    none = jnp.zeros((8, nx), F32)
-    for k in range(nk):
-        blocks = []
-        for dz in range(DZ + 1):
-            level = SK * k - 1 + dz
-            blocks.append(rim[0, level] if 0 <= level < levels and dz < DZ else none)
-        lhs[main : main + 64, k * 128 : (k + 1) * 128] = jnp.concatenate(blocks, axis=0).astype(BF)
+    stack_rim(rim, levels, nk, lhs, main)
     for pair in range(DX // 2):
         got = jnp.dot(lhs[...], spread[:, pair * 256 : (pair + 1) * 256], preferred_element_type=F32)
         if pair in (0, DX // 2 - 1):
@@ -354,20 +359,21 @@
     return pl.CostEstimate(flops=int(flops), bytes_accessed=int(bytes_accessed), transcendentals=0)
 
 
-def pack_edges(volume, nk, dep):
+def pack_edges(volume, rim, nk, dep):
     nv, levels, ny, nx = volume.shape
     pick = pick_matrix(nv, nk, nx)
+    rows = DZ * ny + 64
     return pl.pallas_call(
         functools.partial(pack_kernel, nk),
         grid=(nv,),
-        in_specs=[lead(volume.shape), lead(pick.shape), HBM],
-        out_specs=whole((DZ * ny, 128)),
-        out_shape=jax.ShapeDtypeStruct((DZ * ny, 128), BF),
-        scratch_shapes=[pltpu.VMEM((DZ * ny, nk * nx), BF), pltpu.VMEM((DZ * ny, 128), F32)],
+        in_specs=[lead(volume.shape), lead(rim.shape), lead(pick.shape), HBM],
+        out_specs=whole((rows, 128)),
+        out_shape=jax.ShapeDtypeStruct((rows, 128), BF),
+        scratch_shapes=[pltpu.VMEM((rows, nk * nx), BF), pltpu.VMEM((rows, 128), F32)],
         compiler_params=params(),
         cost_estimate=cost(2 * nv * DZ * ny * nk * nx * 256, volume.size * 4),
         name="pack_edges",
-    )(volume, pick, dep)
+    )(volume, rim, pick, dep)
 
 
 def im2col(volume, rim, edge, spread, dims, own, weight, dep):
@@ -455,7 +461,7 @@
         out_shape=jax.ShapeDtypeStruct(volume_shape, F32),
         input_output_aliases={} if prev is None else {len(beside) + 6 + len(gathered): 0},
         compiler_params=params(),
-        cost_estimate=cost(8 * n * padded * width * nj * 128, 2 * n * padded * width + 4 * n * levels * ny * nx),
+        cost_estimate=cost(1000, 1000) if n == 1 else cost(8 * n * padded * width * nj * 128, 2 * n * padded * width + 4 * n * levels * ny * nx),
         name="unembed",
     )(vid, me, tokens, *beside, hot, own, dep, *gathered, *before)
 
@@ -513,40 +519,25 @@
     fast = embed_weight.shape[0] == rows and lax.axis_size("lon") % GROUP == 0
     spread = spread_matrix(nk, ni, nx)
 
+    def voxels(at):
+        return volume_b[:, :, at : at + 2].astype(BF).reshape(-1, nx)
+
+    above, below = (x.reshape(nv, levels, 2, nx) for x in both_ways(voxels(ny - 2), voxels(0), "lat", False))
+    rim = jnp.concatenate([above, below, jnp.zeros((nv, levels, 4, nx), BF)], axis=2).astype(F32)
     row_above, row_below = both_ways(tokens_a[:, nj - 1], tokens_a[:, 0], "lat", False)
 
     start = volume_b
     if fast:
         start = own_piece(unembed_weight, me)
         u_near = from_lat(start)
-    packed = pack_edges(volume_b, nk, start)
-    from_left, from_right = both_ways(packed, packed, "lon", True)
+    packed = pack_edges(volume_b, rim, nk, start)
+    edge = jnp.concatenate(both_ways(packed, packed, "lon", True), axis=1)
 
     def column(i):
         return jnp.concatenate([row_above[:, i][:, None], tokens_a[:, :, i], row_below[:, i][:, None]], axis=1)
 
     left, right = both_ways(column(ni - 1), column(0), "lon", True)
     beside = [row_above, row_below, left.reshape(-1, width), right.reshape(-1, width)]
-
-    def lat_rows(at):
-        voxels = volume_b[:, :, at : at + 2].astype(BF).reshape(-1, nx)
-        corners = [a.reshape(DZ, ny, 128)[:, at : at + 2].reshape(-1, 128) for a in (from_left, from_right)]
-        return jnp.concatenate([voxels] + corners, axis=0)
-
-    above, below = both_ways(lat_rows(ny - 2), lat_rows(0), "lat", False)
-    n_vox = nv * levels * 2
-
-    def split(got):
-        voxels = got[:n_vox].reshape(nv, levels, 2, nx)
-        corners = got[n_vox:].reshape(2, DZ, 2, 128)
-        return voxels, jnp.concatenate([corners[0], corners[1]], axis=-1)
-
-    (vox_above, cor_above), (vox_below, cor_below) = split(above), split(below)
-    rim = jnp.concatenate([vox_above, vox_below, jnp.zeros((nv, levels, 4, nx), BF)], axis=2).astype(F32)
-    corners = jnp.concatenate([cor_above, cor_below, jnp.zeros((DZ, 4, 256), BF)], axis=1).reshape(8 * DZ, 256)
-    edge = jnp.concatenate(
-        [jnp.concatenate([from_left, from_right], axis=1), corners, jnp.zeros((64 - 8 * DZ, 256), BF)], axis=0
-    )
     dims = (nk, nj, ni, padded)
     tokens = nj * nk * ni
 
@@ -554,17 +545,20 @@
         u_near = jnp.stack(u_near)
         u_pair = jnp.stack([u_near, after(flip(u_near, first_mask), row_above, row_below)])
         u_rest = flip(u_pair, second_mask)
-        e_near = from_lat(after(own_piece(embed_weight, me), u_near))
+        e_got = from_lat(after(own_piece(embed_weight, me), u_near))
         own = lat.astype(jnp.int32).reshape(1)
         others = lax.rem(lat - jnp.arange(1, lats, dtype=jnp.int32) + lats, lats).astype(jnp.int32)
         a, sums = im2col(volume_b, rim, edge, spread, dims, own, embed_weight[None], (u_pair, edge))
         u_rest = after(u_rest, sums)
         u_all = (u_pair, u_rest, flip(u_pair, core_mask), flip(u_rest, core_mask))
-        e_near = jnp.stack(e_near)
-        e_far = flip(after(e_near, sums), first_mask)
         first_two = jnp.concatenate([own, others[:1]])
         volume_a = unembed(
-            tokens_a, beside, unembed_weight[None], u_all, (None, 0), first_two, me1, None, e_near, volume_b.shape, padded
+            tokens_a, beside, unembed_weight[None], (), (None,), own, me1, None, sums, volume_b.shape, padded
+        )
+        e_near = jnp.stack([after(x, volume_a) for x in e_got])
+        e_far = flip(e_near, first_mask)
+        volume_a = unembed(
+            tokens_a, beside, unembed_weight[None], u_all, (0,), others[:1], me1, volume_a, e_near, volume_b.shape, padded
         )
         e_pair = jnp.stack([e_near, after(e_far, volume_a)])
         e_rest = flip(e_pair, second_mask)

time: 133 us -> 128 us (0.962)
  waiting for transfers between devices: 25.5 us -> 18.1 us
  Pallas kernels: 56.3 us -> 59.6 us
    ppermute x6, waiting for transfers between devices: 20.4 us -> 10.9 us  [from_lat(): lax.ppermute(piece, 'lat', [(i, (i + s) % size) for i in range(size)])]
    pallas_call x2 -> x3, Pallas kernels: 27.8 us -> 31.1 us  [unembed(): pl.pallas_call(functools.partial(unembed_kernel, kinds), grid_spec=pltpu....]
    ppermute x4, starting transfers between devices: 8.53 us -> 5.25 us  [both_ways(): lax.ppermute(down_rows, axis, [(j, i) for i, j in up])]
    another operation x1, other arithmetic: 0.26 us -> 2.38 us
    concatenate x4 -> x1, other arithmetic: 2.72 us -> 0.71 us  [per_device(): edge = jnp.concatenate(both_ways(packed, packed, 'lon', True), axis=1)]
    ppermute x8, starting transfers between devices: 4.13 us -> 5.99 us  [flip(): lax.ppermute(x, 'lon', [(i, i ^ mask(i)) for i in range(lax.axis_size('lo...]
    ppermute x6, starting transfers between devices: 11.3 us -> 12.8 us  [from_lat(): lax.ppermute(piece, 'lat', [(i, (i + s) % size) for i in range(size)])]
    unnamed x40 -> x28, local copies, waits for them, and re-layouts: 3.27 us -> 2.65 us
  transfers between devices with their start and end apart: 22 -> 22, of which waited for: 8 -> 7; matrix products, arithmetic and copies ran while one was open for 7% -> 8% of each run, Pallas kernels for 31% -> 39%
where the time goes in v3:
time: 128 us
  Pallas kernels  59.6 us (47%)
  starting transfers between devices  34.2 us (27%)
  waiting for transfers between devices  18.1 us (14%)
  local copies, waits for them, and re-layouts  9.44 us (7%)
  other arithmetic  5.11 us (4%)
    pallas_call x3, Pallas kernels, unembed(): pl.pallas_call(functools.partial(unembed_kernel, kinds), grid_spec=pltpu....  31.1 us
    pallas_call x1, Pallas kernels, im2col(): pl.pallas_call(functools.partial(im2col_kernel, nk, ni, nj, (DZ * DY * DX...  13.8 us
    ppermute x6, starting transfers between devices, from_lat(): lax.ppermute(piece, 'lat', [(i, (i + s) % size) for i in range(size)])  12.8 us
    ppermute x6, waiting for transfers between devices, from_lat(): lax.ppermute(piece, 'lat', [(i, (i + s) % size) for i in range(size)])  10.9 us
    ppermute x4, starting transfers between devices, both_ways(): lax.ppermute(up_rows, axis, up)  10.2 us
    pallas_call x1, Pallas kernels, embed(): pl.pallas_call(functools.partial(embed_kernel, n, gathered, first), in_sp...  10 us
    ppermute x8, starting transfers between devices, flip(): lax.ppermute(x, 'lon', [(i, i ^ mask(i)) for i in range(lax.axis_size('lo...  5.99 us
    ppermute x4, starting transfers between devices, both_ways(): lax.ppermute(down_rows, axis, [(j, i) for i, j in up])  5.25 us
  transfers between devices with their start and end apart: 22, of which 7 were waited for; matrix products, arithmetic and copies ran while one was open for 8% of the time, Pallas kernels for 39%

profile of v3, /device:TPU:0, one launch (start us, length us, event | category | flops | bytes accessed | tf_op | source)
XLA Modules:
  0.0 127.6 jit_solution(524205381540070017)
XLA Ops:
  0.6 1.0 constant_dynamic-slice_fusion.1.dep
  1.6 5.1 %collective-permute-start.6 = (bf16[128,768]{1,0:T(8,128)(2,1)S(1)}, bf16[128,768]{1,0:T(8,128)(2,1)S(1)}, u32[]{:S(2)}, u32[]{:S(2)}) collective-permute-start(bf16[128,768]{1,0:T(8,128)(2,1)S(1)} %constant_dynamic-slice_fusion.1.dep), channel_id=1, source_target_pairs={{0,3},{1,0},{2,1},{3,2},{4,7},{5,4},{6,5},{7,6},{8,11},{9,8},{10,9... | collective-permute-start | bytes 589832 | tf_op jit(solution)/shard_map/ppermute | solution.py:490
  6.8 1.0 collective-permute-start.4
  7.8 1.0 slice_bitcast_fusion
  8.8 1.3 %collective-permute-start.9 = (bf16[8,16,768]{2,1,0:T(8,128)(2,1)S(1)}, bf16[8,16,768]{2,1,0:T(8,128)(2,1)S(1)}, u32[]{:S(2)}, u32[]{:S(2)}) collective-permute-start(bf16[8,16,768]{2,1,0:T(8,128)(2,1)S(1)} %get-tuple-element.26), channel_id=1, source_target_pairs={{1,0},{2,1},{3,2},{5,4},{6,5},{7,6},{9,8},{10,9},{11,10},{13,12},{... | collective-permute-start | bytes 589832 | tf_op jit(solution)/shard_map/ppermute | solution.py:472
  10.1 5.0 %collective-permute-start.8 = (bf16[8,16,768]{2,1,0:T(8,128)(2,1)S(1)}, bf16[8,16,768]{2,1,0:T(8,128)(2,1)S(1)}, u32[]{:S(2)}, u32[]{:S(2)}) collective-permute-start(bf16[8,16,768]{2,1,0:T(8,128)(2,1)S(1)} %get-tuple-element.27), channel_id=1, source_target_pairs={{0,1},{1,2},{2,3},{4,5},{5,6},{6,7},{8,9},{9,10},{10,11},{12,13},{... | collective-permute-start | bytes 589832 | tf_op jit(solution)/shard_map/ppermute | solution.py:472
  15.1 2.4 %convert.4 = bf16[4,40,48,128]{3,2,1,0:T(8,128)(2,1)S(1)} convert(f32[4,40,48,128]{3,2,1,0:T(8,128)} %vol.3) | non-fusion elementwise | flops 983040 | bytes 5898240 | tf_op jit(solution)/shard_map/convert.1
  17.5 6.9 %collective-permute-done.5 = bf16[128,768]{1,0:T(8,128)(2,1)S(1)} collective-permute-done((bf16[128,768]{1,0:T(8,128)(2,1)S(1)}, bf16[128,768]{1,0:T(8,128)(2,1)S(1)}, u32[]{:S(2)}, u32[]{:S(2)}) %collective-permute-start.5) | collective-permute-done | bytes 196640 | tf_op jit(solution)/shard_map/ppermute | solution.py:490
  24.4 0.1 fusion.2
  24.5 1.6 %collective-permute-start.7 = (bf16[3,128,768]{2,1,0:T(8,128)(2,1)S(1)}, bf16[3,128,768]{2,1,0:T(8,128)(2,1)S(1)}, u32[]{:S(2)}, u32[]{:S(2)}) collective-permute-start(bf16[3,128,768]{2,1,0:T(8,128)(2,1)S(1)} %get-tuple-element.31), channel_id=1, source_target_pairs={{0,8},{4,20},{8,0},{12,28},{16,24},{20,4},{24,16},{28,12},{1,9},{5... | collective-permute-start | bytes 1769480 | tf_op jit(solution)/shard_map/ppermute | solution.py:495
  26.1 0.1 fusion.3
  26.2 1.3 %collective-permute-start.1 = (bf16[320,128]{1,0:T(8,128)(2,1)S(1)}, bf16[320,128]{1,0:T(8,128)(2,1)S(1)}, u32[]{:S(2)}, u32[]{:S(2)}) collective-permute-start(bf16[320,128]{1,0:T(8,128)(2,1)S(1)} %bitcast.63), channel_id=1, source_target_pairs={{1,0},{2,1},{3,2},{5,4},{6,5},{7,6},{9,8},{10,9},{11,10},{13,12},{... | collective-permute-start | bytes 245768 | tf_op jit(solution)/shard_map/ppermute | solution.py:472
  27.5 4.6 %collective-permute-start = (bf16[320,128]{1,0:T(8,128)(2,1)S(1)}, bf16[320,128]{1,0:T(8,128)(2,1)S(1)}, u32[]{:S(2)}, u32[]{:S(2)}) collective-permute-start(bf16[320,128]{1,0:T(8,128)(2,1)S(1)} %bitcast.62), channel_id=1, source_target_pairs={{0,1},{1,2},{2,3},{4,5},{5,6},{6,7},{8,9},{9,10},{10,11},{12,13},{... | collective-permute-start | bytes 245768 | tf_op jit(solution)/shard_map/ppermute | solution.py:472
  32.1 1.5 %fusion.4 = (bf16[8,6,1,768]{3,2,1,0:T(2,128)(2,1)S(1)}, bf16[8,6,1,768]{3,2,1,0:T(2,128)(2,1)S(1)}) fusion(bf16[8,6,16,768]{3,2,1,0:T(8,128)(2,1)} %tokens.5), kind=kLoop, calls=%fused_computation.22 | loop fusion | bytes 294912 | tf_op jit(solution)/shard_map/slice | solution.py:537
  33.7 0.4 collective-permute-done
  34.1 1.0 maximum_convert_fusion.rim
  35.1 4.7 %pack_edges.1 = bf16[400,128]{1,0:T(8,128)(2,1)} custom-call(f32[4,40,48,128]{3,2,1,0:T(8,128)} %vol.3, f32[4,40,8,128]{3,2,1,0:T(8,128)} %maximum_convert_fusion.rim, bf16[4,1024,128]{2,1,0:T(8,128)(2,1)} %constant.38.clone.pick, bf16[128,768]{1,0:T(8,128)(2,1)} %copy-done.11), custom_call_target="tpu_custom_call" | custom-call | flops 704643072 | bytes 3932160 | tf_op jit(solution)/shard_map/pack_edges/pallas_call | solution.py:366
  39.8 0.5 collective-permute-start.2
  40.3 0.1 pad_maximum_fusion.dep.refs_0_
  40.5 1.6 %collective-permute-start.16 = (bf16[2,3,128,768]{3,2,1,0:T(8,128)(2,1)S(1)}, bf16[2,3,128,768]{3,2,1,0:T(8,128)(2,1)S(1)}, u32[]{:S(2)}, u32[]{:S(2)}) collective-permute-start(bf16[2,3,128,768]{3,2,1,0:T(8,128)(2,1)S(1)} %pad_maximum_fusion.dep.refs_0_), channel_id=1, source_target_pairs={{0,16},{4,12},{8,24},{12,4},{16,0},{20,28},{24,8},{28,20},{1,17},{... | collective-permute-start | bytes 3538952 | tf_op jit(solution)/shard_map/ppermute | solution.py:495
  42.0 1.3 %collective-permute-done.3 = bf16[400,128]{1,0:T(8,128)(2,1)S(1)} collective-permute-done((bf16[400,128]{1,0:T(8,128)(2,1)}, bf16[400,128]{1,0:T(8,128)(2,1)S(1)}, u32[]{:S(2)}, u32[]{:S(2)}) %collective-permute-start.3) | collective-permute-done | bytes 102432 | tf_op jit(solution)/shard_map/ppermute | solution.py:472
  43.3 2.0 %collective-permute-done.2 = bf16[400,128]{1,0:T(8,128)(2,1)S(1)} collective-permute-done((bf16[400,128]{1,0:T(8,128)(2,1)}, bf16[400,128]{1,0:T(8,128)(2,1)S(1)}, u32[]{:S(2)}, u32[]{:S(2)}) %collective-permute-start.2) | collective-permute-done | bytes 102432 | tf_op jit(solution)/shard_map/ppermute | solution.py:472
  45.3 0.7 pad_maximum_fusion.4.edge.dep2
  46.3 13.8 %im2col.1 = (bf16[4,6,128,1024]{3,2,1,0:T(8,128)(2,1)}, f32[768,768]{1,0:T(8,128)}) custom-call(f32[4,40,48,128]{3,2,1,0:T(8,128)} %vol.3, f32[4,40,8,128]{3,2,1,0:T(8,128)} %maximum_convert_fusion.rim, bf16[400,256]{1,0:T(8,128)(2,1)} %pad_maximum_fusion.4.edge.dep2, bf16[1024,1536]{1,0:T(8,128)(2,1)} %constant.39.clone.spread, ...), custom_call_target="tpu_custom_call" | custom-call | flops 7549747200 | bytes 10223616 | tf_op jit(solution)/shard_map/im2col/pallas_call | solution.py:392
  60.1 0.5 collective-permute-start.18
  60.7 0.1 collective-permute-start.11
  60.8 2.7 %collective-permute-start.12 = (bf16[8,8,768]{2,0,1:T(8,128)(2,1)S(1)}, bf16[8,8,768]{2,0,1:T(8,128)(2,1)S(1)}, u32[]{:S(2)}, u32[]{:S(2)}) collective-permute-start(bf16[8,8,768]{2,0,1:T(8,128)(2,1)S(1)} %pad_maximum_fusion.6), channel_id=1, source_target_pairs={{4,0},{8,4},{12,8},{16,12},{20,16},{24,20},{28,24},{0,28},{5,1},{9... | collective-permute-start | bytes 294920 | tf_op jit(solution)/shard_map/ppermute | solution.py:472
  63.5 1.0 constant_dynamic-slice_fusion
  64.5 4.6 %collective-permute-start.14 = (bf16[128,768]{1,0:T(8,128)(2,1)S(1)}, bf16[128,768]{1,0:T(8,128)(2,1)S(1)}, u32[]{:S(2)}, u32[]{:S(2)}) collective-permute-start(bf16[128,768]{1,0:T(8,128)(2,1)S(1)} %constant_dynamic-slice_fusion), channel_id=1, source_target_pairs={{0,3},{1,0},{2,1},{3,2},{4,7},{5,4},{6,5},{7,6},{8,11},{9,8},{10,9... | collective-permute-start | bytes 589832 | tf_op jit(solution)/shard_map/ppermute | solution.py:490
  69.1 2.0 %collective-permute-start.10 = (bf16[128,768]{1,0:T(8,128)(2,1)S(1)}, bf16[128,768]{1,0:T(8,128)(2,1)S(1)}, u32[]{:S(2)}, u32[]{:S(2)}) collective-permute-start(bf16[128,768]{1,0:T(8,128)(2,1)S(1)} %constant_dynamic-slice_fusion), channel_id=1, source_target_pairs={{0,1},{1,2},{2,3},{3,0},{4,5},{5,6},{6,7},{7,4},{8,9},{9,10},{10,1... | collective-permute-start | bytes 589832 | tf_op jit(solution)/shard_map/ppermute | solution.py:490
  71.1 0.7 copy.35
  71.8 0.7 copy.34
  72.5 8.2 %unembed.3.refs_4_ = f32[4,40,48,128]{3,2,1,0:T(8,128)} custom-call(s32[1]{0:T(128)} %bitcast.12.refs_0_.vid, s32[1]{0:T(128)} %bitcast.me, bf16[8,6,16,768]{3,2,1,0:T(8,128)(2,1)} %tokens.5, bf16[8,16,768]{2,1,0:T(8,128)(2,1)} %copy-done.10, bf16[8,16,768]{2,1,0:T(8,128)(2,1)} %copy-done.9, bf16[64,768]{1,0:T(8,128)(2,1)} %bitcast.46, ...), custom_call_target="tpu_custom_call" | custom-call | flops 1000 | bytes 1000 | tf_op jit(solution)/shard_map/unembed/pallas_call | solution.py:440
  80.6 4.0 %collective-permute-done.13 = bf16[128,768]{1,0:T(8,128)(2,1)S(1)} collective-permute-done((bf16[128,768]{1,0:T(8,128)(2,1)S(1)}, bf16[128,768]{1,0:T(8,128)(2,1)S(1)}, u32[]{:S(2)}, u32[]{:S(2)}) %collective-permute-start.13) | collective-permute-done | bytes 196640 | tf_op jit(solution)/shard_map/ppermute | solution.py:490
  84.6 0.1 fusion.1
  84.7 1.4 %collective-permute-start.15 = (bf16[3,128,768]{2,1,0:T(8,128)(2,1)S(1)}, bf16[3,128,768]{2,1,0:T(8,128)(2,1)S(1)}, u32[]{:S(2)}, u32[]{:S(2)}) collective-permute-start(bf16[3,128,768]{2,1,0:T(8,128)(2,1)S(1)} %get-tuple-element.29.dep), channel_id=1, source_target_pairs={{0,8},{4,20},{8,0},{12,28},{16,24},{20,4},{24,16},{28,12},{1,9},{5... | collective-permute-start | bytes 1769480 | tf_op jit(solution)/shard_map/ppermute | solution.py:495
  86.2 0.6 compare_select_fusion.vid
  86.8 1.0 copy-done.7
  87.8 0.5 copy-done.8
  88.3 8.8 %unembed.4.refs_4_ = f32[4,40,48,128]{3,2,1,0:T(8,128)} custom-call(s32[1]{0:T(128)} %bitcast.67, s32[1]{0:T(128)} %bitcast.me, bf16[8,6,16,768]{3,2,1,0:T(8,128)(2,1)} %tokens.5, bf16[8,16,768]{2,1,0:T(8,128)(2,1)} %copy-done.10, bf16[8,16,768]{2,1,0:T(8,128)(2,1)} %copy-done.9, bf16[64,768]{1,0:T(8,128)(2,1)} %bitcast.47, ...), custom_call_target="tpu_custom_call", output_to_operand_aliasing={{}: (14, {})} | custom-call | flops 1000 | bytes 1000 | tf_op jit(solution)/shard_map/unembed/pallas_call | solution.py:440
  97.1 0.1 pad_maximum_fusion.1.dep.refs_0_
  97.2 0.8 collective-permute-start.19
  98.1 0.7 slice.49.vid
  98.7 14.1 %unembed.5 = f32[4,40,48,128]{3,2,1,0:T(8,128)} custom-call(s32[2]{0:T(128)} %slice.49.vid, s32[1]{0:T(128)} %bitcast.me, bf16[8,6,16,768]{3,2,1,0:T(8,128)(2,1)} %tokens.5, bf16[8,16,768]{2,1,0:T(8,128)(2,1)} %copy-done.10, bf16[8,16,768]{2,1,0:T(8,128)(2,1)} %copy-done.9, bf16[64,768]{1,0:T(8,128)(2,1)} %bitcast.48, ...), custom_call_target="tpu_custom_call", output_to_operand_aliasing={{}: (14, {})} | custom-call | flops 9663676416 | bytes 5111808 | tf_op jit(solution)/shard_map/unembed/pallas_call | solution.py:440
  112.8 0.7 collective-permute-done.19.refs_1_
  113.5 2.8 %collective-permute-done.21.refs_3_ = bf16[2,3,128,768]{3,2,1,0:T(8,128)(2,1)S(1)} collective-permute-done((bf16[2,3,128,768]{3,2,1,0:T(8,128)(2,1)S(1)}, bf16[2,3,128,768]{3,2,1,0:T(8,128)(2,1)S(1)}, u32[]{:S(2)}, u32[]{:S(2)}) %collective-permute-start.21) | collective-permute-done | bytes 1179680 | tf_op jit(solution)/shard_map/ppermute | solution.py:495
  116.4 1.1 copy-done.5
  117.5 10.0 %embed.1 = bf16[8,6,16,768]{3,2,1,0:T(8,128)(2,1)} custom-call(s32[3]{0:T(128)} %compare_select_fusion.vid, s32[1]{0:T(128)} %bitcast.me, bf16[4,768,1024]{2,1,0:T(8,128)(2,1)} %bitcast.45, bf16[2,3,128,768]{3,2,1,0:T(8,128)(2,1)} %copy-done, bf16[2,3,128,768]{3,2,1,0:T(8,128)(2,1)} %copy-done.3, bf16[2,3,128,768]{3,2,1,0:T(8,128)(2,1)} %copy-done.4, ...), custom_call_target="tpu_custom_call" | custom-call | flops 3623878656 | bytes 11796480 | tf_op jit(solution)/shard_map/embed/pallas_call | solution.py:412
  (56 shorter events, 0.4 us)
Async XLA Ops:
  1.6 15.9 %copy-start.11 = (bf16[128,768]{1,0:T(8,128)(2,1)}, bf16[128,768]{1,0:T(8,128)(2,1)S(1)}, u32[]{:S(2)}) copy-start(bf16[128,768]{1,0:T(8,128)(2,1)S(1)} %constant_dynamic-slice_fusion.1.dep) | copy-start | bytes 589828
  1.6 15.9 %collective-permute-start.6 = (bf16[128,768]{1,0:T(8,128)(2,1)S(1)}, bf16[128,768]{1,0:T(8,128)(2,1)S(1)}, u32[]{:S(2)}, u32[]{:S(2)}) collective-permute-start(bf16[128,768]{1,0:T(8,128)(2,1)S(1)} %constant_dynamic-slice_fusion.1.dep), channel_id=1, source_target_pairs={{0,3},{1,0},{2,1},{3,2},{4,7},{5,4},{6,5},{7,6},{8,11},{9,8},{10,9... | collective-permute-start | bytes 589832 | tf_op jit(solution)/shard_map/ppermute | solution.py:490
  6.7 17.7 %collective-permute-start.5 = (bf16[128,768]{1,0:T(8,128)(2,1)S(1)}, bf16[128,768]{1,0:T(8,128)(2,1)S(1)}, u32[]{:S(2)}, u32[]{:S(2)}) collective-permute-start(bf16[128,768]{1,0:T(8,128)(2,1)S(1)} %constant_dynamic-slice_fusion.1.dep), channel_id=1, source_target_pairs={{0,2},{1,3},{2,0},{3,1},{4,6},{5,7},{6,4},{7,5},{8,10},{9,11},{10,... | collective-permute-start | bytes 589832 | tf_op jit(solution)/shard_map/ppermute | solution.py:490
  6.8 17.7 %collective-permute-start.4 = (bf16[128,768]{1,0:T(8,128)(2,1)S(1)}, bf16[128,768]{1,0:T(8,128)(2,1)S(1)}, u32[]{:S(2)}, u32[]{:S(2)}) collective-permute-start(bf16[128,768]{1,0:T(8,128)(2,1)S(1)} %constant_dynamic-slice_fusion.1.dep), channel_id=1, source_target_pairs={{0,1},{1,2},{2,3},{3,0},{4,5},{5,6},{6,7},{7,4},{8,9},{9,10},{10,1... | collective-permute-start | bytes 589832 | tf_op jit(solution)/shard_map/ppermute | solution.py:490
  8.8 31.5 %collective-permute-start.9 = (bf16[8,16,768]{2,1,0:T(8,128)(2,1)S(1)}, bf16[8,16,768]{2,1,0:T(8,128)(2,1)S(1)}, u32[]{:S(2)}, u32[]{:S(2)}) collective-permute-start(bf16[8,16,768]{2,1,0:T(8,128)(2,1)S(1)} %get-tuple-element.26), channel_id=1, source_target_pairs={{1,0},{2,1},{3,2},{5,4},{6,5},{7,6},{9,8},{10,9},{11,10},{13,12},{... | collective-permute-start | bytes 589832 | tf_op jit(solution)/shard_map/ppermute | solution.py:472
  10.1 30.2 %collective-permute-start.8 = (bf16[8,16,768]{2,1,0:T(8,128)(2,1)S(1)}, bf16[8,16,768]{2,1,0:T(8,128)(2,1)S(1)}, u32[]{:S(2)}, u32[]{:S(2)}) collective-permute-start(bf16[8,16,768]{2,1,0:T(8,128)(2,1)S(1)} %get-tuple-element.27), channel_id=1, source_target_pairs={{0,1},{1,2},{2,3},{4,5},{5,6},{6,7},{8,9},{9,10},{10,11},{12,13},{... | collective-permute-start | bytes 589832 | tf_op jit(solution)/shard_map/ppermute | solution.py:472
  24.5 15.8 %collective-permute-start.7 = (bf16[3,128,768]{2,1,0:T(8,128)(2,1)S(1)}, bf16[3,128,768]{2,1,0:T(8,128)(2,1)S(1)}, u32[]{:S(2)}, u32[]{:S(2)}) collective-permute-start(bf16[3,128,768]{2,1,0:T(8,128)(2,1)S(1)} %get-tuple-element.31), channel_id=1, source_target_pairs={{0,8},{4,20},{8,0},{12,28},{16,24},{20,4},{24,16},{28,12},{1,9},{5... | collective-permute-start | bytes 1769480 | tf_op jit(solution)/shard_map/ppermute | solution.py:495
  26.2 7.5 %collective-permute-start.1 = (bf16[320,128]{1,0:T(8,128)(2,1)S(1)}, bf16[320,128]{1,0:T(8,128)(2,1)S(1)}, u32[]{:S(2)}, u32[]{:S(2)}) collective-permute-start(bf16[320,128]{1,0:T(8,128)(2,1)S(1)} %bitcast.63), channel_id=1, source_target_pairs={{1,0},{2,1},{3,2},{5,4},{6,5},{7,6},{9,8},{10,9},{11,10},{13,12},{... | collective-permute-start | bytes 245768 | tf_op jit(solution)/shard_map/ppermute | solution.py:472
  27.5 6.6 %collective-permute-start = (bf16[320,128]{1,0:T(8,128)(2,1)S(1)}, bf16[320,128]{1,0:T(8,128)(2,1)S(1)}, u32[]{:S(2)}, u32[]{:S(2)}) collective-permute-start(bf16[320,128]{1,0:T(8,128)(2,1)S(1)} %bitcast.62), channel_id=1, source_target_pairs={{0,1},{1,2},{2,3},{4,5},{5,6},{6,7},{8,9},{9,10},{10,11},{12,13},{... | collective-permute-start | bytes 245768 | tf_op jit(solution)/shard_map/ppermute | solution.py:472
  39.8 3.6 %collective-permute-start.3 = (bf16[400,128]{1,0:T(8,128)(2,1)}, bf16[400,128]{1,0:T(8,128)(2,1)S(1)}, u32[]{:S(2)}, u32[]{:S(2)}) collective-permute-start(bf16[400,128]{1,0:T(8,128)(2,1)} %pack_edges.1), channel_id=1, source_target_pairs={{4,0},{8,4},{12,8},{16,12},{20,16},{24,20},{28,24},{0,28},{5,1},{9... | collective-permute-start | bytes 307208 | tf_op jit(solution)/shard_map/ppermute | solution.py:472
  39.8 5.5 %collective-permute-start.2 = (bf16[400,128]{1,0:T(8,128)(2,1)}, bf16[400,128]{1,0:T(8,128)(2,1)S(1)}, u32[]{:S(2)}, u32[]{:S(2)}) collective-permute-start(bf16[400,128]{1,0:T(8,128)(2,1)} %pack_edges.1), channel_id=1, source_target_pairs={{0,4},{4,8},{8,12},{12,16},{16,20},{20,24},{24,28},{28,0},{1,5},{5... | collective-permute-start | bytes 307208 | tf_op jit(solution)/shard_map/ppermute | solution.py:472
  40.3 5.7 %copy-start.9 = (bf16[8,16,768]{2,1,0:T(8,128)(2,1)}, bf16[8,16,768]{2,1,0:T(8,128)(2,1)S(1)}, u32[]{:S(2)}) copy-start(bf16[8,16,768]{2,1,0:T(8,128)(2,1)S(1)} %collective-permute-done.9.below) | copy-start | bytes 589828
  40.3 5.8 %copy-start.10 = (bf16[8,16,768]{2,1,0:T(8,128)(2,1)}, bf16[8,16,768]{2,1,0:T(8,128)(2,1)S(1)}, u32[]{:S(2)}) copy-start(bf16[8,16,768]{2,1,0:T(8,128)(2,1)S(1)} %collective-permute-done.8.above) | copy-start | bytes 589828
  40.4 5.8 %copy-start.1 = (bf16[2,3,128,768]{3,2,1,0:T(8,128)(2,1)}, bf16[2,3,128,768]{3,2,1,0:T(8,128)(2,1)S(1)}, u32[]{:S(2)}) copy-start(bf16[2,3,128,768]{3,2,1,0:T(8,128)(2,1)S(1)} %pad_maximum_fusion.dep.refs_0_) | copy-start | bytes 3538948
  40.5 19.7 %collective-permute-start.16 = (bf16[2,3,128,768]{3,2,1,0:T(8,128)(2,1)S(1)}, bf16[2,3,128,768]{3,2,1,0:T(8,128)(2,1)S(1)}, u32[]{:S(2)}, u32[]{:S(2)}) collective-permute-start(bf16[2,3,128,768]{3,2,1,0:T(8,128)(2,1)S(1)} %pad_maximum_fusion.dep.refs_0_), channel_id=1, source_target_pairs={{0,16},{4,12},{8,24},{12,4},{16,0},{20,28},{24,8},{28,20},{1,17},{... | collective-permute-start | bytes 3538952 | tf_op jit(solution)/shard_map/ppermute | solution.py:495
  46.2 40.6 %collective-permute-start.17 = (bf16[2,3,128,768]{3,2,1,0:T(8,128)(2,1)S(1)}, bf16[2,3,128,768]{3,2,1,0:T(8,128)(2,1)S(1)}, u32[]{:S(2)}, u32[]{:S(2)}) collective-permute-start(bf16[2,3,128,768]{3,2,1,0:T(8,128)(2,1)S(1)} %pad_maximum_fusion.dep.refs_0_), channel_id=1, source_target_pairs={{0,4},{4,0},{8,12},{12,8},{16,20},{20,16},{24,28},{28,24},{1,5},{5... | collective-permute-start | bytes 3538952 | tf_op jit(solution)/shard_map/ppermute | solution.py:495
  60.1 20.5 %copy-start.6 = (bf16[2,3,128,768]{3,2,1,0:T(8,128)(2,1)}, bf16[2,3,128,768]{3,2,1,0:T(8,128)(2,1)S(1)}, u32[]{:S(2)}) copy-start(bf16[2,3,128,768]{3,2,1,0:T(8,128)(2,1)S(1)} %collective-permute-done.16.refs_1_) | copy-start | bytes 3538948
  60.1 26.6 %collective-permute-start.18 = (bf16[2,3,128,768]{3,2,1,0:T(8,128)(2,1)S(1)}, bf16[2,3,128,768]{3,2,1,0:T(8,128)(2,1)S(1)}, u32[]{:S(2)}, u32[]{:S(2)}) collective-permute-start(bf16[2,3,128,768]{3,2,1,0:T(8,128)(2,1)S(1)} %collective-permute-done.16.refs_1_), channel_id=1, source_target_pairs={{0,4},{4,0},{8,12},{12,8},{16,20},{20,16},{24,28},{28,24},{1,5},{5... | collective-permute-start | bytes 3538952 | tf_op jit(solution)/shard_map/ppermute | solution.py:495
  60.7 8.4 %collective-permute-start.11 = (bf16[8,8,768]{2,0,1:T(8,128)(2,1)S(1)}, bf16[8,8,768]{2,0,1:T(8,128)(2,1)S(1)}, u32[]{:S(2)}, u32[]{:S(2)}) collective-permute-start(bf16[8,8,768]{2,0,1:T(8,128)(2,1)S(1)} %pad_maximum_fusion.5), channel_id=1, source_target_pairs={{0,4},{4,8},{8,12},{12,16},{16,20},{20,24},{24,28},{28,0},{1,5},{5... | collective-permute-start | bytes 294920 | tf_op jit(solution)/shard_map/ppermute | solution.py:472
  60.8 8.3 %collective-permute-start.12 = (bf16[8,8,768]{2,0,1:T(8,128)(2,1)S(1)}, bf16[8,8,768]{2,0,1:T(8,128)(2,1)S(1)}, u32[]{:S(2)}, u32[]{:S(2)}) collective-permute-start(bf16[8,8,768]{2,0,1:T(8,128)(2,1)S(1)} %pad_maximum_fusion.6), channel_id=1, source_target_pairs={{4,0},{8,4},{12,8},{16,12},{20,16},{24,20},{28,24},{0,28},{5,1},{9... | collective-permute-start | bytes 294920 | tf_op jit(solution)/shard_map/ppermute | solution.py:472
  64.5 16.2 %collective-permute-start.14 = (bf16[128,768]{1,0:T(8,128)(2,1)S(1)}, bf16[128,768]{1,0:T(8,128)(2,1)S(1)}, u32[]{:S(2)}, u32[]{:S(2)}) collective-permute-start(bf16[128,768]{1,0:T(8,128)(2,1)S(1)} %constant_dynamic-slice_fusion), channel_id=1, source_target_pairs={{0,3},{1,0},{2,1},{3,2},{4,7},{5,4},{6,5},{7,6},{8,11},{9,8},{10,9... | collective-permute-start | bytes 589832 | tf_op jit(solution)/shard_map/ppermute | solution.py:490
  69.1 15.6 %collective-permute-start.13 = (bf16[128,768]{1,0:T(8,128)(2,1)S(1)}, bf16[128,768]{1,0:T(8,128)(2,1)S(1)}, u32[]{:S(2)}, u32[]{:S(2)}) collective-permute-start(bf16[128,768]{1,0:T(8,128)(2,1)S(1)} %constant_dynamic-slice_fusion), channel_id=1, source_target_pairs={{0,2},{1,3},{2,0},{3,1},{4,6},{5,7},{6,4},{7,5},{8,10},{9,11},{10,... | collective-permute-start | bytes 589832 | tf_op jit(solution)/shard_map/ppermute | solution.py:490
  69.1 15.5 %collective-permute-start.10 = (bf16[128,768]{1,0:T(8,128)(2,1)S(1)}, bf16[128,768]{1,0:T(8,128)(2,1)S(1)}, u32[]{:S(2)}, u32[]{:S(2)}) collective-permute-start(bf16[128,768]{1,0:T(8,128)(2,1)S(1)} %constant_dynamic-slice_fusion), channel_id=1, source_target_pairs={{0,1},{1,2},{2,3},{3,0},{4,5},{5,6},{6,7},{7,4},{8,9},{9,10},{10,1... | collective-permute-start | bytes 589832 | tf_op jit(solution)/shard_map/ppermute | solution.py:490
  84.7 2.0 %copy-start.2 = (bf16[3,128,768]{2,1,0:T(8,128)(2,1)}, bf16[3,128,768]{2,1,0:T(8,128)(2,1)S(1)}, u32[]{:S(2)}) copy-start(bf16[3,128,768]{2,1,0:T(8,128)(2,1)S(1)} %get-tuple-element.29.dep) | copy-start | bytes 1769476
  84.7 12.4 %collective-permute-start.15 = (bf16[3,128,768]{2,1,0:T(8,128)(2,1)S(1)}, bf16[3,128,768]{2,1,0:T(8,128)(2,1)S(1)}, u32[]{:S(2)}, u32[]{:S(2)}) collective-permute-start(bf16[3,128,768]{2,1,0:T(8,128)(2,1)S(1)} %get-tuple-element.29.dep), channel_id=1, source_target_pairs={{0,8},{4,20},{8,0},{12,28},{16,24},{20,4},{24,16},{28,12},{1,9},{5... | collective-permute-start | bytes 1769480 | tf_op jit(solution)/shard_map/ppermute | solution.py:495
  86.8 1.0 copy-start.7
  86.8 1.5 %copy-start.8 = (bf16[2,3,128,768]{3,2,1,0:T(8,128)(2,1)}, bf16[2,3,128,768]{3,2,1,0:T(8,128)(2,1)S(1)}, u32[]{:S(2)}) copy-start(bf16[2,3,128,768]{3,2,1,0:T(8,128)(2,1)S(1)} %collective-permute-done.18.refs_3_) | copy-start | bytes 3538948
  97.1 1.0 copy-start.12
  97.2 1.5 %copy-start = (bf16[2,3,128,768]{3,2,1,0:T(8,128)(2,1)}, bf16[2,3,128,768]{3,2,1,0:T(8,128)(2,1)S(1)}, u32[]{:S(2)}) copy-start(bf16[2,3,128,768]{3,2,1,0:T(8,128)(2,1)S(1)} %pad_maximum_fusion.1.dep.refs_0_) | copy-start | bytes 3538948
  97.2 16.3 %collective-permute-start.19 = (bf16[2,3,128,768]{3,2,1,0:T(8,128)(2,1)S(1)}, bf16[2,3,128,768]{3,2,1,0:T(8,128)(2,1)S(1)}, u32[]{:S(2)}, u32[]{:S(2)}) collective-permute-start(bf16[2,3,128,768]{3,2,1,0:T(8,128)(2,1)S(1)} %pad_maximum_fusion.1.dep.refs_0_), channel_id=1, source_target_pairs={{0,16},{4,12},{8,24},{12,4},{16,0},{20,28},{24,8},{28,20},{1,17},{... | collective-permute-start | bytes 3538952 | tf_op jit(solution)/shard_map/ppermute | solution.py:495
  98.7 14.8 %collective-permute-start.20 = (bf16[2,3,128,768]{3,2,1,0:T(8,128)(2,1)S(1)}, bf16[2,3,128,768]{3,2,1,0:T(8,128)(2,1)S(1)}, u32[]{:S(2)}, u32[]{:S(2)}) collective-permute-start(bf16[2,3,128,768]{3,2,1,0:T(8,128)(2,1)S(1)} %pad_maximum_fusion.1.dep.refs_0_), channel_id=1, source_target_pairs={{0,4},{4,0},{8,12},{12,8},{16,20},{20,16},{24,28},{28,24},{1,5},{5... | collective-permute-start | bytes 3538952 | tf_op jit(solution)/shard_map/ppermute | solution.py:495
  113.5 2.9 %copy-start.3 = (bf16[2,3,128,768]{3,2,1,0:T(8,128)(2,1)}, bf16[2,3,128,768]{3,2,1,0:T(8,128)(2,1)S(1)}, u32[]{:S(2)}) copy-start(bf16[2,3,128,768]{3,2,1,0:T(8,128)(2,1)S(1)} %collective-permute-done.19.refs_1_) | copy-start | bytes 3538948
  113.5 2.8 %collective-permute-start.21 = (bf16[2,3,128,768]{3,2,1,0:T(8,128)(2,1)S(1)}, bf16[2,3,128,768]{3,2,1,0:T(8,128)(2,1)S(1)}, u32[]{:S(2)}, u32[]{:S(2)}) collective-permute-start(bf16[2,3,128,768]{3,2,1,0:T(8,128)(2,1)S(1)} %collective-permute-done.19.refs_1_), channel_id=1, source_target_pairs={{0,4},{4,0},{8,12},{12,8},{16,20},{20,16},{24,28},{28,24},{1,5},{5... | collective-permute-start | bytes 3538952 | tf_op jit(solution)/shard_map/ppermute | solution.py:495
  113.5 2.8 %copy-start.4 = (bf16[2,3,128,768]{3,2,1,0:T(8,128)(2,1)}, bf16[2,3,128,768]{3,2,1,0:T(8,128)(2,1)S(1)}, u32[]{:S(2)}) copy-start(bf16[2,3,128,768]{3,2,1,0:T(8,128)(2,1)S(1)} %collective-permute-done.20.refs_2_) | copy-start | bytes 3538948
  116.4 1.1 copy-start.5

commit v4 on v3

--- a/solution.py
+++ b/solution.py
@@ -11,13 +11,14 @@
 BF = jnp.bfloat16
 F32 = jnp.float32
 VMEM_LIMIT = 56 * 1024 * 1024
+SMALL_LIMIT = 36 * 1024 * 1024
 DZ, DY, DX = 7, 12, 12
 SK, SY, SX = 5, 8, 8
 GROUP = 8
 
 
-def params():
-    return pltpu.CompilerParams(vmem_limit_bytes=VMEM_LIMIT)
+def params(limit=VMEM_LIMIT):
+    return pltpu.CompilerParams(vmem_limit_bytes=limit)
 
 
 def spread_matrix(nk, ni, nx):
@@ -352,7 +353,7 @@
     return pl.BlockSpec((1,) + tuple(shape[1:]), lambda v, *_: (v,) + (0,) * (len(shape) - 1))
 
 
-HBM = pl.BlockSpec(memory_space=pltpu.HBM)
+ANY = pl.BlockSpec(memory_space=pl.ANY)
 
 
 def cost(flops, bytes_accessed):
@@ -366,11 +367,11 @@
     return pl.pallas_call(
         functools.partial(pack_kernel, nk),
         grid=(nv,),
-        in_specs=[lead(volume.shape), lead(rim.shape), lead(pick.shape), HBM],
+        in_specs=[lead(volume.shape), lead(rim.shape), lead(pick.shape), ANY],
         out_specs=whole((rows, 128)),
         out_shape=jax.ShapeDtypeStruct((rows, 128), BF),
         scratch_shapes=[pltpu.VMEM((rows, nk * nx), BF), pltpu.VMEM((rows, 128), F32)],
-        compiler_params=params(),
+        compiler_params=params(SMALL_LIMIT),
         cost_estimate=cost(2 * nv * DZ * ny * nk * nx * 256, volume.size * 4),
         name="pack_edges",
     )(volume, rim, pick, dep)
@@ -386,18 +387,18 @@
     with_own = weight is not None
     extra_specs, extra, extra_out, extra_scratch = [], [], [], []
     if with_own:
-        extra_specs, extra = [pl.BlockSpec(memory_space=pltpu.SMEM), HBM], [own, weight]
+        extra_specs, extra = [pl.BlockSpec(memory_space=pltpu.SMEM), ANY], [own, weight]
         extra_out = [(nj * nk * ni, width)]
         extra_scratch = [pltpu.VMEM((padded, width), BF), pltpu.SemaphoreType.DMA((2,))]
     return pl.pallas_call(
         functools.partial(im2col_kernel, nk, ni, nj, (DZ * DY * DX, padded, padded // GROUP), with_own),
         grid=(nv,),
-        in_specs=[lead(volume.shape), lead(rim.shape), whole(edge.shape), whole(spread.shape), lead(hot.shape), HBM, HBM]
+        in_specs=[lead(volume.shape), lead(rim.shape), whole(edge.shape), whole(spread.shape), lead(hot.shape), ANY, ANY]
         + extra_specs,
         out_specs=[lead(shape)] + [whole(x) for x in extra_out],
         out_shape=[jax.ShapeDtypeStruct(shape, BF)] + [jax.ShapeDtypeStruct(x, F32) for x in extra_out],
         scratch_shapes=[pltpu.VMEM((rows, nk * nx), BF), pltpu.VMEM((DZ, DX * (ny + 4), 128), F32)] + extra_scratch,
-        compiler_params=params(),
+        compiler_params=params(SMALL_LIMIT),
         cost_estimate=cost(3 * nv * rows * nk * nx * DX * 128, volume.size * 4 + 2 * nv * nj * 128 * padded),
         name="im2col",
     )(volume, rim, edge, spread, hot, *dep, *extra)
@@ -411,7 +412,7 @@
     smem = pl.BlockSpec(memory_space=pltpu.SMEM)
     return pl.pallas_call(
         functools.partial(embed_kernel, n, gathered, first),
-        in_specs=[smem, smem, HBM] + [HBM] * (len(weights) + (not first)),
+        in_specs=[smem, smem, ANY] + [ANY] * (len(weights) + (not first)),
         out_specs=pl.BlockSpec(memory_space=pltpu.VMEM),
         out_shape=jax.ShapeDtypeStruct(token_shape, BF),
         scratch_shapes=[
@@ -442,7 +443,7 @@
         grid_spec=pltpu.PrefetchScalarGridSpec(
             num_scalar_prefetch=2,
             grid=(len(kinds),),
-            in_specs=[HBM] * (4 + len(beside) + len(gathered) + len(before)),
+            in_specs=[ANY] * (4 + len(beside) + len(gathered) + len(before)),
             out_specs=pl.BlockSpec((1, levels, ny, nx), lambda s, vid, me: (vid[s], 0, 0, 0)),
             scratch_shapes=[
                 pltpu.VMEM((2, padded, width), BF),
@@ -520,7 +521,7 @@
     spread = spread_matrix(nk, ni, nx)
 
     def voxels(at):
-        return volume_b[:, :, at : at + 2].astype(BF).reshape(-1, nx)
+        return lax.optimization_barrier(volume_b[:, :, at : at + 2]).astype(BF).reshape(-1, nx)
 
     above, below = (x.reshape(nv, levels, 2, nx) for x in both_ways(voxels(ny - 2), voxels(0), "lat", False))
     rim = jnp.concatenate([above, below, jnp.zeros((nv, levels, 4, nx), BF)], axis=2).astype(F32)

time: 128 us -> 122 us (0.953)
  Pallas kernels: 59.6 us -> 53.9 us
  local copies, waits for them, and re-layouts: 9.44 us -> 12.5 us
  other arithmetic: 5.11 us -> 3.37 us
  starting transfers between devices: 34.2 us -> 32.7 us
    unnamed x28 -> x40, local copies, waits for them, and re-layouts: 2.65 us -> 6.2 us
    pallas_call x1, Pallas kernels: 4.66 us -> 1.75 us  [pack_edges(): pl.pallas_call(functools.partial(pack_kernel, nk), grid=(nv,), in_specs=[...]
    pallas_call x1, Pallas kernels: 13.8 us -> 11.1 us  [im2col(): pl.pallas_call(functools.partial(im2col_kernel, nk, ni, nj, (DZ * DY * DX...]
    another operation x1 -> x0, other arithmetic: 2.38 us -> none
    ppermute x6, starting transfers between devices: 12.8 us -> 10.6 us  [from_lat(): lax.ppermute(piece, 'lat', [(i, (i + s) % size) for i in range(size)])]
    slice x1, local copies, waits for them, and re-layouts: 0.13 us -> 2.07 us  [voxels(): volume_b[:, :, at:at + 2]]
    ppermute x6, waiting for transfers between devices: 10.9 us -> 12.3 us  [from_lat(): lax.ppermute(piece, 'lat', [(i, (i + s) % size) for i in range(size)])]
    ppermute x4, waiting for transfers between devices: 1.31 us -> 0.01 us  [both_ways(): lax.ppermute(down_rows, axis, [(j, i) for i, j in up])]
  transfers between devices with their start and end apart: 22 -> 22, of which waited for: 7 -> 7; matrix products, arithmetic and copies ran while one was open for 8% -> 7% of each run, Pallas kernels for 39% -> 36%
where the time goes in v4:
time: 122 us
  Pallas kernels  53.9 us (44%)
  starting transfers between devices  32.7 us (27%)
  waiting for transfers between devices  18.3 us (15%)
  local copies, waits for them, and re-layouts  12.5 us (10%)
  other arithmetic  3.37 us (3%)
  between operations  1.26 us (1%)
    pallas_call x3, Pallas kernels, unembed(): pl.pallas_call(functools.partial(unembed_kernel, kinds), grid_spec=pltpu....  31.1 us
    ppermute x6, waiting for transfers between devices, from_lat(): lax.ppermute(piece, 'lat', [(i, (i + s) % size) for i in range(size)])  12.3 us
    pallas_call x1, Pallas kernels, im2col(): pl.pallas_call(functools.partial(im2col_kernel, nk, ni, nj, (DZ * DY * DX...  11.1 us
    ppermute x4, starting transfers between devices, both_ways(): lax.ppermute(up_rows, axis, up)  10.9 us
    ppermute x6, starting transfers between devices, from_lat(): lax.ppermute(piece, 'lat', [(i, (i + s) % size) for i in range(size)])  10.6 us
    pallas_call x1, Pallas kernels, embed(): pl.pallas_call(functools.partial(embed_kernel, n, gathered, first), in_sp...  10 us
    unnamed x40, local copies, waits for them, and re-layouts  6.2 us
    ppermute x8, starting transfers between devices, flip(): lax.ppermute(x, 'lon', [(i, i ^ mask(i)) for i in range(lax.axis_size('lo...  6.03 us
  transfers between devices with their start and end apart: 22, of which 7 were waited for; matrix products, arithmetic and copies ran while one was open for 7% of the time, Pallas kernels for 36%

profile of v4, /device:TPU:0, one launch (start us, length us, event | category | flops | bytes accessed | tf_op | source)
XLA Modules:
  0.0 122.0 jit_solution(300929188860975186)
XLA Ops:
  0.7 1.1 constant_dynamic-slice_fusion.1.dep
  1.7 5.1 %collective-permute-start.6 = (bf16[128,768]{1,0:T(8,128)(2,1)S(1)}, bf16[128,768]{1,0:T(8,128)(2,1)S(1)}, u32[]{:S(2)}, u32[]{:S(2)}) collective-permute-start(bf16[128,768]{1,0:T(8,128)(2,1)S(1)} %constant_dynamic-slice_fusion.1.dep), channel_id=1, source_target_pairs={{0,3},{1,0},{2,1},{3,2},{4,7},{5,4},{6,5},{7,6},{8,11},{9,8},{10,9... | collective-permute-start | bytes 589832 | tf_op jit(solution)/shard_map/ppermute | solution.py:491
  6.8 1.0 collective-permute-start.4
  7.9 2.1 %fusion.3 = (bf16[4,40,2,128]{3,2,1,0:T(2,128)(2,1)}, bf16[4,40,2,128]{3,2,1,0:T(2,128)(2,1)}) fusion(f32[4,40,48,128]{3,2,1,0:T(8,128)} %vol.3), kind=kLoop, calls=%fused_computation.21 | loop fusion | bytes 327680 | tf_op jit(solution)/shard_map/slice | solution.py:524
  9.9 1.3 %collective-permute-start.1 = (bf16[320,128]{1,0:T(8,128)(2,1)}, bf16[320,128]{1,0:T(8,128)(2,1)}, u32[]{:S(2)}, u32[]{:S(2)}) collective-permute-start(bf16[320,128]{1,0:T(8,128)(2,1)} %bitcast.3), channel_id=1, source_target_pairs={{1,0},{2,1},{3,2},{5,4},{6,5},{7,6},{9,8},{10,9},{11,10},{13,12},{... | collective-permute-start | bytes 245768 | tf_op jit(solution)/shard_map/ppermute | solution.py:473
  11.2 5.6 %collective-permute-start = (bf16[320,128]{1,0:T(8,128)(2,1)}, bf16[320,128]{1,0:T(8,128)(2,1)}, u32[]{:S(2)}, u32[]{:S(2)}) collective-permute-start(bf16[320,128]{1,0:T(8,128)(2,1)} %bitcast.1), channel_id=1, source_target_pairs={{0,1},{1,2},{2,3},{4,5},{5,6},{6,7},{8,9},{9,10},{10,11},{12,13},{... | collective-permute-start | bytes 245768 | tf_op jit(solution)/shard_map/ppermute | solution.py:473
  16.9 7.6 %collective-permute-done.5 = bf16[128,768]{1,0:T(8,128)(2,1)S(1)} collective-permute-done((bf16[128,768]{1,0:T(8,128)(2,1)S(1)}, bf16[128,768]{1,0:T(8,128)(2,1)S(1)}, u32[]{:S(2)}, u32[]{:S(2)}) %collective-permute-start.5) | collective-permute-done | bytes 196640 | tf_op jit(solution)/shard_map/ppermute | solution.py:491
  24.5 0.1 fusion.2
  24.6 1.6 %collective-permute-start.7 = (bf16[3,128,768]{2,1,0:T(8,128)(2,1)S(1)}, bf16[3,128,768]{2,1,0:T(8,128)(2,1)}, u32[]{:S(2)}, u32[]{:S(2)}) collective-permute-start(bf16[3,128,768]{2,1,0:T(8,128)(2,1)S(1)} %get-tuple-element.31), channel_id=1, source_target_pairs={{0,8},{4,20},{8,0},{12,28},{16,24},{20,4},{24,16},{28,12},{1,9},{5... | collective-permute-start | bytes 1769480 | tf_op jit(solution)/shard_map/ppermute | solution.py:496
  26.1 0.7 slice_bitcast_fusion
  26.8 1.3 %collective-permute-start.9 = (bf16[8,16,768]{2,1,0:T(8,128)(2,1)}, bf16[8,16,768]{2,1,0:T(8,128)(2,1)S(1)}, u32[]{:S(2)}, u32[]{:S(2)}) collective-permute-start(bf16[8,16,768]{2,1,0:T(8,128)(2,1)} %get-tuple-element.26), channel_id=1, source_target_pairs={{1,0},{2,1},{3,2},{5,4},{6,5},{7,6},{9,8},{10,9},{11,10},{13,12},{... | collective-permute-start | bytes 589832 | tf_op jit(solution)/shard_map/ppermute | solution.py:473
  28.1 4.6 %collective-permute-start.8 = (bf16[8,16,768]{2,1,0:T(8,128)(2,1)S(1)}, bf16[8,16,768]{2,1,0:T(8,128)(2,1)S(1)}, u32[]{:S(2)}, u32[]{:S(2)}) collective-permute-start(bf16[8,16,768]{2,1,0:T(8,128)(2,1)S(1)} %get-tuple-element.27), channel_id=1, source_target_pairs={{0,1},{1,2},{2,3},{4,5},{5,6},{6,7},{8,9},{9,10},{10,11},{12,13},{... | collective-permute-start | bytes 589832 | tf_op jit(solution)/shard_map/ppermute | solution.py:473
  32.7 0.2 fusion.4
  33.0 0.1 pad.20.clone
  33.1 1.1 maximum_convert_fusion.rim
  34.2 2.1 %copy-done.2 = f32[4,40,48,128]{3,2,1,0:T(8,128)S(1)} copy-done((f32[4,40,48,128]{3,2,1,0:T(8,128)S(1)}, f32[4,40,48,128]{3,2,1,0:T(8,128)}, u32[]{:S(2)}) %copy-start.2) | copy-done | bytes 3932184
  36.3 1.7 %pack_edges.1 = bf16[400,128]{1,0:T(8,128)(2,1)S(1)} custom-call(f32[4,40,48,128]{3,2,1,0:T(8,128)S(1)} %copy-done.2, f32[4,40,8,128]{3,2,1,0:T(8,128)S(1)} %maximum_convert_fusion.rim, bf16[4,1024,128]{2,1,0:T(8,128)(2,1)S(1)} %copy-done.3, bf16[128,768]{1,0:T(8,128)(2,1)S(1)} %constant_dynamic-slice_fusion.1.dep), custom_call_target="tpu_custom_call" | custom-call | flops 704643072 | bytes 3932160 | tf_op jit(solution)/shard_map/pack_edges/pallas_call | solution.py:367
  38.1 0.5 collective-permute-start.2
  38.7 1.3 %pad_maximum_fusion.dep.refs_0_ = bf16[2,3,128,768]{3,2,1,0:T(8,128)(2,1)S(1)} fusion(bf16[1,3,128,768]{3,2,1,0:T(8,128)(2,1)} %bitcast.11, bf16[1,3,128,768]{3,2,1,0:T(8,128)(2,1)S(1)} %get-tuple-element.30), kind=kLoop, calls=%fused_computation | loop fusion | flops 589824 | bytes 2359296 | tf_op jit(solution)/shard_map/stack | solution.py:547
  40.0 1.6 %collective-permute-start.16 = (bf16[2,3,128,768]{3,2,1,0:T(8,128)(2,1)S(1)}, bf16[2,3,128,768]{3,2,1,0:T(8,128)(2,1)S(1)}, u32[]{:S(2)}, u32[]{:S(2)}) collective-permute-start(bf16[2,3,128,768]{3,2,1,0:T(8,128)(2,1)S(1)} %pad_maximum_fusion.dep.refs_0_), channel_id=1, source_target_pairs={{0,16},{4,12},{8,24},{12,4},{16,0},{20,28},{24,8},{28,20},{1,17},{... | collective-permute-start | bytes 3538952 | tf_op jit(solution)/shard_map/ppermute | solution.py:496
  41.6 1.7 %collective-permute-done.2 = bf16[400,128]{1,0:T(8,128)(2,1)S(1)} collective-permute-done((bf16[400,128]{1,0:T(8,128)(2,1)S(1)}, bf16[400,128]{1,0:T(8,128)(2,1)S(1)}, u32[]{:S(2)}, u32[]{:S(2)}) %collective-permute-start.2) | collective-permute-done | bytes 102432 | tf_op jit(solution)/shard_map/ppermute | solution.py:473
  43.6 11.1 %im2col.1 = (bf16[4,6,128,1024]{3,2,1,0:T(8,128)(2,1)}, f32[768,768]{1,0:T(8,128)S(1)}) custom-call(f32[4,40,48,128]{3,2,1,0:T(8,128)S(1)} %copy-done.2, f32[4,40,8,128]{3,2,1,0:T(8,128)S(1)} %maximum_convert_fusion.rim, bf16[400,256]{1,0:T(8,128)(2,1)S(1)} %pad_maximum_fusion.4.edge.dep2, bf16[1024,1536]{1,0:T(8,128)(2,1)S(1)} %copy-done.5, ...), custom_call_target="tpu_custom_call" | custom-call | flops 7549747200 | bytes 10223616 | tf_op jit(solution)/shard_map/im2col/pallas_call | solution.py:393
  54.7 1.4 %copy-done = f32[768,768]{1,0:T(8,128)} copy-done((f32[768,768]{1,0:T(8,128)}, f32[768,768]{1,0:T(8,128)S(1)}, u32[]{:S(2)}) %copy-start) | copy-done | bytes 2359320
  56.2 0.1 collective-permute-done.16.refs_1_
  56.3 0.4 collective-permute-start.18
  56.7 0.2 collective-permute-start.11
  56.9 2.5 %collective-permute-start.12 = (bf16[8,8,768]{2,0,1:T(8,128)(2,1)S(1)}, bf16[8,8,768]{2,0,1:T(8,128)(2,1)S(1)}, u32[]{:S(2)}, u32[]{:S(2)}) collective-permute-start(bf16[8,8,768]{2,0,1:T(8,128)(2,1)S(1)} %pad_maximum_fusion.6), channel_id=1, source_target_pairs={{4,0},{8,4},{12,8},{16,12},{20,16},{24,20},{28,24},{0,28},{5,1},{9... | collective-permute-start | bytes 294920 | tf_op jit(solution)/shard_map/ppermute | solution.py:473
  59.5 1.7 %collective-permute-start.14 = (bf16[128,768]{1,0:T(8,128)(2,1)S(1)}, bf16[128,768]{1,0:T(8,128)(2,1)S(1)}, u32[]{:S(2)}, u32[]{:S(2)}) collective-permute-start(bf16[128,768]{1,0:T(8,128)(2,1)S(1)} %constant_dynamic-slice_fusion), channel_id=1, source_target_pairs={{0,3},{1,0},{2,1},{3,2},{4,7},{5,4},{6,5},{7,6},{8,11},{9,8},{10,9... | collective-permute-start | bytes 589832 | tf_op jit(solution)/shard_map/ppermute | solution.py:491
  61.2 0.6 collective-permute-done.11
  61.8 2.8 %collective-permute-start.13 = (bf16[128,768]{1,0:T(8,128)(2,1)S(1)}, bf16[128,768]{1,0:T(8,128)(2,1)S(1)}, u32[]{:S(2)}, u32[]{:S(2)}) collective-permute-start(bf16[128,768]{1,0:T(8,128)(2,1)S(1)} %constant_dynamic-slice_fusion), channel_id=1, source_target_pairs={{0,2},{1,3},{2,0},{3,1},{4,6},{5,7},{6,4},{7,5},{8,10},{9,11},{10,... | collective-permute-start | bytes 589832 | tf_op jit(solution)/shard_map/ppermute | solution.py:491
  64.6 0.7 copy.35
  65.2 0.6 copy.34
  65.9 8.2 %unembed.3.refs_4_ = f32[4,40,48,128]{3,2,1,0:T(8,128)} custom-call(s32[1]{0:T(128)} %bitcast.12.refs_0_.vid, s32[1]{0:T(128)} %bitcast.me, bf16[8,6,16,768]{3,2,1,0:T(8,128)(2,1)} %tokens.5, bf16[8,16,768]{2,1,0:T(8,128)(2,1)} %copy-done.17, bf16[8,16,768]{2,1,0:T(8,128)(2,1)} %copy-done.16, bf16[64,768]{1,0:T(8,128)(2,1)} %bitcast.47, ...), custom_call_target="tpu_custom_call" | custom-call | flops 1000 | bytes 1000 | tf_op jit(solution)/shard_map/unembed/pallas_call | solution.py:441
  74.1 4.6 %collective-permute-done.13 = bf16[128,768]{1,0:T(8,128)(2,1)S(1)} collective-permute-done((bf16[128,768]{1,0:T(8,128)(2,1)S(1)}, bf16[128,768]{1,0:T(8,128)(2,1)S(1)}, u32[]{:S(2)}, u32[]{:S(2)}) %collective-permute-start.13) | collective-permute-done | bytes 196640 | tf_op jit(solution)/shard_map/ppermute | solution.py:491
  78.7 0.1 fusion.1
  78.8 1.7 %collective-permute-start.15 = (bf16[3,128,768]{2,1,0:T(8,128)(2,1)S(1)}, bf16[3,128,768]{2,1,0:T(8,128)(2,1)S(1)}, u32[]{:S(2)}, u32[]{:S(2)}) collective-permute-start(bf16[3,128,768]{2,1,0:T(8,128)(2,1)S(1)} %get-tuple-element.29.dep), channel_id=1, source_target_pairs={{0,8},{4,20},{8,0},{12,28},{16,24},{20,4},{24,16},{28,12},{1,9},{5... | collective-permute-start | bytes 1769480 | tf_op jit(solution)/shard_map/ppermute | solution.py:496
  80.5 0.6 compare_select_fusion.vid
  81.2 1.0 copy-done.14
  82.2 0.5 copy-done.15
  82.7 8.8 %unembed.4.refs_4_ = f32[4,40,48,128]{3,2,1,0:T(8,128)} custom-call(s32[1]{0:T(128)} %bitcast.62, s32[1]{0:T(128)} %bitcast.me, bf16[8,6,16,768]{3,2,1,0:T(8,128)(2,1)} %tokens.5, bf16[8,16,768]{2,1,0:T(8,128)(2,1)} %copy-done.17, bf16[8,16,768]{2,1,0:T(8,128)(2,1)} %copy-done.16, bf16[64,768]{1,0:T(8,128)(2,1)} %bitcast.48, ...), custom_call_target="tpu_custom_call", output_to_operand_aliasing={{}: (14, {})} | custom-call | flops 1000 | bytes 1000 | tf_op jit(solution)/shard_map/unembed/pallas_call | solution.py:441
  91.5 0.1 pad_maximum_fusion.1.dep.refs_0_
  91.7 0.7 collective-permute-start.19
  92.4 0.6 slice.47.vid
  93.0 14.1 %unembed.5 = f32[4,40,48,128]{3,2,1,0:T(8,128)} custom-call(s32[2]{0:T(128)} %slice.47.vid, s32[1]{0:T(128)} %bitcast.me, bf16[8,6,16,768]{3,2,1,0:T(8,128)(2,1)} %tokens.5, bf16[8,16,768]{2,1,0:T(8,128)(2,1)} %copy-done.17, bf16[8,16,768]{2,1,0:T(8,128)(2,1)} %copy-done.16, bf16[64,768]{1,0:T(8,128)(2,1)} %bitcast.49, ...), custom_call_target="tpu_custom_call", output_to_operand_aliasing={{}: (14, {})} | custom-call | flops 9663676416 | bytes 5111808 | tf_op jit(solution)/shard_map/unembed/pallas_call | solution.py:441
  107.1 0.8 collective-permute-done.19.refs_1_
  108.0 2.8 %collective-permute-done.21.refs_3_ = bf16[2,3,128,768]{3,2,1,0:T(8,128)(2,1)S(1)} collective-permute-done((bf16[2,3,128,768]{3,2,1,0:T(8,128)(2,1)S(1)}, bf16[2,3,128,768]{3,2,1,0:T(8,128)(2,1)S(1)}, u32[]{:S(2)}, u32[]{:S(2)}) %collective-permute-start.21) | collective-permute-done | bytes 1179680 | tf_op jit(solution)/shard_map/ppermute | solution.py:496
  110.8 1.1 copy-done.12
  111.8 10.0 %embed.1 = bf16[8,6,16,768]{3,2,1,0:T(8,128)(2,1)} custom-call(s32[3]{0:T(128)} %compare_select_fusion.vid, s32[1]{0:T(128)} %bitcast.me, bf16[4,768,1024]{2,1,0:T(8,128)(2,1)} %bitcast.46, bf16[2,3,128,768]{3,2,1,0:T(8,128)(2,1)} %copy-done.8, bf16[2,3,128,768]{3,2,1,0:T(8,128)(2,1)} %copy-done.10, bf16[2,3,128,768]{3,2,1,0:T(8,128)(2,1)} %copy-done.11, ...), custom_call_target="tpu_custom_call" | custom-call | flops 3623878656 | bytes 11796480 | tf_op jit(solution)/shard_map/embed/pallas_call | solution.py:413
  (67 shorter events, 0.5 us)
Async XLA Ops:
  0.6 25.5 %copy-start.7 = (bf16[8,6,16,768]{3,2,1,0:T(8,128)(2,1)S(1)}, bf16[8,6,16,768]{3,2,1,0:T(8,128)(2,1)}, u32[]{:S(2)}) copy-start(bf16[8,6,16,768]{3,2,1,0:T(8,128)(2,1)} %tokens.5) | copy-start | bytes 3538948
  1.7 15.1 %collective-permute-start.6 = (bf16[128,768]{1,0:T(8,128)(2,1)S(1)}, bf16[128,768]{1,0:T(8,128)(2,1)S(1)}, u32[]{:S(2)}, u32[]{:S(2)}) collective-permute-start(bf16[128,768]{1,0:T(8,128)(2,1)S(1)} %constant_dynamic-slice_fusion.1.dep), channel_id=1, source_target_pairs={{0,3},{1,0},{2,1},{3,2},{4,7},{5,4},{6,5},{7,6},{8,11},{9,8},{10,9... | collective-permute-start | bytes 589832 | tf_op jit(solution)/shard_map/ppermute | solution.py:491
  6.8 17.6 %collective-permute-start.5 = (bf16[128,768]{1,0:T(8,128)(2,1)S(1)}, bf16[128,768]{1,0:T(8,128)(2,1)S(1)}, u32[]{:S(2)}, u32[]{:S(2)}) collective-permute-start(bf16[128,768]{1,0:T(8,128)(2,1)S(1)} %constant_dynamic-slice_fusion.1.dep), channel_id=1, source_target_pairs={{0,2},{1,3},{2,0},{3,1},{4,6},{5,7},{6,4},{7,5},{8,10},{9,11},{10,... | collective-permute-start | bytes 589832 | tf_op jit(solution)/shard_map/ppermute | solution.py:491
  6.8 17.6 %collective-permute-start.4 = (bf16[128,768]{1,0:T(8,128)(2,1)S(1)}, bf16[128,768]{1,0:T(8,128)(2,1)S(1)}, u32[]{:S(2)}, u32[]{:S(2)}) collective-permute-start(bf16[128,768]{1,0:T(8,128)(2,1)S(1)} %constant_dynamic-slice_fusion.1.dep), channel_id=1, source_target_pairs={{0,1},{1,2},{2,3},{3,0},{4,5},{5,6},{6,7},{7,4},{8,9},{9,10},{10,1... | collective-permute-start | bytes 589832 | tf_op jit(solution)/shard_map/ppermute | solution.py:491
  9.9 23.1 %collective-permute-start.1 = (bf16[320,128]{1,0:T(8,128)(2,1)}, bf16[320,128]{1,0:T(8,128)(2,1)}, u32[]{:S(2)}, u32[]{:S(2)}) collective-permute-start(bf16[320,128]{1,0:T(8,128)(2,1)} %bitcast.3), channel_id=1, source_target_pairs={{1,0},{2,1},{3,2},{5,4},{6,5},{7,6},{9,8},{10,9},{11,10},{13,12},{... | collective-permute-start | bytes 245768 | tf_op jit(solution)/shard_map/ppermute | solution.py:473
  11.2 21.8 %collective-permute-start = (bf16[320,128]{1,0:T(8,128)(2,1)}, bf16[320,128]{1,0:T(8,128)(2,1)}, u32[]{:S(2)}, u32[]{:S(2)}) collective-permute-start(bf16[320,128]{1,0:T(8,128)(2,1)} %bitcast.1), channel_id=1, source_target_pairs={{0,1},{1,2},{2,3},{4,5},{5,6},{6,7},{8,9},{9,10},{10,11},{12,13},{... | collective-permute-start | bytes 245768 | tf_op jit(solution)/shard_map/ppermute | solution.py:473
  24.6 9.6 %copy-start.3 = (bf16[4,1024,128]{2,1,0:T(8,128)(2,1)S(1)}, bf16[4,1024,128]{2,1,0:T(8,128)(2,1)}, u32[]{:S(2)}) copy-start(bf16[4,1024,128]{2,1,0:T(8,128)(2,1)} %constant.38.clone.pick) | copy-start | bytes 3145732
  24.6 14.1 %collective-permute-start.7 = (bf16[3,128,768]{2,1,0:T(8,128)(2,1)S(1)}, bf16[3,128,768]{2,1,0:T(8,128)(2,1)}, u32[]{:S(2)}, u32[]{:S(2)}) collective-permute-start(bf16[3,128,768]{2,1,0:T(8,128)(2,1)S(1)} %get-tuple-element.31), channel_id=1, source_target_pairs={{0,8},{4,20},{8,0},{12,28},{16,24},{20,4},{24,16},{28,12},{1,9},{5... | collective-permute-start | bytes 1769480 | tf_op jit(solution)/shard_map/ppermute | solution.py:496
  26.8 11.8 %collective-permute-start.9 = (bf16[8,16,768]{2,1,0:T(8,128)(2,1)}, bf16[8,16,768]{2,1,0:T(8,128)(2,1)S(1)}, u32[]{:S(2)}, u32[]{:S(2)}) collective-permute-start(bf16[8,16,768]{2,1,0:T(8,128)(2,1)} %get-tuple-element.26), channel_id=1, source_target_pairs={{1,0},{2,1},{3,2},{5,4},{6,5},{7,6},{9,8},{10,9},{11,10},{13,12},{... | collective-permute-start | bytes 589832 | tf_op jit(solution)/shard_map/ppermute | solution.py:473
  28.1 10.5 %collective-permute-start.8 = (bf16[8,16,768]{2,1,0:T(8,128)(2,1)S(1)}, bf16[8,16,768]{2,1,0:T(8,128)(2,1)S(1)}, u32[]{:S(2)}, u32[]{:S(2)}) collective-permute-start(bf16[8,16,768]{2,1,0:T(8,128)(2,1)S(1)} %get-tuple-element.27), channel_id=1, source_target_pairs={{0,1},{1,2},{2,3},{4,5},{5,6},{6,7},{8,9},{9,10},{10,11},{12,13},{... | collective-permute-start | bytes 589832 | tf_op jit(solution)/shard_map/ppermute | solution.py:473
  34.2 2.1 %copy-start.2 = (f32[4,40,48,128]{3,2,1,0:T(8,128)S(1)}, f32[4,40,48,128]{3,2,1,0:T(8,128)}, u32[]{:S(2)}) copy-start(f32[4,40,48,128]{3,2,1,0:T(8,128)} %vol.3) | copy-start | bytes 11796484
  36.3 7.3 %copy-start.5 = (bf16[1024,1536]{1,0:T(8,128)(2,1)S(1)}, bf16[1024,1536]{1,0:T(8,128)(2,1)}, u32[]{:S(2)}) copy-start(bf16[1024,1536]{1,0:T(8,128)(2,1)} %constant.39.clone.spread) | copy-start | bytes 9437188
  38.1 3.5 %collective-permute-start.3 = (bf16[400,128]{1,0:T(8,128)(2,1)S(1)}, bf16[400,128]{1,0:T(8,128)(2,1)S(1)}, u32[]{:S(2)}, u32[]{:S(2)}) collective-permute-start(bf16[400,128]{1,0:T(8,128)(2,1)S(1)} %pack_edges.1), channel_id=1, source_target_pairs={{4,0},{8,4},{12,8},{16,12},{20,16},{24,20},{28,24},{0,28},{5,1},{9... | collective-permute-start | bytes 307208 | tf_op jit(solution)/shard_map/ppermute | solution.py:473
  38.1 5.2 %collective-permute-start.2 = (bf16[400,128]{1,0:T(8,128)(2,1)S(1)}, bf16[400,128]{1,0:T(8,128)(2,1)S(1)}, u32[]{:S(2)}, u32[]{:S(2)}) collective-permute-start(bf16[400,128]{1,0:T(8,128)(2,1)S(1)} %pack_edges.1), channel_id=1, source_target_pairs={{0,4},{4,8},{8,12},{12,16},{16,20},{20,24},{24,28},{28,0},{1,5},{5... | collective-permute-start | bytes 307208 | tf_op jit(solution)/shard_map/ppermute | solution.py:473
  38.6 4.7 %copy-start.16 = (bf16[8,16,768]{2,1,0:T(8,128)(2,1)}, bf16[8,16,768]{2,1,0:T(8,128)(2,1)S(1)}, u32[]{:S(2)}) copy-start(bf16[8,16,768]{2,1,0:T(8,128)(2,1)S(1)} %collective-permute-done.9.below) | copy-start | bytes 589828
  38.6 4.8 %copy-start.17 = (bf16[8,16,768]{2,1,0:T(8,128)(2,1)}, bf16[8,16,768]{2,1,0:T(8,128)(2,1)S(1)}, u32[]{:S(2)}) copy-start(bf16[8,16,768]{2,1,0:T(8,128)(2,1)S(1)} %collective-permute-done.8.above) | copy-start | bytes 589828
  38.6 4.9 %copy-start.4 = (bf16[1008,768]{1,0:T(8,128)(2,1)S(1)}, bf16[1008,768]{1,0:T(8,128)(2,1)}, u32[]{:S(2)}) copy-start(bf16[1008,768]{1,0:T(8,128)(2,1)} %param.12) | copy-start | bytes 4644868
  38.7 4.9 %copy-start.6 = (bf16[4,256,512]{2,1,0:T(8,128)(2,1)S(1)}, bf16[4,256,512]{2,1,0:T(8,128)(2,1)}, u32[]{:S(2)}) copy-start(bf16[4,256,512]{2,1,0:T(8,128)(2,1)} %constant.40.clone.edge_hot) | copy-start | bytes 3145732
  40.0 14.7 %copy-start.1 = (bf16[2,3,128,768]{3,2,1,0:T(8,128)(2,1)}, bf16[2,3,128,768]{3,2,1,0:T(8,128)(2,1)S(1)}, u32[]{:S(2)}) copy-start(bf16[2,3,128,768]{3,2,1,0:T(8,128)(2,1)S(1)} %pad_maximum_fusion.dep.refs_0_) | copy-start | bytes 3538948
  40.0 16.3 %collective-permute-start.16 = (bf16[2,3,128,768]{3,2,1,0:T(8,128)(2,1)S(1)}, bf16[2,3,128,768]{3,2,1,0:T(8,128)(2,1)S(1)}, u32[]{:S(2)}, u32[]{:S(2)}) collective-permute-start(bf16[2,3,128,768]{3,2,1,0:T(8,128)(2,1)S(1)} %pad_maximum_fusion.dep.refs_0_), channel_id=1, source_target_pairs={{0,16},{4,12},{8,24},{12,4},{16,0},{20,28},{24,8},{28,20},{1,17},{... | collective-permute-start | bytes 3538952 | tf_op jit(solution)/shard_map/ppermute | solution.py:496
  43.5 37.6 %collective-permute-start.17 = (bf16[2,3,128,768]{3,2,1,0:T(8,128)(2,1)S(1)}, bf16[2,3,128,768]{3,2,1,0:T(8,128)(2,1)S(1)}, u32[]{:S(2)}, u32[]{:S(2)}) collective-permute-start(bf16[2,3,128,768]{3,2,1,0:T(8,128)(2,1)S(1)} %pad_maximum_fusion.dep.refs_0_), channel_id=1, source_target_pairs={{0,4},{4,0},{8,12},{12,8},{16,20},{20,16},{24,28},{28,24},{1,5},{5... | collective-permute-start | bytes 3538952 | tf_op jit(solution)/shard_map/ppermute | solution.py:496
  54.7 1.5 %copy-start = (f32[768,768]{1,0:T(8,128)}, f32[768,768]{1,0:T(8,128)S(1)}, u32[]{:S(2)}) copy-start(f32[768,768]{1,0:T(8,128)S(1)} %get-tuple-element.15.dep.refs_4_) | copy-start | bytes 7077892
  56.3 17.8 %copy-start.13 = (bf16[2,3,128,768]{3,2,1,0:T(8,128)(2,1)}, bf16[2,3,128,768]{3,2,1,0:T(8,128)(2,1)S(1)}, u32[]{:S(2)}) copy-start(bf16[2,3,128,768]{3,2,1,0:T(8,128)(2,1)S(1)} %collective-permute-done.16.refs_1_) | copy-start | bytes 3538948
  56.3 24.9 %collective-permute-start.18 = (bf16[2,3,128,768]{3,2,1,0:T(8,128)(2,1)S(1)}, bf16[2,3,128,768]{3,2,1,0:T(8,128)(2,1)S(1)}, u32[]{:S(2)}, u32[]{:S(2)}) collective-permute-start(bf16[2,3,128,768]{3,2,1,0:T(8,128)(2,1)S(1)} %collective-permute-done.16.refs_1_), channel_id=1, source_target_pairs={{0,4},{4,0},{8,12},{12,8},{16,20},{20,16},{24,28},{28,24},{1,5},{5... | collective-permute-start | bytes 3538952 | tf_op jit(solution)/shard_map/ppermute | solution.py:496
  56.7 5.1 %collective-permute-start.11 = (bf16[8,8,768]{2,0,1:T(8,128)(2,1)S(1)}, bf16[8,8,768]{2,0,1:T(8,128)(2,1)S(1)}, u32[]{:S(2)}, u32[]{:S(2)}) collective-permute-start(bf16[8,8,768]{2,0,1:T(8,128)(2,1)S(1)} %pad_maximum_fusion.5), channel_id=1, source_target_pairs={{0,4},{4,8},{8,12},{12,16},{16,20},{20,24},{24,28},{28,0},{1,5},{5... | collective-permute-start | bytes 294920 | tf_op jit(solution)/shard_map/ppermute | solution.py:473
  56.9 7.6 %collective-permute-start.12 = (bf16[8,8,768]{2,0,1:T(8,128)(2,1)S(1)}, bf16[8,8,768]{2,0,1:T(8,128)(2,1)S(1)}, u32[]{:S(2)}, u32[]{:S(2)}) collective-permute-start(bf16[8,8,768]{2,0,1:T(8,128)(2,1)S(1)} %pad_maximum_fusion.6), channel_id=1, source_target_pairs={{4,0},{8,4},{12,8},{16,12},{20,16},{24,20},{28,24},{0,28},{5,1},{9... | collective-permute-start | bytes 294920 | tf_op jit(solution)/shard_map/ppermute | solution.py:473
  59.5 14.5 %collective-permute-start.14 = (bf16[128,768]{1,0:T(8,128)(2,1)S(1)}, bf16[128,768]{1,0:T(8,128)(2,1)S(1)}, u32[]{:S(2)}, u32[]{:S(2)}) collective-permute-start(bf16[128,768]{1,0:T(8,128)(2,1)S(1)} %constant_dynamic-slice_fusion), channel_id=1, source_target_pairs={{0,3},{1,0},{2,1},{3,2},{4,7},{5,4},{6,5},{7,6},{8,11},{9,8},{10,9... | collective-permute-start | bytes 589832 | tf_op jit(solution)/shard_map/ppermute | solution.py:491
  61.8 16.9 %collective-permute-start.13 = (bf16[128,768]{1,0:T(8,128)(2,1)S(1)}, bf16[128,768]{1,0:T(8,128)(2,1)S(1)}, u32[]{:S(2)}, u32[]{:S(2)}) collective-permute-start(bf16[128,768]{1,0:T(8,128)(2,1)S(1)} %constant_dynamic-slice_fusion), channel_id=1, source_target_pairs={{0,2},{1,3},{2,0},{3,1},{4,6},{5,7},{6,4},{7,5},{8,10},{9,11},{10,... | collective-permute-start | bytes 589832 | tf_op jit(solution)/shard_map/ppermute | solution.py:491
  64.6 14.1 %collective-permute-start.10 = (bf16[128,768]{1,0:T(8,128)(2,1)S(1)}, bf16[128,768]{1,0:T(8,128)(2,1)S(1)}, u32[]{:S(2)}, u32[]{:S(2)}) collective-permute-start(bf16[128,768]{1,0:T(8,128)(2,1)S(1)} %constant_dynamic-slice_fusion), channel_id=1, source_target_pairs={{0,1},{1,2},{2,3},{3,0},{4,5},{5,6},{6,7},{7,4},{8,9},{9,10},{10,1... | collective-permute-start | bytes 589832 | tf_op jit(solution)/shard_map/ppermute | solution.py:491
  78.8 2.4 %copy-start.9 = (bf16[3,128,768]{2,1,0:T(8,128)(2,1)}, bf16[3,128,768]{2,1,0:T(8,128)(2,1)S(1)}, u32[]{:S(2)}) copy-start(bf16[3,128,768]{2,1,0:T(8,128)(2,1)S(1)} %get-tuple-element.29.dep) | copy-start | bytes 1769476
  78.8 12.7 %collective-permute-start.15 = (bf16[3,128,768]{2,1,0:T(8,128)(2,1)S(1)}, bf16[3,128,768]{2,1,0:T(8,128)(2,1)S(1)}, u32[]{:S(2)}, u32[]{:S(2)}) collective-permute-start(bf16[3,128,768]{2,1,0:T(8,128)(2,1)S(1)} %get-tuple-element.29.dep), channel_id=1, source_target_pairs={{0,8},{4,20},{8,0},{12,28},{16,24},{20,4},{24,16},{28,12},{1,9},{5... | collective-permute-start | bytes 1769480 | tf_op jit(solution)/shard_map/ppermute | solution.py:496
  81.1 1.1 copy-start.14
  81.1 1.5 %copy-start.15 = (bf16[2,3,128,768]{3,2,1,0:T(8,128)(2,1)}, bf16[2,3,128,768]{3,2,1,0:T(8,128)(2,1)S(1)}, u32[]{:S(2)}) copy-start(bf16[2,3,128,768]{3,2,1,0:T(8,128)(2,1)S(1)} %collective-permute-done.18.refs_3_) | copy-start | bytes 3538948
  91.5 0.9 copy-start.18
  91.7 1.4 %copy-start.8 = (bf16[2,3,128,768]{3,2,1,0:T(8,128)(2,1)}, bf16[2,3,128,768]{3,2,1,0:T(8,128)(2,1)S(1)}, u32[]{:S(2)}) copy-start(bf16[2,3,128,768]{3,2,1,0:T(8,128)(2,1)S(1)} %pad_maximum_fusion.1.dep.refs_0_) | copy-start | bytes 3538948
  91.7 16.3 %collective-permute-start.19 = (bf16[2,3,128,768]{3,2,1,0:T(8,128)(2,1)S(1)}, bf16[2,3,128,768]{3,2,1,0:T(8,128)(2,1)S(1)}, u32[]{:S(2)}, u32[]{:S(2)}) collective-permute-start(bf16[2,3,128,768]{3,2,1,0:T(8,128)(2,1)S(1)} %pad_maximum_fusion.1.dep.refs_0_), channel_id=1, source_target_pairs={{0,16},{4,12},{8,24},{12,4},{16,0},{20,28},{24,8},{28,20},{1,17},{... | collective-permute-start | bytes 3538952 | tf_op jit(solution)/shard_map/ppermute | solution.py:496
  93.0 14.9 %collective-permute-start.20 = (bf16[2,3,128,768]{3,2,1,0:T(8,128)(2,1)S(1)}, bf16[2,3,128,768]{3,2,1,0:T(8,128)(2,1)S(1)}, u32[]{:S(2)}, u32[]{:S(2)}) collective-permute-start(bf16[2,3,128,768]{3,2,1,0:T(8,128)(2,1)S(1)} %pad_maximum_fusion.1.dep.refs_0_), channel_id=1, source_target_pairs={{0,4},{4,0},{8,12},{12,8},{16,20},{20,16},{24,28},{28,24},{1,5},{5... | collective-permute-start | bytes 3538952 | tf_op jit(solution)/shard_map/ppermute | solution.py:496
  107.9 2.9 %copy-start.10 = (bf16[2,3,128,768]{3,2,1,0:T(8,128)(2,1)}, bf16[2,3,128,768]{3,2,1,0:T(8,128)(2,1)S(1)}, u32[]{:S(2)}) copy-start(bf16[2,3,128,768]{3,2,1,0:T(8,128)(2,1)S(1)} %collective-permute-done.19.refs_1_) | copy-start | bytes 3538948
  107.9 2.8 %collective-permute-start.21 = (bf16[2,3,128,768]{3,2,1,0:T(8,128)(2,1)S(1)}, bf16[2,3,128,768]{3,2,1,0:T(8,128)(2,1)S(1)}, u32[]{:S(2)}, u32[]{:S(2)}) collective-permute-start(bf16[2,3,128,768]{3,2,1,0:T(8,128)(2,1)S(1)} %collective-permute-done.19.refs_1_), channel_id=1, source_target_pairs={{0,4},{4,0},{8,12},{12,8},{16,20},{20,16},{24,28},{28,24},{1,5},{5... | collective-permute-start | bytes 3538952 | tf_op jit(solution)/shard_map/ppermute | solution.py:496
  107.9 2.8 %copy-start.11 = (bf16[2,3,128,768]{3,2,1,0:T(8,128)(2,1)}, bf16[2,3,128,768]{3,2,1,0:T(8,128)(2,1)S(1)}, u32[]{:S(2)}) copy-start(bf16[2,3,128,768]{3,2,1,0:T(8,128)(2,1)S(1)} %collective-permute-done.20.refs_2_) | copy-start | bytes 3538948
  110.8 1.1 copy-start.12

commit v5 on v4

--- a/solution.py
+++ b/solution.py
@@ -259,7 +259,6 @@
     def _():
         for c in copies(s, begin) + token_copies:
             c.start()
-        hot_copy.start()
         if c_lanes > 2 * half:
             t_side[2 * half :, :] = jnp.zeros((c_lanes - 2 * half, width), BF)
 
@@ -267,6 +266,7 @@
     def _():
         for c in copies(s, begin) + token_copies:
             c.wait()
+        hot_copy.start()
 
     @pl.when(s > 0)
     def _():
@@ -544,12 +544,13 @@
 
     if fast:
         u_near = jnp.stack(u_near)
+        e_own = own_piece(embed_weight, me)
         u_pair = jnp.stack([u_near, after(flip(u_near, first_mask), row_above, row_below)])
         u_rest = flip(u_pair, second_mask)
-        e_got = from_lat(after(own_piece(embed_weight, me), u_near))
+        e_got = from_lat(after(e_own, u_near))
         own = lat.astype(jnp.int32).reshape(1)
         others = lax.rem(lat - jnp.arange(1, lats, dtype=jnp.int32) + lats, lats).astype(jnp.int32)
-        a, sums = im2col(volume_b, rim, edge, spread, dims, own, embed_weight[None], (u_pair, edge))
+        a, sums = im2col(volume_b, rim, edge, spread, dims, own, embed_weight[None], (u_pair, after(edge, e_own)))
         u_rest = after(u_rest, sums)
         u_all = (u_pair, u_rest, flip(u_pair, core_mask), flip(u_rest, core_mask))
         first_two = jnp.concatenate([own, others[:1]])

time: 122 us -> 122 us (level)
  starting transfers between devices: 32.7 us -> 29.2 us
  local copies, waits for them, and re-layouts: 12.5 us -> 14.7 us
    ppermute x4, starting transfers between devices: 10.9 us -> 7.55 us  [both_ways(): lax.ppermute(up_rows, axis, up)]
    ppermute x6, starting transfers between devices: 10.6 us -> 7.54 us  [from_lat(): lax.ppermute(piece, 'lat', [(i, (i + s) % size) for i in range(size)])]
    ppermute x6, waiting for transfers between devices: 12.3 us -> 9.93 us  [from_lat(): lax.ppermute(piece, 'lat', [(i, (i + s) % size) for i in range(size)])]
    ppermute x4, starting transfers between devices: 5.16 us -> 7.41 us  [both_ways(): lax.ppermute(down_rows, axis, [(j, i) for i, j in up])]
    ppermute x4, waiting for transfers between devices: 2.33 us -> 4.55 us  [both_ways(): lax.ppermute(up_rows, axis, up)]
    slice x1, local copies, waits for them, and re-layouts: 0.23 us -> 1.47 us  [column(): tokens_a[:, :, i]]
    unnamed x40 -> x39, local copies, waits for them, and re-layouts: 6.2 us -> 6.2 us
  transfers between devices with their start and end apart: 22 -> 22, of which waited for: 7 -> 7; matrix products, arithmetic and copies ran while one was open for 7% -> 9% of each run, Pallas kernels for 36% -> 36%
where the time goes in v5:
time: 122 us; the launch traced here: 121 us
  Pallas kernels  53.8 us (44%)
  starting transfers between devices  29.2 us (24%)
  waiting for transfers between devices  18.9 us (15%)
  local copies, waits for them, and re-layouts  14.7 us (12%)
  other arithmetic  3.3 us (3%)
  between operations  1.27 us (1%)
    pallas_call x3, Pallas kernels, unembed(): pl.pallas_call(functools.partial(unembed_kernel, kinds), grid_spec=pltpu....  31 us
    pallas_call x1, Pallas kernels, im2col(): pl.pallas_call(functools.partial(im2col_kernel, nk, ni, nj, (DZ * DY * DX...  11.1 us
    pallas_call x1, Pallas kernels, embed(): pl.pallas_call(functools.partial(embed_kernel, n, gathered, first), in_sp...  10 us
    ppermute x6, waiting for transfers between devices, from_lat(): lax.ppermute(piece, 'lat', [(i, (i + s) % size) for i in range(size)])  9.93 us
    ppermute x4, starting transfers between devices, both_ways(): lax.ppermute(up_rows, axis, up)  7.55 us
    ppermute x6, starting transfers between devices, from_lat(): lax.ppermute(piece, 'lat', [(i, (i + s) % size) for i in range(size)])  7.54 us
    ppermute x4, starting transfers between devices, both_ways(): lax.ppermute(down_rows, axis, [(j, i) for i, j in up])  7.41 us
    ppermute x8, starting transfers between devices, flip(): lax.ppermute(x, 'lon', [(i, i ^ mask(i)) for i in range(lax.axis_size('lo...  6.72 us
  transfers between devices with their start and end apart: 22, of which 7 were waited for; matrix products, arithmetic and copies ran while one was open for 9% of the time, Pallas kernels for 36%

profile of v5, /device:TPU:0, one launch (start us, length us, event | category | flops | bytes accessed | tf_op | source)
XLA Modules:
  0.0 121.2 jit_solution(388486388117003240)
XLA Ops:
  0.6 1.0 constant_dynamic-slice_fusion.1.dep
  1.6 5.1 %collective-permute-start.6 = (bf16[128,768]{1,0:T(8,128)(2,1)S(1)}, bf16[128,768]{1,0:T(8,128)(2,1)S(1)}, u32[]{:S(2)}, u32[]{:S(2)}) collective-permute-start(bf16[128,768]{1,0:T(8,128)(2,1)S(1)} %constant_dynamic-slice_fusion.1.dep), channel_id=1, source_target_pairs={{0,3},{1,0},{2,1},{3,2},{4,7},{5,4},{6,5},{7,6},{8,11},{9,8},{10,9... | collective-permute-start | bytes 589832 | tf_op jit(solution)/shard_map/ppermute | solution.py:491
  6.7 1.0 collective-permute-start.4
  7.8 2.0 %fusion.3 = (bf16[4,40,2,128]{3,2,1,0:T(2,128)(2,1)S(1)}, bf16[4,40,2,128]{3,2,1,0:T(2,128)(2,1)}) fusion(f32[4,40,48,128]{3,2,1,0:T(8,128)} %vol.3), kind=kLoop, calls=%fused_computation.22 | loop fusion | bytes 327680 | tf_op jit(solution)/shard_map/slice | solution.py:524
  9.8 1.3 %collective-permute-start.1 = (bf16[320,128]{1,0:T(8,128)(2,1)}, bf16[320,128]{1,0:T(8,128)(2,1)}, u32[]{:S(2)}, u32[]{:S(2)}) collective-permute-start(bf16[320,128]{1,0:T(8,128)(2,1)} %bitcast.3), channel_id=1, source_target_pairs={{1,0},{2,1},{3,2},{5,4},{6,5},{7,6},{9,8},{10,9},{11,10},{13,12},{... | collective-permute-start | bytes 245768 | tf_op jit(solution)/shard_map/ppermute | solution.py:473
  11.1 5.6 %collective-permute-start = (bf16[320,128]{1,0:T(8,128)(2,1)S(1)}, bf16[320,128]{1,0:T(8,128)(2,1)}, u32[]{:S(2)}, u32[]{:S(2)}) collective-permute-start(bf16[320,128]{1,0:T(8,128)(2,1)S(1)} %bitcast.62), channel_id=1, source_target_pairs={{0,1},{1,2},{2,3},{4,5},{5,6},{6,7},{8,9},{9,10},{10,11},{12,13},{... | collective-permute-start | bytes 245768 | tf_op jit(solution)/shard_map/ppermute | solution.py:473
  16.7 1.7 %slice_bitcast_fusion = (bf16[8,16,768]{2,1,0:T(8,128)(2,1)}, bf16[8,16,768]{2,1,0:T(8,128)(2,1)S(1)}) fusion(bf16[8,6,16,768]{3,2,1,0:T(8,128)(2,1)} %tokens.5), kind=kLoop, calls=%fused_computation.5 | loop fusion | bytes 786432 | tf_op jit(solution)/shard_map/squeeze | solution.py:528
  18.5 1.3 %collective-permute-start.9 = (bf16[8,16,768]{2,1,0:T(8,128)(2,1)}, bf16[8,16,768]{2,1,0:T(8,128)(2,1)S(1)}, u32[]{:S(2)}, u32[]{:S(2)}) collective-permute-start(bf16[8,16,768]{2,1,0:T(8,128)(2,1)} %get-tuple-element.28), channel_id=1, source_target_pairs={{1,0},{2,1},{3,2},{5,4},{6,5},{7,6},{9,8},{10,9},{11,10},{13,12},{... | collective-permute-start | bytes 589832 | tf_op jit(solution)/shard_map/ppermute | solution.py:473
  19.7 4.7 %collective-permute-done.5 = bf16[128,768]{1,0:T(8,128)(2,1)S(1)} collective-permute-done((bf16[128,768]{1,0:T(8,128)(2,1)S(1)}, bf16[128,768]{1,0:T(8,128)(2,1)S(1)}, u32[]{:S(2)}, u32[]{:S(2)}) %collective-permute-start.5) | collective-permute-done | bytes 196640 | tf_op jit(solution)/shard_map/ppermute | solution.py:491
  24.4 1.3 %collective-permute-start.8 = (bf16[8,16,768]{2,1,0:T(8,128)(2,1)S(1)}, bf16[8,16,768]{2,1,0:T(8,128)(2,1)S(1)}, u32[]{:S(2)}, u32[]{:S(2)}) collective-permute-start(bf16[8,16,768]{2,1,0:T(8,128)(2,1)S(1)} %get-tuple-element.29), channel_id=1, source_target_pairs={{0,1},{1,2},{2,3},{4,5},{5,6},{6,7},{8,9},{9,10},{10,11},{12,13},{... | collective-permute-start | bytes 589832 | tf_op jit(solution)/shard_map/ppermute | solution.py:473
  25.7 0.1 fusion.2
  25.8 1.6 %collective-permute-start.7 = (bf16[3,128,768]{2,1,0:T(8,128)(2,1)S(1)}, bf16[3,128,768]{2,1,0:T(8,128)(2,1)}, u32[]{:S(2)}, u32[]{:S(2)}) collective-permute-start(bf16[3,128,768]{2,1,0:T(8,128)(2,1)S(1)} %get-tuple-element.33), channel_id=1, source_target_pairs={{0,8},{4,20},{8,0},{12,28},{16,24},{20,4},{24,16},{28,12},{1,9},{5... | collective-permute-start | bytes 1769480 | tf_op jit(solution)/shard_map/ppermute | solution.py:496
  27.4 1.5 %fusion.4 = (bf16[8,6,1,768]{3,2,1,0:T(2,128)(2,1)S(1)}, bf16[8,6,1,768]{3,2,1,0:T(2,128)(2,1)S(1)}) fusion(bf16[8,6,16,768]{3,2,1,0:T(8,128)(2,1)} %tokens.5), kind=kLoop, calls=%fused_computation.23 | loop fusion | bytes 294912 | tf_op jit(solution)/shard_map/slice | solution.py:538
  28.9 0.1 pad.18.clone
  29.0 1.1 maximum_convert_fusion.rim
  30.1 2.1 %copy-done.2 = f32[4,40,48,128]{3,2,1,0:T(8,128)S(1)} copy-done((f32[4,40,48,128]{3,2,1,0:T(8,128)S(1)}, f32[4,40,48,128]{3,2,1,0:T(8,128)}, u32[]{:S(2)}) %copy-start.2) | copy-done | bytes 3932184
  32.2 1.7 %pack_edges.1 = bf16[400,128]{1,0:T(8,128)(2,1)S(1)} custom-call(f32[4,40,48,128]{3,2,1,0:T(8,128)S(1)} %copy-done.2, f32[4,40,8,128]{3,2,1,0:T(8,128)S(1)} %maximum_convert_fusion.rim, bf16[4,1024,128]{2,1,0:T(8,128)(2,1)S(1)} %copy-done.3, bf16[128,768]{1,0:T(8,128)(2,1)S(1)} %constant_dynamic-slice_fusion.1.dep), custom_call_target="tpu_custom_call" | custom-call | flops 704643072 | bytes 3932160 | tf_op jit(solution)/shard_map/pack_edges/pallas_call | solution.py:367
  34.1 2.7 %collective-permute-start.3 = (bf16[400,128]{1,0:T(8,128)(2,1)S(1)}, bf16[400,128]{1,0:T(8,128)(2,1)S(1)}, u32[]{:S(2)}, u32[]{:S(2)}) collective-permute-start(bf16[400,128]{1,0:T(8,128)(2,1)S(1)} %pack_edges.1), channel_id=1, source_target_pairs={{4,0},{8,4},{12,8},{16,12},{20,16},{24,20},{28,24},{0,28},{5,1},{9... | collective-permute-start | bytes 307208 | tf_op jit(solution)/shard_map/ppermute | solution.py:473
  36.7 2.3 %collective-permute-done.2 = bf16[400,128]{1,0:T(8,128)(2,1)S(1)} collective-permute-done((bf16[400,128]{1,0:T(8,128)(2,1)S(1)}, bf16[400,128]{1,0:T(8,128)(2,1)S(1)}, u32[]{:S(2)}, u32[]{:S(2)}) %collective-permute-start.2) | collective-permute-done | bytes 102432 | tf_op jit(solution)/shard_map/ppermute | solution.py:473
  39.1 1.3 %pad_maximum_fusion.dep.refs_0_ = bf16[2,3,128,768]{3,2,1,0:T(8,128)(2,1)S(1)} fusion(bf16[1,3,128,768]{3,2,1,0:T(8,128)(2,1)} %bitcast.11, bf16[1,3,128,768]{3,2,1,0:T(8,128)(2,1)S(1)} %get-tuple-element.32), kind=kLoop, calls=%fused_computation | loop fusion | flops 589824 | bytes 2359296 | tf_op jit(solution)/shard_map/stack | solution.py:548
  40.4 2.6 %collective-permute-start.16 = (bf16[2,3,128,768]{3,2,1,0:T(8,128)(2,1)S(1)}, bf16[2,3,128,768]{3,2,1,0:T(8,128)(2,1)S(1)}, u32[]{:S(2)}, u32[]{:S(2)}) collective-permute-start(bf16[2,3,128,768]{3,2,1,0:T(8,128)(2,1)S(1)} %pad_maximum_fusion.dep.refs_0_), channel_id=1, source_target_pairs={{0,16},{4,12},{8,24},{12,4},{16,0},{20,28},{24,8},{28,20},{1,17},{... | collective-permute-start | bytes 3538952 | tf_op jit(solution)/shard_map/ppermute | solution.py:496
  43.2 0.1 collective-permute-start.17
  43.3 11.1 %im2col.1 = (bf16[4,6,128,1024]{3,2,1,0:T(8,128)(2,1)}, f32[768,768]{1,0:T(8,128)S(1)}) custom-call(f32[4,40,48,128]{3,2,1,0:T(8,128)S(1)} %copy-done.2, f32[4,40,8,128]{3,2,1,0:T(8,128)S(1)} %maximum_convert_fusion.rim, bf16[400,256]{1,0:T(8,128)(2,1)S(1)} %constant_dynamic-update-slice_fusion.edge.dep2, bf16[1024,1536]{1,0:T(8,128)(2,1)S(1)} %copy-done.5, ...), custom_call_target="tpu_custom_call" | custom-call | flops 7549747200 | bytes 10223616 | tf_op jit(solution)/shard_map/im2col/pallas_call | solution.py:393
  54.4 1.5 %copy-done = f32[768,768]{1,0:T(8,128)} copy-done((f32[768,768]{1,0:T(8,128)}, f32[768,768]{1,0:T(8,128)S(1)}, u32[]{:S(2)}) %copy-start) | copy-done | bytes 2359320
  55.9 1.3 %collective-permute-done.16.refs_1_ = bf16[2,3,128,768]{3,2,1,0:T(8,128)(2,1)S(1)} collective-permute-done((bf16[2,3,128,768]{3,2,1,0:T(8,128)(2,1)S(1)}, bf16[2,3,128,768]{3,2,1,0:T(8,128)(2,1)S(1)}, u32[]{:S(2)}, u32[]{:S(2)}) %collective-permute-start.16) | collective-permute-done | bytes 1179680 | tf_op jit(solution)/shard_map/ppermute | solution.py:496
  57.3 0.6 collective-permute-start.11
  57.8 2.2 %collective-permute-start.12 = (bf16[8,8,768]{2,0,1:T(8,128)(2,1)S(1)}, bf16[8,8,768]{2,0,1:T(8,128)(2,1)S(1)}, u32[]{:S(2)}, u32[]{:S(2)}) collective-permute-start(bf16[8,8,768]{2,0,1:T(8,128)(2,1)S(1)} %pad_maximum_fusion.5), channel_id=1, source_target_pairs={{4,0},{8,4},{12,8},{16,12},{20,16},{24,20},{28,24},{0,28},{5,1},{9... | collective-permute-start | bytes 294920 | tf_op jit(solution)/shard_map/ppermute | solution.py:473
  60.0 2.2 %collective-permute-done.11 = bf16[8,8,768]{2,0,1:T(8,128)(2,1)S(1)} collective-permute-done((bf16[8,8,768]{2,0,1:T(8,128)(2,1)S(1)}, bf16[8,8,768]{2,0,1:T(8,128)(2,1)S(1)}, u32[]{:S(2)}, u32[]{:S(2)}) %collective-permute-start.11) | collective-permute-done | bytes 98336 | tf_op jit(solution)/shard_map/ppermute | solution.py:473
  62.3 1.4 %collective-permute-start.13 = (bf16[128,768]{1,0:T(8,128)(2,1)S(1)}, bf16[128,768]{1,0:T(8,128)(2,1)S(1)}, u32[]{:S(2)}, u32[]{:S(2)}) collective-permute-start(bf16[128,768]{1,0:T(8,128)(2,1)S(1)} %constant_dynamic-slice_fusion), channel_id=1, source_target_pairs={{0,2},{1,3},{2,0},{3,1},{4,6},{5,7},{6,4},{7,5},{8,10},{9,11},{10,... | collective-permute-start | bytes 589832 | tf_op jit(solution)/shard_map/ppermute | solution.py:491
  63.7 0.7 copy.35
  64.3 0.7 copy.34
  65.0 8.2 %unembed.3.refs_4_ = f32[4,40,48,128]{3,2,1,0:T(8,128)} custom-call(s32[1]{0:T(128)} %bitcast.12.refs_0_.vid, s32[1]{0:T(128)} %bitcast.me, bf16[8,6,16,768]{3,2,1,0:T(8,128)(2,1)} %tokens.5, bf16[8,16,768]{2,1,0:T(8,128)(2,1)} %copy-done.16, bf16[8,16,768]{2,1,0:T(8,128)(2,1)} %copy-done.15, bf16[64,768]{1,0:T(8,128)(2,1)} %bitcast.47, ...), custom_call_target="tpu_custom_call" | custom-call | flops 1000 | bytes 1000 | tf_op jit(solution)/shard_map/unembed/pallas_call | solution.py:441
  73.2 5.3 %collective-permute-done.13 = bf16[128,768]{1,0:T(8,128)(2,1)S(1)} collective-permute-done((bf16[128,768]{1,0:T(8,128)(2,1)S(1)}, bf16[128,768]{1,0:T(8,128)(2,1)S(1)}, u32[]{:S(2)}, u32[]{:S(2)}) %collective-permute-start.13) | collective-permute-done | bytes 196640 | tf_op jit(solution)/shard_map/ppermute | solution.py:491
  78.4 0.1 fusion.1
  78.5 1.2 %collective-permute-start.15 = (bf16[3,128,768]{2,1,0:T(8,128)(2,1)S(1)}, bf16[3,128,768]{2,1,0:T(8,128)(2,1)S(1)}, u32[]{:S(2)}, u32[]{:S(2)}) collective-permute-start(bf16[3,128,768]{2,1,0:T(8,128)(2,1)S(1)} %get-tuple-element.31.dep), channel_id=1, source_target_pairs={{0,8},{4,20},{8,0},{12,28},{16,24},{20,4},{24,16},{28,12},{1,9},{5... | collective-permute-start | bytes 1769480 | tf_op jit(solution)/shard_map/ppermute | solution.py:496
  79.8 0.6 compare_select_fusion.vid
  80.4 1.0 copy-done.13
  81.4 0.5 copy-done.14
  81.9 8.8 %unembed.4.refs_4_ = f32[4,40,48,128]{3,2,1,0:T(8,128)} custom-call(s32[1]{0:T(128)} %bitcast.63, s32[1]{0:T(128)} %bitcast.me, bf16[8,6,16,768]{3,2,1,0:T(8,128)(2,1)} %tokens.5, bf16[8,16,768]{2,1,0:T(8,128)(2,1)} %copy-done.16, bf16[8,16,768]{2,1,0:T(8,128)(2,1)} %copy-done.15, bf16[64,768]{1,0:T(8,128)(2,1)} %bitcast.48, ...), custom_call_target="tpu_custom_call", output_to_operand_aliasing={{}: (14, {})} | custom-call | flops 1000 | bytes 1000 | tf_op jit(solution)/shard_map/unembed/pallas_call | solution.py:441
  90.7 0.1 pad_maximum_fusion.1.dep.refs_0_
  90.8 1.1 collective-permute-start.19
  91.9 0.7 slice.47.vid
  92.6 14.1 %unembed.5 = f32[4,40,48,128]{3,2,1,0:T(8,128)} custom-call(s32[2]{0:T(128)} %slice.47.vid, s32[1]{0:T(128)} %bitcast.me, bf16[8,6,16,768]{3,2,1,0:T(8,128)(2,1)} %tokens.5, bf16[8,16,768]{2,1,0:T(8,128)(2,1)} %copy-done.16, bf16[8,16,768]{2,1,0:T(8,128)(2,1)} %copy-done.15, bf16[64,768]{1,0:T(8,128)(2,1)} %bitcast.49, ...), custom_call_target="tpu_custom_call", output_to_operand_aliasing={{}: (14, {})} | custom-call | flops 9663676416 | bytes 5111808 | tf_op jit(solution)/shard_map/unembed/pallas_call | solution.py:441
  106.7 0.4 collective-permute-done.19.refs_1_
  107.1 0.2 collective-permute-start.21
  107.3 2.7 %collective-permute-done.21.refs_3_ = bf16[2,3,128,768]{3,2,1,0:T(8,128)(2,1)S(1)} collective-permute-done((bf16[2,3,128,768]{3,2,1,0:T(8,128)(2,1)S(1)}, bf16[2,3,128,768]{3,2,1,0:T(8,128)(2,1)S(1)}, u32[]{:S(2)}, u32[]{:S(2)}) %collective-permute-start.21) | collective-permute-done | bytes 1179680 | tf_op jit(solution)/shard_map/ppermute | solution.py:496
  110.0 1.0 copy-done.11
  111.0 10.0 %embed.1 = bf16[8,6,16,768]{3,2,1,0:T(8,128)(2,1)} custom-call(s32[3]{0:T(128)} %compare_select_fusion.vid, s32[1]{0:T(128)} %bitcast.me, bf16[4,768,1024]{2,1,0:T(8,128)(2,1)} %bitcast.46, bf16[2,3,128,768]{3,2,1,0:T(8,128)(2,1)} %copy-done.7, bf16[2,3,128,768]{3,2,1,0:T(8,128)(2,1)} %copy-done.9, bf16[2,3,128,768]{3,2,1,0:T(8,128)(2,1)} %copy-done.10, ...), custom_call_target="tpu_custom_call" | custom-call | flops 3623878656 | bytes 11796480 | tf_op jit(solution)/shard_map/embed/pallas_call | solution.py:413
  (66 shorter events, 0.5 us)
Async XLA Ops:
  1.6 16.8 %collective-permute-start.6 = (bf16[128,768]{1,0:T(8,128)(2,1)S(1)}, bf16[128,768]{1,0:T(8,128)(2,1)S(1)}, u32[]{:S(2)}, u32[]{:S(2)}) collective-permute-start(bf16[128,768]{1,0:T(8,128)(2,1)S(1)} %constant_dynamic-slice_fusion.1.dep), channel_id=1, source_target_pairs={{0,3},{1,0},{2,1},{3,2},{4,7},{5,4},{6,5},{7,6},{8,11},{9,8},{10,9... | collective-permute-start | bytes 589832 | tf_op jit(solution)/shard_map/ppermute | solution.py:491
  6.7 17.7 %collective-permute-start.5 = (bf16[128,768]{1,0:T(8,128)(2,1)S(1)}, bf16[128,768]{1,0:T(8,128)(2,1)S(1)}, u32[]{:S(2)}, u32[]{:S(2)}) collective-permute-start(bf16[128,768]{1,0:T(8,128)(2,1)S(1)} %constant_dynamic-slice_fusion.1.dep), channel_id=1, source_target_pairs={{0,2},{1,3},{2,0},{3,1},{4,6},{5,7},{6,4},{7,5},{8,10},{9,11},{10,... | collective-permute-start | bytes 589832 | tf_op jit(solution)/shard_map/ppermute | solution.py:491
  6.7 19.0 %collective-permute-start.4 = (bf16[128,768]{1,0:T(8,128)(2,1)S(1)}, bf16[128,768]{1,0:T(8,128)(2,1)S(1)}, u32[]{:S(2)}, u32[]{:S(2)}) collective-permute-start(bf16[128,768]{1,0:T(8,128)(2,1)S(1)} %constant_dynamic-slice_fusion.1.dep), channel_id=1, source_target_pairs={{0,1},{1,2},{2,3},{3,0},{4,5},{5,6},{6,7},{7,4},{8,9},{9,10},{10,1... | collective-permute-start | bytes 589832 | tf_op jit(solution)/shard_map/ppermute | solution.py:491
  9.8 19.2 %collective-permute-start.1 = (bf16[320,128]{1,0:T(8,128)(2,1)}, bf16[320,128]{1,0:T(8,128)(2,1)}, u32[]{:S(2)}, u32[]{:S(2)}) collective-permute-start(bf16[320,128]{1,0:T(8,128)(2,1)} %bitcast.3), channel_id=1, source_target_pairs={{1,0},{2,1},{3,2},{5,4},{6,5},{7,6},{9,8},{10,9},{11,10},{13,12},{... | collective-permute-start | bytes 245768 | tf_op jit(solution)/shard_map/ppermute | solution.py:473
  11.1 17.9 %collective-permute-start = (bf16[320,128]{1,0:T(8,128)(2,1)S(1)}, bf16[320,128]{1,0:T(8,128)(2,1)}, u32[]{:S(2)}, u32[]{:S(2)}) collective-permute-start(bf16[320,128]{1,0:T(8,128)(2,1)S(1)} %bitcast.62), channel_id=1, source_target_pairs={{0,1},{1,2},{2,3},{4,5},{5,6},{6,7},{8,9},{9,10},{10,11},{12,13},{... | collective-permute-start | bytes 245768 | tf_op jit(solution)/shard_map/ppermute | solution.py:473
  18.5 20.6 %collective-permute-start.9 = (bf16[8,16,768]{2,1,0:T(8,128)(2,1)}, bf16[8,16,768]{2,1,0:T(8,128)(2,1)S(1)}, u32[]{:S(2)}, u32[]{:S(2)}) collective-permute-start(bf16[8,16,768]{2,1,0:T(8,128)(2,1)} %get-tuple-element.28), channel_id=1, source_target_pairs={{1,0},{2,1},{3,2},{5,4},{6,5},{7,6},{9,8},{10,9},{11,10},{13,12},{... | collective-permute-start | bytes 589832 | tf_op jit(solution)/shard_map/ppermute | solution.py:473
  24.4 14.7 %collective-permute-start.8 = (bf16[8,16,768]{2,1,0:T(8,128)(2,1)S(1)}, bf16[8,16,768]{2,1,0:T(8,128)(2,1)S(1)}, u32[]{:S(2)}, u32[]{:S(2)}) collective-permute-start(bf16[8,16,768]{2,1,0:T(8,128)(2,1)S(1)} %get-tuple-element.29), channel_id=1, source_target_pairs={{0,1},{1,2},{2,3},{4,5},{5,6},{6,7},{8,9},{9,10},{10,11},{12,13},{... | collective-permute-start | bytes 589832 | tf_op jit(solution)/shard_map/ppermute | solution.py:473
  25.8 4.3 %copy-start.3 = (bf16[4,1024,128]{2,1,0:T(8,128)(2,1)S(1)}, bf16[4,1024,128]{2,1,0:T(8,128)(2,1)}, u32[]{:S(2)}) copy-start(bf16[4,1024,128]{2,1,0:T(8,128)(2,1)} %constant.38.clone.pick) | copy-start | bytes 3145732
  25.8 13.3 %collective-permute-start.7 = (bf16[3,128,768]{2,1,0:T(8,128)(2,1)S(1)}, bf16[3,128,768]{2,1,0:T(8,128)(2,1)}, u32[]{:S(2)}, u32[]{:S(2)}) collective-permute-start(bf16[3,128,768]{2,1,0:T(8,128)(2,1)S(1)} %get-tuple-element.33), channel_id=1, source_target_pairs={{0,8},{4,20},{8,0},{12,28},{16,24},{20,4},{24,16},{28,12},{1,9},{5... | collective-permute-start | bytes 1769480 | tf_op jit(solution)/shard_map/ppermute | solution.py:496
  30.1 2.1 %copy-start.2 = (f32[4,40,48,128]{3,2,1,0:T(8,128)S(1)}, f32[4,40,48,128]{3,2,1,0:T(8,128)}, u32[]{:S(2)}) copy-start(f32[4,40,48,128]{3,2,1,0:T(8,128)} %vol.3) | copy-start | bytes 11796484
  32.2 1.8 %copy-start.4 = (bf16[1008,768]{1,0:T(8,128)(2,1)S(1)}, bf16[1008,768]{1,0:T(8,128)(2,1)}, u32[]{:S(2)}) copy-start(bf16[1008,768]{1,0:T(8,128)(2,1)} %param.12) | copy-start | bytes 4644868
  32.2 11.1 %copy-start.6 = (bf16[4,256,512]{2,1,0:T(8,128)(2,1)S(1)}, bf16[4,256,512]{2,1,0:T(8,128)(2,1)}, u32[]{:S(2)}) copy-start(bf16[4,256,512]{2,1,0:T(8,128)(2,1)} %constant.40.clone.edge_hot) | copy-start | bytes 3145732
  33.9 5.1 %collective-permute-start.2 = (bf16[400,128]{1,0:T(8,128)(2,1)S(1)}, bf16[400,128]{1,0:T(8,128)(2,1)S(1)}, u32[]{:S(2)}, u32[]{:S(2)}) collective-permute-start(bf16[400,128]{1,0:T(8,128)(2,1)S(1)} %pack_edges.1), channel_id=1, source_target_pairs={{0,4},{4,8},{8,12},{12,16},{16,20},{20,24},{24,28},{28,0},{1,5},{5... | collective-permute-start | bytes 307208 | tf_op jit(solution)/shard_map/ppermute | solution.py:473
  34.0 9.3 %copy-start.5 = (bf16[1024,1536]{1,0:T(8,128)(2,1)S(1)}, bf16[1024,1536]{1,0:T(8,128)(2,1)}, u32[]{:S(2)}) copy-start(bf16[1024,1536]{1,0:T(8,128)(2,1)} %constant.39.clone.spread) | copy-start | bytes 9437188
  34.1 8.9 %collective-permute-start.3 = (bf16[400,128]{1,0:T(8,128)(2,1)S(1)}, bf16[400,128]{1,0:T(8,128)(2,1)S(1)}, u32[]{:S(2)}, u32[]{:S(2)}) collective-permute-start(bf16[400,128]{1,0:T(8,128)(2,1)S(1)} %pack_edges.1), channel_id=1, source_target_pairs={{4,0},{8,4},{12,8},{16,12},{20,16},{24,20},{28,24},{0,28},{5,1},{9... | collective-permute-start | bytes 307208 | tf_op jit(solution)/shard_map/ppermute | solution.py:473
  39.1 4.0 %copy-start.15 = (bf16[8,16,768]{2,1,0:T(8,128)(2,1)}, bf16[8,16,768]{2,1,0:T(8,128)(2,1)S(1)}, u32[]{:S(2)}) copy-start(bf16[8,16,768]{2,1,0:T(8,128)(2,1)S(1)} %collective-permute-done.9.below) | copy-start | bytes 589828
  39.1 4.0 %copy-start.16 = (bf16[8,16,768]{2,1,0:T(8,128)(2,1)}, bf16[8,16,768]{2,1,0:T(8,128)(2,1)S(1)}, u32[]{:S(2)}) copy-start(bf16[8,16,768]{2,1,0:T(8,128)(2,1)S(1)} %collective-permute-done.8.above) | copy-start | bytes 589828
  40.4 14.0 %copy-start.1 = (bf16[2,3,128,768]{3,2,1,0:T(8,128)(2,1)}, bf16[2,3,128,768]{3,2,1,0:T(8,128)(2,1)S(1)}, u32[]{:S(2)}) copy-start(bf16[2,3,128,768]{3,2,1,0:T(8,128)(2,1)S(1)} %pad_maximum_fusion.dep.refs_0_) | copy-start | bytes 3538948
  40.4 16.8 %collective-permute-start.16 = (bf16[2,3,128,768]{3,2,1,0:T(8,128)(2,1)S(1)}, bf16[2,3,128,768]{3,2,1,0:T(8,128)(2,1)S(1)}, u32[]{:S(2)}, u32[]{:S(2)}) collective-permute-start(bf16[2,3,128,768]{3,2,1,0:T(8,128)(2,1)S(1)} %pad_maximum_fusion.dep.refs_0_), channel_id=1, source_target_pairs={{0,16},{4,12},{8,24},{12,4},{16,0},{20,28},{24,8},{28,20},{1,17},{... | collective-permute-start | bytes 3538952 | tf_op jit(solution)/shard_map/ppermute | solution.py:496
  43.2 37.2 %collective-permute-start.17 = (bf16[2,3,128,768]{3,2,1,0:T(8,128)(2,1)S(1)}, bf16[2,3,128,768]{3,2,1,0:T(8,128)(2,1)S(1)}, u32[]{:S(2)}, u32[]{:S(2)}) collective-permute-start(bf16[2,3,128,768]{3,2,1,0:T(8,128)(2,1)S(1)} %pad_maximum_fusion.dep.refs_0_), channel_id=1, source_target_pairs={{0,4},{4,0},{8,12},{12,8},{16,20},{20,16},{24,28},{28,24},{1,5},{5... | collective-permute-start | bytes 3538952 | tf_op jit(solution)/shard_map/ppermute | solution.py:496
  54.4 1.5 %copy-start = (f32[768,768]{1,0:T(8,128)}, f32[768,768]{1,0:T(8,128)S(1)}, u32[]{:S(2)}) copy-start(f32[768,768]{1,0:T(8,128)S(1)} %get-tuple-element.17.dep.refs_4_) | copy-start | bytes 7077892
  57.2 16.0 %copy-start.12 = (bf16[2,3,128,768]{3,2,1,0:T(8,128)(2,1)}, bf16[2,3,128,768]{3,2,1,0:T(8,128)(2,1)S(1)}, u32[]{:S(2)}) copy-start(bf16[2,3,128,768]{3,2,1,0:T(8,128)(2,1)S(1)} %collective-permute-done.16.refs_1_) | copy-start | bytes 3538948
  57.2 23.2 %collective-permute-start.18 = (bf16[2,3,128,768]{3,2,1,0:T(8,128)(2,1)S(1)}, bf16[2,3,128,768]{3,2,1,0:T(8,128)(2,1)S(1)}, u32[]{:S(2)}, u32[]{:S(2)}) collective-permute-start(bf16[2,3,128,768]{3,2,1,0:T(8,128)(2,1)S(1)} %collective-permute-done.16.refs_1_), channel_id=1, source_target_pairs={{0,4},{4,0},{8,12},{12,8},{16,20},{20,16},{24,28},{28,24},{1,5},{5... | collective-permute-start | bytes 3538952 | tf_op jit(solution)/shard_map/ppermute | solution.py:496
  57.3 5.0 %collective-permute-start.11 = (bf16[8,8,768]{2,0,1:T(8,128)(2,1)S(1)}, bf16[8,8,768]{2,0,1:T(8,128)(2,1)S(1)}, u32[]{:S(2)}, u32[]{:S(2)}) collective-permute-start(bf16[8,8,768]{2,0,1:T(8,128)(2,1)S(1)} %pad_maximum_fusion.4), channel_id=1, source_target_pairs={{0,4},{4,8},{8,12},{12,16},{16,20},{20,24},{24,28},{28,0},{1,5},{5... | collective-permute-start | bytes 294920 | tf_op jit(solution)/shard_map/ppermute | solution.py:473
  57.8 5.8 %collective-permute-start.12 = (bf16[8,8,768]{2,0,1:T(8,128)(2,1)S(1)}, bf16[8,8,768]{2,0,1:T(8,128)(2,1)S(1)}, u32[]{:S(2)}, u32[]{:S(2)}) collective-permute-start(bf16[8,8,768]{2,0,1:T(8,128)(2,1)S(1)} %pad_maximum_fusion.5), channel_id=1, source_target_pairs={{4,0},{8,4},{12,8},{16,12},{20,16},{24,20},{28,24},{0,28},{5,1},{9... | collective-permute-start | bytes 294920 | tf_op jit(solution)/shard_map/ppermute | solution.py:473
  60.0 13.1 %collective-permute-start.14 = (bf16[128,768]{1,0:T(8,128)(2,1)S(1)}, bf16[128,768]{1,0:T(8,128)(2,1)S(1)}, u32[]{:S(2)}, u32[]{:S(2)}) collective-permute-start(bf16[128,768]{1,0:T(8,128)(2,1)S(1)} %constant_dynamic-slice_fusion), channel_id=1, source_target_pairs={{0,3},{1,0},{2,1},{3,2},{4,7},{5,4},{6,5},{7,6},{8,11},{9,8},{10,9... | collective-permute-start | bytes 589832 | tf_op jit(solution)/shard_map/ppermute | solution.py:491
  62.3 16.2 %collective-permute-start.13 = (bf16[128,768]{1,0:T(8,128)(2,1)S(1)}, bf16[128,768]{1,0:T(8,128)(2,1)S(1)}, u32[]{:S(2)}, u32[]{:S(2)}) collective-permute-start(bf16[128,768]{1,0:T(8,128)(2,1)S(1)} %constant_dynamic-slice_fusion), channel_id=1, source_target_pairs={{0,2},{1,3},{2,0},{3,1},{4,6},{5,7},{6,4},{7,5},{8,10},{9,11},{10,... | collective-permute-start | bytes 589832 | tf_op jit(solution)/shard_map/ppermute | solution.py:491
  63.7 14.8 %collective-permute-start.10 = (bf16[128,768]{1,0:T(8,128)(2,1)S(1)}, bf16[128,768]{1,0:T(8,128)(2,1)S(1)}, u32[]{:S(2)}, u32[]{:S(2)}) collective-permute-start(bf16[128,768]{1,0:T(8,128)(2,1)S(1)} %constant_dynamic-slice_fusion), channel_id=1, source_target_pairs={{0,1},{1,2},{2,3},{3,0},{4,5},{5,6},{6,7},{7,4},{8,9},{9,10},{10,1... | collective-permute-start | bytes 589832 | tf_op jit(solution)/shard_map/ppermute | solution.py:491
  78.5 1.9 %copy-start.8 = (bf16[3,128,768]{2,1,0:T(8,128)(2,1)}, bf16[3,128,768]{2,1,0:T(8,128)(2,1)S(1)}, u32[]{:S(2)}) copy-start(bf16[3,128,768]{2,1,0:T(8,128)(2,1)S(1)} %get-tuple-element.31.dep) | copy-start | bytes 1769476
  78.5 12.1 %collective-permute-start.15 = (bf16[3,128,768]{2,1,0:T(8,128)(2,1)S(1)}, bf16[3,128,768]{2,1,0:T(8,128)(2,1)S(1)}, u32[]{:S(2)}, u32[]{:S(2)}) collective-permute-start(bf16[3,128,768]{2,1,0:T(8,128)(2,1)S(1)} %get-tuple-element.31.dep), channel_id=1, source_target_pairs={{0,8},{4,20},{8,0},{12,28},{16,24},{20,4},{24,16},{28,12},{1,9},{5... | collective-permute-start | bytes 1769480 | tf_op jit(solution)/shard_map/ppermute | solution.py:496
  80.4 1.1 copy-start.13
  80.4 1.5 %copy-start.14 = (bf16[2,3,128,768]{3,2,1,0:T(8,128)(2,1)}, bf16[2,3,128,768]{3,2,1,0:T(8,128)(2,1)S(1)}, u32[]{:S(2)}) copy-start(bf16[2,3,128,768]{3,2,1,0:T(8,128)(2,1)S(1)} %collective-permute-done.18.refs_3_) | copy-start | bytes 3538948
  90.7 1.2 %copy-start.17 = (s32[3]{0:T(128)S(1)}, s32[3]{0:T(128)}, u32[]{:S(2)}) copy-start(s32[3]{0:T(128)} %compare_select_fusion.vid) | copy-start | bytes 40
  90.8 1.8 %copy-start.7 = (bf16[2,3,128,768]{3,2,1,0:T(8,128)(2,1)}, bf16[2,3,128,768]{3,2,1,0:T(8,128)(2,1)S(1)}, u32[]{:S(2)}) copy-start(bf16[2,3,128,768]{3,2,1,0:T(8,128)(2,1)S(1)} %pad_maximum_fusion.1.dep.refs_0_) | copy-start | bytes 3538948
  90.8 16.3 %collective-permute-start.19 = (bf16[2,3,128,768]{3,2,1,0:T(8,128)(2,1)S(1)}, bf16[2,3,128,768]{3,2,1,0:T(8,128)(2,1)S(1)}, u32[]{:S(2)}, u32[]{:S(2)}) collective-permute-start(bf16[2,3,128,768]{3,2,1,0:T(8,128)(2,1)S(1)} %pad_maximum_fusion.1.dep.refs_0_), channel_id=1, source_target_pairs={{0,16},{4,12},{8,24},{12,4},{16,0},{20,28},{24,8},{28,20},{1,17},{... | collective-permute-start | bytes 3538952 | tf_op jit(solution)/shard_map/ppermute | solution.py:496
  92.6 14.7 %collective-permute-start.20 = (bf16[2,3,128,768]{3,2,1,0:T(8,128)(2,1)S(1)}, bf16[2,3,128,768]{3,2,1,0:T(8,128)(2,1)S(1)}, u32[]{:S(2)}, u32[]{:S(2)}) collective-permute-start(bf16[2,3,128,768]{3,2,1,0:T(8,128)(2,1)S(1)} %pad_maximum_fusion.1.dep.refs_0_), channel_id=1, source_target_pairs={{0,4},{4,0},{8,12},{12,8},{16,20},{20,16},{24,28},{28,24},{1,5},{5... | collective-permute-start | bytes 3538952 | tf_op jit(solution)/shard_map/ppermute | solution.py:496
  107.1 2.9 %copy-start.9 = (bf16[2,3,128,768]{3,2,1,0:T(8,128)(2,1)}, bf16[2,3,128,768]{3,2,1,0:T(8,128)(2,1)S(1)}, u32[]{:S(2)}) copy-start(bf16[2,3,128,768]{3,2,1,0:T(8,128)(2,1)S(1)} %collective-permute-done.19.refs_1_) | copy-start | bytes 3538948
  107.1 2.8 %collective-permute-start.21 = (bf16[2,3,128,768]{3,2,1,0:T(8,128)(2,1)S(1)}, bf16[2,3,128,768]{3,2,1,0:T(8,128)(2,1)S(1)}, u32[]{:S(2)}, u32[]{:S(2)}) collective-permute-start(bf16[2,3,128,768]{3,2,1,0:T(8,128)(2,1)S(1)} %collective-permute-done.19.refs_1_), channel_id=1, source_target_pairs={{0,4},{4,0},{8,12},{12,8},{16,20},{20,16},{24,28},{28,24},{1,5},{5... | collective-permute-start | bytes 3538952 | tf_op jit(solution)/shard_map/ppermute | solution.py:496
  107.3 2.7 %copy-start.10 = (bf16[2,3,128,768]{3,2,1,0:T(8,128)(2,1)}, bf16[2,3,128,768]{3,2,1,0:T(8,128)(2,1)S(1)}, u32[]{:S(2)}) copy-start(bf16[2,3,128,768]{3,2,1,0:T(8,128)(2,1)S(1)} %collective-permute-done.20.refs_2_) | copy-start | bytes 3538948
  110.0 1.1 copy-start.11
